TPU v7x, 128 devices: a whole 4x4x4 slice. The times are simulated.
128 devices in a mesh: grp: 16 (over x_lo, y, core), hd: 8 (over x_hi, z).
Axes of the slice: x: 4 (x_hi: 2, x_lo: 2; x = x_hi * 2 + x_lo), y: 4, z: 4, core: 2. Of those that a mesh axis runs over, the one named last changes fastest.
Arguments:
- query_rows: bfloat16 [16, 1024, 8192], P('grp', 'hd'), may hold values from -8 to 8
- key_rows: bfloat16 [16, 1024, 1024], P('grp', 'hd'), may hold values from -8 to 8
- value_rows: bfloat16 [16, 1024, 1024], P('grp', 'hd'), may hold values from -6 to 6
- lengths: int32 [16], replicated, may hold values from 256 to 1024, as said below
Outputs:
- attended: bfloat16 [16, 1024, 8192], P('grp', 'hd')
Inputs may be any that keep to these rules, and one draw needn't show every extreme that they name: `lengths`: each length lies in 256 to 1024; some sequence has length exactly 1024.
All inputs are finite; a program needn't handle non-finite values.
Results may differ from a plain program's by a relative error of at most 0.0044.
Values may be sent and summed in bfloat16 or wider, within the bound.
No kernel may reach another device: no remote copies, remote signals or barrier semaphores. Data moves between devices by JAX's collectives and lax.ppermute only.
A program may use at most 128 MiB of HBM per device.

v0:
```python
import math

import jax
import jax.numpy as jnp
from jax import lax
from jax.sharding import PartitionSpec as P

DH = 128


def spread(value, axis, root):
    mine = lax.axis_index(axis) == root
    return lax.psum(jnp.where(mine, value, jnp.zeros_like(value)), axis)


def local_attend(own_q, query_pos, own_k, own_v, pre_k, pre_v, own_len, pre_len, is_prompt):
    row_count = own_q.shape[0]
    key_span = own_k.shape[0]
    kv_count = own_k.shape[1] // DH
    group_size = own_q.shape[1] // DH // kv_count
    all_keys = (
        jnp.concatenate([pre_k, own_k], 0).reshape(2 * key_span, kv_count, DH).transpose(1, 0, 2)
    )
    all_values = (
        jnp.concatenate([pre_v, own_v], 0).reshape(2 * key_span, kv_count, DH).transpose(1, 0, 2)
    )
    heads_q = own_q.reshape(row_count, kv_count, group_size, DH).transpose(1, 0, 2, 3)
    block_rows = math.gcd(row_count, 512)
    n_blocks = row_count // block_rows
    key_pos = jnp.arange(key_span, dtype=jnp.int32)
    pre_ok = (key_pos < pre_len) & jnp.logical_not(is_prompt)
    score_scale = 1.0 / math.sqrt(DH)

    def per_head(triple):
        q_head, k_head, v_head = triple

        def per_block(bundle):
            q_blk, pos_blk = bundle
            own_ok = (key_pos[None, :] <= pos_blk[:, None]) & (key_pos[None, :] < own_len)
            allowed = jnp.concatenate(
                [jnp.broadcast_to(pre_ok[None, :], (block_rows, key_span)), own_ok], 1
            )
            scores = (
                jnp.einsum("qgd,kd->gqk", q_blk, k_head, preferred_element_type=jnp.float32)
                * score_scale
            )
            scores = jnp.where(allowed[None], scores, jnp.float32(-1e30))
            row_top = jnp.max(scores, -1, keepdims=True)
            probs = jnp.exp(scores - row_top)
            total = jnp.sum(probs, -1)
            weights = probs.astype(jnp.bfloat16)
            mixed = jnp.einsum("gqk,kd->gqd", weights, v_head, preferred_element_type=jnp.float32)
            return (mixed / total[..., None]).transpose(1, 0, 2)

        pieces = lax.map(
            per_block,
            (
                q_head.reshape(n_blocks, block_rows, group_size, DH),
                query_pos.reshape(n_blocks, block_rows),
            ),
        )
        return pieces.reshape(row_count, group_size, DH)

    result = lax.map(per_head, (heads_q, all_keys, all_values))
    result = result.transpose(1, 0, 2, 3).reshape(row_count, -1)
    live = query_pos < own_len
    return jnp.where(live[:, None], result, 0.0).astype(jnp.bfloat16)


def on_device(query_rows, key_rows, value_rows, lengths):
    seq_index = lax.axis_index("grp")
    own_len = lengths[seq_index]
    prompt_len = lengths[0]
    is_prompt = seq_index == 0
    own_q = query_rows[0]
    own_k = key_rows[0]
    own_v = value_rows[0]
    head_q, head_k, head_v = (
        lax.all_to_all(own_q, "hd", split_axis=1, concat_axis=0, tiled=True),
        lax.all_to_all(own_k, "hd", split_axis=1, concat_axis=0, tiled=True),
        lax.all_to_all(own_v, "hd", split_axis=1, concat_axis=0, tiled=True),
    )
    head_pk, head_pv = (spread(head_k, "grp", 0), spread(head_v, "grp", 0))
    positions = jnp.arange(head_q.shape[0], dtype=jnp.int32)
    head_out = local_attend(
        head_q, positions, head_k, head_v, head_pk, head_pv, own_len, prompt_len, is_prompt
    )
    result = lax.all_to_all(head_out, "hd", split_axis=0, concat_axis=1, tiled=True)
    return result[None]


def solution(mesh):
    placed = (P("grp", "hd", None), P("grp", "hd", None), P("grp", "hd", None), P())
    return jax.shard_map(
        on_device, mesh=mesh, in_specs=placed, out_specs=P("grp", "hd", None), check_vma=False
    )
```

profile of v0, /device:TPU:1, one launch (start us, length us, event | category | flops | bytes accessed | tf_op | source)
XLA Modules:
  0.0 315.8 jit_solution(5610257248418667366)
XLA Ops:
  6.5 1.0 copy.25
  7.5 0.0 copy-start.2
  7.5 0.8 copy.14
  8.3 8.3 %all-to-all-start.2 = ((bf16[128,8,128]{2,0,1:T(8,128)(2,1)}), bf16[128,8,128]{2,0,1:T(8,128)(2,1)S(1)}, u32[]{:S(2)}, u32[]{:S(2)}) async-start(bf16[128,8,128]{2,0,1:T(8,128)(2,1)} %copy.14), calls=%async_computation.2 | async-start | bytes 524288 | tf_op jit(solution)/shard_map/all_to_all | solution.py:81
  16.6 1.0 copy.24
  17.6 0.7 copy.13
  18.4 5.8 %all-to-all-done.2 = bf16[128,8,128]{2,0,1:T(8,128)(2,1)S(1)} async-done(((bf16[128,8,128]{2,0,1:T(8,128)(2,1)}), bf16[128,8,128]{2,0,1:T(8,128)(2,1)S(1)}, u32[]{:S(2)}, u32[]{:S(2)}) %all-to-all-start.2) | async-done | bytes 262176 | tf_op jit(solution)/shard_map/all_to_all | solution.py:81
  24.2 3.4 %all-to-all-start.1 = ((bf16[128,8,128]{2,0,1:T(8,128)(2,1)}), bf16[128,8,128]{2,0,1:T(8,128)(2,1)S(1)}, u32[]{:S(2)}, u32[]{:S(2)}) async-start(bf16[128,8,128]{2,0,1:T(8,128)(2,1)} %copy.13), calls=%async_computation.1 | async-start | bytes 524288 | tf_op jit(solution)/shard_map/all_to_all | solution.py:80
  27.6 3.0 copy.22
  30.6 2.5 copy.12
  33.1 2.2 all-to-all-done.1
  35.3 4.4 %all-to-all-start = ((bf16[128,8,1024]{2,0,1:T(8,128)(2,1)}), bf16[128,8,1024]{2,0,1:T(8,128)(2,1)S(1)}, u32[]{:S(2)}, u32[]{:S(2)}) async-start(bf16[128,8,1024]{2,0,1:T(8,128)(2,1)} %copy.12), calls=%async_computation | async-start | bytes 4194304 | tf_op jit(solution)/shard_map/all_to_all | solution.py:79
  39.7 0.2 all-reduce.3.cloned.1.call-start
  39.9 0.8 broadcast_select_fusion
  40.7 0.7 broadcast_select_fusion.1
  41.4 0.0 all-reduce.3.cloned.1.call-update
  41.5 0.0 copy-done.2
  41.5 0.7 fusion.20
  42.1 1.2 add_compare_fusion
  43.4 121.9 %all-reduce.3.cloned.1.call-done = (bf16[1024,128]{1,0:T(8,128)(2,1)}, bf16[1024,128]{1,0:T(8,128)(2,1)}) async-done(((bf16[1024,128]{1,0:T(8,128)(2,1)}, bf16[1024,128]{1,0:T(8,128)(2,1)}), (bf16[1024,128]{1,0:T(8,128)(2,1)}, bf16[1024,128]{1,0:T(8,128)(2,1)})) %all-reduce.3.cloned.1.call-update) | async-done | bytes 524304 | tf_op jit(solution)/shard_map/psum | solution.py:13
  165.2 1.9 pad_maximum_fusion
  167.1 0.0 all-to-all-done
  167.2 1.3 copy-done
  168.5 2.2 copy.23
  170.7 0.0 copy-start.3
  170.7 95.7 %while.23 = (s32[]{:T(128)}, bf16[2,512,8,128]{3,2,1,0:T(8,128)(2,1)}, s32[2,512]{1,0:T(2,128)S(1)}, s32[]{:T(128)}, bf16[2,512,8,128]{3,2,1,0:T(8,128)(2,1)S(1)...) while((s32[]{:T(128)}, ...), condition=%wide.region_5.6_spmd.clone.clone, body=%wide.region_2.5_spmd.clone.clone.sunk | while | flops 4390382592 | bytes 115440280 | solution.py:55
  170.7 1.3 iota_compare_fusion.4
  172.0 0.4 fusion.28
  172.5 0.6 pad_add_fusion.2
  173.1 0.1 constant_dynamic-slice_fusion.5
  173.1 13.9 %bitcast_reduce_fusion.2 = (f32[8,512]{1,0:T(8,128)S(1)}, f32[512,8,2048]{2,0,1:T(8,128)}) fusion(pred[512,2048]{1,0:T(8,128)(4,1)S(1)} %pad_add_fusion.2, bf16[2048,128]{1,0:T(8,128)(2,1)S(1)} %get-tuple-element.282, bf16[1,512,8,128]{3,2,1,0:T(8,128)(2,1)S(1)} %constant_dynamic-slice_fusion.5), kind=kOutput, calls=%fused_computation.3.clone.1 | convolution fusion | flops 2172645376 | bytes 36192256 | tf_op jit(solution)/shard_map/while/body/eval_jaxpr/while/body/eval_jaxpr/qgd,kd->gqk/dot_general | solution.py:44
  187.1 15.1 %fusion.29 = f32[8,512]{1,0:T(8,128)S(1)} fusion(f32[512,8,2048]{2,0,1:T(8,128)} %get-tuple-element.253, f32[8,512]{1,0:T(8,128)S(1)} %get-tuple-element.254, pred[512,2048]{1,0:T(8,128)(4,1)S(1)} %pad_add_fusion.2), kind=kLoop, calls=%fused_computation.6.clone.1 | loop fusion | flops 33550336 | bytes 34635776 | tf_op jit(solution)/shard_map/while/body/eval_jaxpr/while/body/eval_jaxpr/reduce_sum | solution.py:50
  202.2 0.0 copy-done.1
  202.2 14.7 %fusion.30 = bf16[1,512,8,128]{3,1,2,0:T(8,128)(2,1)S(1)} fusion(f32[512,8,2048]{2,0,1:T(8,128)} %get-tuple-element.253, f32[8,512]{1,0:T(8,128)S(1)} %get-tuple-element.254, pred[512,2048]{1,0:T(8,128)(4,1)S(1)} %pad_add_fusion.2, f32[512,8]{0,1:T(8,128)S(1)} %bitcast.91, bf16[2048,128]{1,0:T(8,128)(2,1)S(1)} %copy-done.1), kind=kOutput, calls=%fused_computation.13.clone.1 | convolution fusion | flops 2182086656 | bytes 36208640 | tf_op jit(solution)/shard_map/while/body/eval_jaxpr/while/body/eval_jaxpr/gqk,kd->gqd/dot_general | solution.py:52
  216.9 1.7 copy_dynamic-update-slice_fusion.2
  218.6 1.3 iota_compare_fusion.4
  219.9 0.4 fusion.28
  220.3 0.6 pad_add_fusion.2
  220.9 0.1 constant_dynamic-slice_fusion.5
  221.0 13.9 %bitcast_reduce_fusion.2 = (f32[8,512]{1,0:T(8,128)S(1)}, f32[512,8,2048]{2,0,1:T(8,128)}) fusion(pred[512,2048]{1,0:T(8,128)(4,1)S(1)} %pad_add_fusion.2, bf16[2048,128]{1,0:T(8,128)(2,1)S(1)} %get-tuple-element.282, bf16[1,512,8,128]{3,2,1,0:T(8,128)(2,1)S(1)} %constant_dynamic-slice_fusion.5), kind=kOutput, calls=%fused_computation.3.clone.1 | convolution fusion | flops 2172645376 | bytes 36192256 | tf_op jit(solution)/shard_map/while/body/eval_jaxpr/while/body/eval_jaxpr/qgd,kd->gqk/dot_general | solution.py:44
  234.9 15.1 %fusion.29 = f32[8,512]{1,0:T(8,128)S(1)} fusion(f32[512,8,2048]{2,0,1:T(8,128)} %get-tuple-element.253, f32[8,512]{1,0:T(8,128)S(1)} %get-tuple-element.254, pred[512,2048]{1,0:T(8,128)(4,1)S(1)} %pad_add_fusion.2), kind=kLoop, calls=%fused_computation.6.clone.1 | loop fusion | flops 33550336 | bytes 34635776 | tf_op jit(solution)/shard_map/while/body/eval_jaxpr/while/body/eval_jaxpr/reduce_sum | solution.py:50
  250.0 14.7 %fusion.30 = bf16[1,512,8,128]{3,1,2,0:T(8,128)(2,1)S(1)} fusion(f32[512,8,2048]{2,0,1:T(8,128)} %get-tuple-element.253, f32[8,512]{1,0:T(8,128)S(1)} %get-tuple-element.254, pred[512,2048]{1,0:T(8,128)(4,1)S(1)} %pad_add_fusion.2, f32[512,8]{0,1:T(8,128)S(1)} %bitcast.91, bf16[2048,128]{1,0:T(8,128)(2,1)S(1)} %copy-done.1), kind=kOutput, calls=%fused_computation.13.clone.1 | convolution fusion | flops 2182086656 | bytes 36208640 | tf_op jit(solution)/shard_map/while/body/eval_jaxpr/while/body/eval_jaxpr/gqk,kd->gqd/dot_general | solution.py:52
  264.7 1.7 copy_dynamic-update-slice_fusion.2
  266.4 2.8 reshape_transpose.3
  269.2 0.4 select_convert_fusion
  269.6 32.8 %all_to_all.67 = bf16[8,128,1024]{2,1,0:T(8,128)(2,1)S(1)} all-to-all(bf16[8,128,1024]{2,1,0:T(8,128)(2,1)S(1)} %select_convert_fusion), channel_id=1, replica_groups=mesh['grp'=16,'hd'=8] {'hd'}, dimensions={0} | all-to-all | bytes 4194304 | tf_op jit(solution)/shard_map/all_to_all | solution.py:88
  302.5 2.4 copy.17
  304.9 4.1 %copy.18 = bf16[1,128,8192]{2,1,0:T(8,128)(2,1)} copy(bf16[1,128,8192]{1,2,0:T(8,128)(2,1)} %bitcast.84) | data formatting | bytes 4194304 | tf_op jit(solution)/shard_map/broadcast_in_dim | solution.py:89
  (11 shorter events, 0.0 us)
Async XLA Ops:
  7.5 33.9 %copy-start.2 = (s32[16]{0:T(128)S(1)}, s32[16]{0:T(128)}, u32[]{:S(2)}) copy-start(s32[16]{0:T(128)} %param.9) | copy-start | bytes 196
  8.3 15.9 %all-to-all-start.2 = ((bf16[128,8,128]{2,0,1:T(8,128)(2,1)}), bf16[128,8,128]{2,0,1:T(8,128)(2,1)S(1)}, u32[]{:S(2)}, u32[]{:S(2)}) async-start(bf16[128,8,128]{2,0,1:T(8,128)(2,1)} %copy.14), calls=%async_computation.2 | async-start | bytes 524288 | tf_op jit(solution)/shard_map/all_to_all | solution.py:81
  24.2 11.1 %all-to-all-start.1 = ((bf16[128,8,128]{2,0,1:T(8,128)(2,1)}), bf16[128,8,128]{2,0,1:T(8,128)(2,1)S(1)}, u32[]{:S(2)}, u32[]{:S(2)}) async-start(bf16[128,8,128]{2,0,1:T(8,128)(2,1)} %copy.13), calls=%async_computation.1 | async-start | bytes 524288 | tf_op jit(solution)/shard_map/all_to_all | solution.py:80
  35.3 131.9 %all-to-all-start = ((bf16[128,8,1024]{2,0,1:T(8,128)(2,1)}), bf16[128,8,1024]{2,0,1:T(8,128)(2,1)S(1)}, u32[]{:S(2)}, u32[]{:S(2)}) async-start(bf16[128,8,1024]{2,0,1:T(8,128)(2,1)} %copy.12), calls=%async_computation | async-start | bytes 4194304 | tf_op jit(solution)/shard_map/all_to_all | solution.py:79
  39.7 125.5 %all-reduce.3.cloned.1.call-start = ((), (), s32[]{:S(2)}) async-start(), calls=%async_computation.4 | async-start | bytes 1048576 | tf_op jit(solution)/shard_map/psum | solution.py:13
  167.2 1.3 copy-start
  170.7 98.5 %copy-start.3 = (pred[8,128]{1,0:T(8,128)(4,1)S(1)}, pred[8,128]{1,0:T(8,128)(4,1)}, u32[]{:S(2)}) copy-start(pred[8,128]{1,0:T(8,128)(4,1)} %add_compare_fusion) | copy-start | bytes 3076
  187.1 15.1 %copy-start.1 = (bf16[2048,128]{1,0:T(8,128)(2,1)S(1)}, bf16[2048,128]{1,0:T(8,128)(2,1)}, u32[]{:S(2)}) copy-start(bf16[2048,128]{1,0:T(8,128)(2,1)} %get-tuple-element.283) | copy-start | bytes 1572868 | tf_op jit(solution)/shard_map/while/body/eval_jaxpr/while
  234.9 15.1 %copy-start.1 = (bf16[2048,128]{1,0:T(8,128)(2,1)S(1)}, bf16[2048,128]{1,0:T(8,128)(2,1)}, u32[]{:S(2)}) copy-start(bf16[2048,128]{1,0:T(8,128)(2,1)} %get-tuple-element.283) | copy-start | bytes 1572868 | tf_op jit(solution)/shard_map/while/body/eval_jaxpr/while
Sparse Core Ops, SparseCore 0:
  43.0 122.1 all-reduce.2
where the time goes:
time: 318 us; the launch traced here: 316 us
  waiting for transfers between devices  130 us (41%)
  matrix products  57.2 us (18%)
  other arithmetic  39.9 us (13%)
  blocking collectives  32.8 us (10%)
  local copies, waits for them, and re-layouts  25.9 us (8%)
  starting transfers between devices  16.3 us (5%)
  between operations  13.5 us (4%)
    psum x1, waiting for transfers between devices, spread(): return lax.psum(jnp.where(mine, value, jnp.zeros_like(value)), axis)  122 us
    all_to_all x1, blocking collectives, on_device(): lax.all_to_all(head_out, 'hd', split_axis=0, concat_axis=1, tiled=True)  32.8 us
    reduce_sum x2, other arithmetic, per_block(): total = jnp.sum(probs, -1)  30.2 us
    dot_general x2, matrix products, per_block(): jnp.einsum('gqk,kd->gqd', weights, v_head, preferred_element_type=jnp.flo...  29.4 us
    dot_general x2, matrix products, per_block(): jnp.einsum('qgd,kd->gqk', q_blk, k_head, preferred_element_type=jnp.float32)  27.9 us
    unnamed x10, local copies, waits for them, and re-layouts  8.52 us
    all_to_all x1, starting transfers between devices, on_device(): lax.all_to_all(own_v, 'hd', split_axis=1, concat_axis=0, tiled=True)  8.32 us
  transfers between devices with their start and end apart: 4, of which 3 were waited for; matrix products, arithmetic and copies ran while one was open for 4% of the time, Pallas kernels for 0%

commit v1 on v0

v1 whole, which is shorter than its diff:
```python
import functools
import math

import jax
import jax.numpy as jnp
from jax import lax
from jax.experimental import pallas as pl
from jax.experimental.pallas import tpu as pltpu
from jax.sharding import PartitionSpec as P

DH = 128
ROWS = 128
KVH = 8
GROUP = 8
PAIR = 2 * DH
SCALE_LOG2 = math.log2(math.e) / math.sqrt(DH)
NEG = -1e30
NT = (((1,), (1,)), ((), ()))
TILE = 512


def attend_kernel(
    info, q_ref, diag, r0p, r0m, r1m, r0x, r1x, r1p, r2a, r2b, *rest
):
    prompt, (o_ref, k_aug, v_aug) = rest[:KVH], rest[KVH:]
    step = pl.program_id(0)
    head = info[step]
    x_hi, z, pre_len, n_live = info[8], info[9], info[10], info[11]
    lane0 = lax.broadcasted_iota(jnp.int32, (ROWS, DH), 1) == 0
    neg = jnp.float32(NEG)

    def place(slot, ref, bias):
        rows = slice(slot * ROWS, (slot + 1) * ROWS)
        k_aug[rows, :DH] = ref[:, :DH]
        v_aug[rows, :DH] = ref[:, DH:]
        k_aug[rows, DH:] = jnp.where(lane0, bias, 0.0).astype(jnp.bfloat16)

    @pl.when(step == 0)
    def _():
        v_aug[:, DH:] = jnp.ones((2048, DH), jnp.bfloat16)

    def bias_if(ok):
        return jnp.where(ok, jnp.float32(0.0), neg)

    place(0, diag, jnp.float32(0.0))
    place(1, r0p, bias_if(z >= 1))
    place(2, r0m, bias_if(z == 3))
    place(3, r1m, bias_if(z >= 2))
    place(4, r0x, bias_if(x_hi == 1))
    place(5, r1x, bias_if(x_hi == 1))
    place(6, r1p, bias_if(x_hi == 1))

    @pl.when(head < 4)
    def _():
        place(7, r2a, bias_if(x_hi == 1))

    @pl.when(head >= 4)
    def _():
        place(7, r2b, bias_if(x_hi == 1))

    for n in range(KVH):

        @pl.when(step == n)
        def _(n=n):
            k_aug[1024:, :DH] = prompt[n][:, :DH]
            v_aug[1024:, :DH] = prompt[n][:, DH:]

    position = lax.broadcasted_iota(jnp.int32, (1024, DH), 0)
    first = lax.broadcasted_iota(jnp.int32, (1024, DH), 1) == 0
    k_aug[1024:, DH:] = jnp.where(first & (position >= pre_len), neg, 0.0).astype(jnp.bfloat16)

    chunks = (pre_len + 255) // 256

    def run(n_keys):
        heads_in_tile = TILE // ROWS
        row = lax.broadcasted_iota(jnp.int32, (TILE, ROWS), 0) % ROWS
        col = lax.broadcasted_iota(jnp.int32, (TILE, ROWS), 1)
        one = jnp.where(
            lax.broadcasted_iota(jnp.int32, (TILE, DH), 1) == 0, 1.0, 0.0
        ).astype(jnp.bfloat16)
        for t in range(GROUP * ROWS // TILE):
            q = jnp.concatenate(
                [
                    q_ref[:, (t * heads_in_tile + j) * DH : (t * heads_in_tile + j + 1) * DH]
                    for j in range(heads_in_tile)
                ],
                0,
            )
            q = jnp.concatenate([q, one], 1)
            s = lax.dot_general(q, k_aug[:n_keys, :], NT, preferred_element_type=jnp.float32)
            s = jnp.concatenate([jnp.where(row >= col, s[:, :ROWS], neg), s[:, ROWS:]], 1)
            top = jnp.max(s, axis=1, keepdims=True)
            p = jnp.exp2((s - top) * SCALE_LOG2).astype(jnp.bfloat16)
            acc = jnp.dot(p, v_aug[:n_keys, :], preferred_element_type=jnp.float32)
            out = acc[:, :DH] / acc[:, DH:]
            out = jnp.where(row < n_live, out, 0.0).astype(jnp.bfloat16)
            for j in range(heads_in_tile):
                h = t * heads_in_tile + j
                o_ref[:, h * DH : (h + 1) * DH] = out[j * ROWS : (j + 1) * ROWS]

    for n in range(5):

        @pl.when((n_live > 0) & (chunks == n))
        def _(n=n):
            run(1024 + 256 * n)

    @pl.when(n_live <= 0)
    def _():
        o_ref[...] = jnp.zeros_like(o_ref)


def attend(info, query, own, prompt):
    def at_head(width):
        return pl.BlockSpec((ROWS, width), lambda i, info: (0, info[i]))

    half = pl.BlockSpec((ROWS, PAIR), lambda i, info: (0, lax.rem(info[i], 4)))
    whole = pl.BlockSpec((1024, PAIR), lambda i, info: (0, 0))
    return pl.pallas_call(
        attend_kernel,
        grid_spec=pltpu.PrefetchScalarGridSpec(
            num_scalar_prefetch=1,
            grid=(KVH,),
            in_specs=[at_head(GROUP * DH)] + [at_head(PAIR)] * 7 + [half] * 2 + [whole] * KVH,
            out_specs=at_head(GROUP * DH),
            scratch_shapes=[
                pltpu.VMEM((2048, PAIR), jnp.bfloat16),
                pltpu.VMEM((2048, PAIR), jnp.bfloat16),
            ],
        ),
        out_shape=jax.ShapeDtypeStruct(query.shape, jnp.bfloat16),
        compiler_params=pltpu.CompilerParams(vmem_limit_bytes=48 << 20),
    )(info, query, *own, *prompt)


def on_device(query_rows, key_rows, value_rows, lengths):
    grp = lax.axis_index("grp")
    hd = lax.axis_index("hd")
    core, y, x_lo = grp % 2, (grp // 2) % 4, grp // 8
    z, x_hi = hd % 4, hd // 4

    kv = jnp.concatenate(
        [key_rows[0].reshape(ROWS, KVH, DH), value_rows[0].reshape(ROWS, KVH, DH)], 2
    ).reshape(ROWS, KVH * PAIR)

    def on_hd(value, pairs):
        return lax.ppermute(value, "hd", pairs)

    def on_grp(value, pairs):
        return lax.ppermute(value, "grp", pairs)

    other = on_grp(kv[:, 4 * PAIR :], [(0, 1)])
    four = jnp.where(core == 0, kv[:, : 4 * PAIR], other)
    piece = four[:, :PAIR]
    for d in range(1, 4):
        got = on_grp(four[:, d * PAIR : (d + 1) * PAIR], [(0, 2 * d), (1, 2 * d + 1)])
        piece = jnp.where(y == d, got, piece)

    r0x = on_hd(kv, [(i, 4 + i) for i in range(4)])
    r0p = on_hd(kv, [(4 * x + i, 4 * x + i + 1) for x in range(2) for i in range(3)])
    r0m = on_hd(kv, [((i + 1) % 4, i) for i in range(4)] + [(4, 7), (5, 4)])

    def on_both(value, pairs):
        return lax.ppermute(value, ("grp", "hd"), pairs)

    c1 = on_both(piece, [(g * 8 + r, (g + 8) * 8 + r) for g in range(8) for r in range(8)])
    c2 = on_both(piece, [(g * 8 + r, g * 8 + (r ^ 4)) for g in range(8) for r in range(8)])
    c3 = on_both(piece, [(g * 8 + r, (g + 8) * 8 + (r ^ 4)) for g in range(8) for r in range(8)])
    same = jnp.where(x_lo == 0, piece, c1)
    far = jnp.where(x_lo == 0, c2, c3)
    both = jnp.stack([jnp.where(x_hi == 0, same, far), jnp.where(x_hi == 0, far, same)])

    def ring(d):
        return [(4 * x + i, 4 * x + (i + d) % 4) for x in range(2) for i in range(4)]

    behind = [both] + [on_hd(both, ring(d)) for d in range(1, 4)]
    orders = [
        jnp.stack([behind[(at - i) % 4] for i in range(4)], 1).reshape(1024, PAIR)
        for at in range(4)
    ]
    mine = lax.select_n(z, *orders)

    r1x = on_hd(r0m, [(i, 4 + i) for i in range(4)])
    r1p = on_hd(r0x, [(4 + i, 4 + (i + 1) % 4) for i in range(4)])
    r1m = on_hd(r0m, [((i + 1) % 4, i) for i in range(4)] + [(7, 6), (4, 7)])
    r2a = on_hd(r1m[:, : 4 * PAIR], [(i, 4 + i) for i in range(4)])
    r2b = on_hd(r1p[:, 4 * PAIR :], [(4 + i, 4 + (i + 1) % 4) for i in range(4)])

    def along_y(d):
        return [(g, (g & 9) | ((g + 2 * d) & 6)) for g in range(16)]

    fours = [mine] + [on_grp(mine, along_y(d)) for d in range(1, 4)]
    swapped = [on_grp(value, [(g, g ^ 1) for g in range(16)]) for value in fours]
    heads = [4 * core + (y - d) % 4 for d in range(4)]
    heads += [4 * (1 - core) + (y - d) % 4 for d in range(4)]

    pre_len = jnp.where(grp == 0, 0, lengths[0])
    n_live = lengths[grp] - hd * ROWS
    info = jnp.stack([jnp.int32(v) for v in heads + [x_hi, z, pre_len, n_live]])
    own = (kv, r0p, r0m, r1m, r0x, r1x, r1p, r2a, r2b)
    return attend(info, query_rows[0], own, fours + swapped)[None]


def solution(mesh):
    placed = (P("grp", "hd", None), P("grp", "hd", None), P("grp", "hd", None), P())
    return jax.shard_map(
        on_device, mesh=mesh, in_specs=placed, out_specs=P("grp", "hd", None), check_vma=False
    )
```

time: 318 us -> 123 us (0.39)
  the two profiles are of different devices: /device:TPU:1 before, /device:TPU:28 now
where the time goes in v1:
time: 123 us; the launch traced here: 121 us
  waiting for transfers between devices  44.3 us (36%)
  starting transfers between devices  35.5 us (29%)
  Pallas kernels  30.6 us (25%)
  local copies, waits for them, and re-layouts  7.99 us (6%)
  between operations  1.76 us (1%)
    pallas_call x1, Pallas kernels, attend(): pl.pallas_call(attend_kernel, grid_spec=pltpu.PrefetchScalarGridSpec(num_...  30.6 us
    ppermute x11, waiting for transfers between devices, on_hd(): return lax.ppermute(value, 'hd', pairs)  25.8 us
    ppermute x11, starting transfers between devices, on_hd(): return lax.ppermute(value, 'hd', pairs)  24.9 us
    ppermute x11, waiting for transfers between devices, on_grp(): return lax.ppermute(value, 'grp', pairs)  14.5 us
    unnamed x15, local copies, waits for them, and re-layouts  5.76 us
    ppermute x11, starting transfers between devices, on_grp(): return lax.ppermute(value, 'grp', pairs)  5.61 us
    ppermute x3, starting transfers between devices, on_both(): return lax.ppermute(value, ('grp', 'hd'), pairs)  5 us
    ppermute x3, waiting for transfers between devices, on_both(): return lax.ppermute(value, ('grp', 'hd'), pairs)  3.9 us
  transfers between devices with their start and end apart: 25, of which 7 were waited for; matrix products, arithmetic and copies ran while one was open for 2% of the time, Pallas kernels for 0%

profile of v1, /device:TPU:28, one launch (start us, length us, event | category | flops | bytes accessed | tf_op | source)
XLA Modules:
  0.0 120.6 jit_solution(5915342064007669096)
XLA Ops:
  0.0 1.0 copy.6
  1.0 1.0 copy.7
  2.0 0.1 pad_maximum_fusion
  2.1 0.1 copy.8
  2.2 0.7 collective-permute-start.8
  3.0 0.7 collective-permute-start.11
  3.7 0.7 collective-permute-start.10
  4.3 1.3 %collective-permute-start.9 = (bf16[128,256]{1,0:T(8,128)(2,1)S(1)}, bf16[128,256]{1,0:T(8,128)(2,1)S(1)}, u32[]{:S(2)}, u32[]{:S(2)}) collective-permute-start(bf16[128,256]{1,0:T(8,128)(2,1)S(1)} %get-tuple-element.9), channel_id=1, source_target_pairs={{0,48},{8,56},{1,49},{9,57},{2,50},{10,58},{3,51},{11,59},{4,52},{... | collective-permute-start | bytes 196616 | tf_op jit(solution)/shard_map/ppermute | solution.py:149
  5.7 0.0 collective-permute-done.11
  5.7 6.8 %collective-permute-done.9 = bf16[128,256]{1,0:T(8,128)(2,1)S(1)} collective-permute-done((bf16[128,256]{1,0:T(8,128)(2,1)S(1)}, bf16[128,256]{1,0:T(8,128)(2,1)S(1)}, u32[]{:S(2)}, u32[]{:S(2)}) %collective-permute-start.9) | collective-permute-done | bytes 65568 | tf_op jit(solution)/shard_map/ppermute | solution.py:149
  12.5 0.0 copy-start.5
  12.5 1.3 %collective-permute-start.14 = (bf16[128,256]{1,0:T(8,128)(2,1)S(1)}, bf16[128,256]{1,0:T(8,128)(2,1)S(1)}, u32[]{:S(2)}, u32[]{:S(2)}) collective-permute-start(bf16[128,256]{1,0:T(8,128)(2,1)S(1)} %fusion.2), channel_id=1, source_target_pairs={{0,68},{1,69},{2,70},{3,71},{4,64},{5,65},{6,66},{7,67},{8,76},{9,... | collective-permute-start | bytes 196616 | tf_op jit(solution)/shard_map/ppermute | solution.py:163
  13.8 2.4 %collective-permute-start.13 = (bf16[128,256]{1,0:T(8,128)(2,1)S(1)}, bf16[128,256]{1,0:T(8,128)(2,1)S(1)}, u32[]{:S(2)}, u32[]{:S(2)}) collective-permute-start(bf16[128,256]{1,0:T(8,128)(2,1)S(1)} %fusion.2), channel_id=1, source_target_pairs={{0,4},{1,5},{2,6},{3,7},{4,0},{5,1},{6,2},{7,3},{8,12},{9,13},{10,... | collective-permute-start | bytes 196616 | tf_op jit(solution)/shard_map/ppermute | solution.py:163
  16.3 1.3 %collective-permute-start.12 = (bf16[128,256]{1,0:T(8,128)(2,1)S(1)}, bf16[128,256]{1,0:T(8,128)(2,1)S(1)}, u32[]{:S(2)}, u32[]{:S(2)}) collective-permute-start(bf16[128,256]{1,0:T(8,128)(2,1)S(1)} %fusion.2), channel_id=1, source_target_pairs={{0,64},{1,65},{2,66},{3,67},{4,68},{5,69},{6,70},{7,71},{8,72},{9,... | collective-permute-start | bytes 196616 | tf_op jit(solution)/shard_map/ppermute | solution.py:163
  17.6 3.9 %collective-permute-done.13 = bf16[128,256]{1,0:T(8,128)(2,1)S(1)} collective-permute-done((bf16[128,256]{1,0:T(8,128)(2,1)S(1)}, bf16[128,256]{1,0:T(8,128)(2,1)S(1)}, u32[]{:S(2)}, u32[]{:S(2)}) %collective-permute-start.13) | collective-permute-done | bytes 65568 | tf_op jit(solution)/shard_map/ppermute | solution.py:163
  21.6 4.0 %collective-permute-start.16 = (bf16[2,128,256]{2,1,0:T(8,128)(2,1)S(1)}, bf16[2,128,256]{2,1,0:T(8,128)(2,1)S(1)}, u32[]{:S(2)}, u32[]{:S(2)}) collective-permute-start(bf16[2,128,256]{2,1,0:T(8,128)(2,1)S(1)} %get-tuple-element.11), channel_id=1, source_target_pairs={{0,2},{1,3},{2,0},{3,1},{4,6},{5,7},{6,4},{7,5},{8,10},{9,11},{10,... | collective-permute-start | bytes 393224 | tf_op jit(solution)/shard_map/ppermute | solution.py:146
  25.5 0.7 collective-permute-start.15
  26.2 1.3 %collective-permute-start.17 = (bf16[2,128,256]{2,1,0:T(8,128)(2,1)S(1)}, bf16[2,128,256]{2,1,0:T(8,128)(2,1)S(1)}, u32[]{:S(2)}, u32[]{:S(2)}) collective-permute-start(bf16[2,128,256]{2,1,0:T(8,128)(2,1)S(1)} %get-tuple-element.11), channel_id=1, source_target_pairs={{0,1},{1,2},{2,3},{3,0},{4,5},{5,6},{6,7},{7,4},{8,9},{9,10},{10,1... | collective-permute-start | bytes 393224 | tf_op jit(solution)/shard_map/ppermute | solution.py:146
  27.5 1.3 %collective-permute-start.3 = (bf16[128,2048]{1,0:T(8,128)(2,1)S(1)}, bf16[128,2048]{1,0:T(8,128)(2,1)S(1)}, u32[]{:S(2)}, u32[]{:S(2)}) collective-permute-start(bf16[128,2048]{1,0:T(8,128)(2,1)S(1)} %bitcast.36), channel_id=1, source_target_pairs={{0,4},{1,5},{2,6},{3,7},{8,12},{9,13},{10,14},{11,15},{16,20},{17,... | collective-permute-start | bytes 1572872 | tf_op jit(solution)/shard_map/ppermute | solution.py:146
  28.8 3.8 %collective-permute-start.1 = (bf16[128,2048]{1,0:T(8,128)(2,1)S(1)}, bf16[128,2048]{1,0:T(8,128)(2,1)S(1)}, u32[]{:S(2)}, u32[]{:S(2)}) collective-permute-start(bf16[128,2048]{1,0:T(8,128)(2,1)S(1)} %bitcast.37), channel_id=1, source_target_pairs={{1,0},{2,1},{3,2},{0,3},{4,7},{5,4},{9,8},{10,9},{11,10},{8,11},{1... | collective-permute-start | bytes 1572872 | tf_op jit(solution)/shard_map/ppermute | solution.py:146
  32.7 2.1 %collective-permute-start = (bf16[128,2048]{1,0:T(8,128)(2,1)S(1)}, bf16[128,2048]{1,0:T(8,128)(2,1)S(1)}, u32[]{:S(2)}, u32[]{:S(2)}) collective-permute-start(bf16[128,2048]{1,0:T(8,128)(2,1)S(1)} %bitcast.38), channel_id=1, source_target_pairs={{0,1},{1,2},{2,3},{4,5},{5,6},{6,7},{8,9},{9,10},{10,11},{12,13},{... | collective-permute-start | bytes 1572872 | tf_op jit(solution)/shard_map/ppermute | solution.py:146
  34.8 0.3 fusion
  35.1 0.1 collective-permute-start.20
  35.2 1.1 collective-permute-start.19
  36.3 5.1 %collective-permute-done.3.r0x = bf16[128,2048]{1,0:T(8,128)(2,1)S(1)} collective-permute-done((bf16[128,2048]{1,0:T(8,128)(2,1)S(1)}, bf16[128,2048]{1,0:T(8,128)(2,1)S(1)}, u32[]{:S(2)}, u32[]{:S(2)}) %collective-permute-start.3) | collective-permute-done | bytes 524320 | tf_op jit(solution)/shard_map/ppermute | solution.py:146
  41.5 0.7 collective-permute-done.1.r0m
  42.1 2.3 %collective-permute-start.5 = (bf16[128,2048]{1,0:T(8,128)(2,1)S(1)}, bf16[128,2048]{1,0:T(8,128)(2,1)S(1)}, u32[]{:S(2)}, u32[]{:S(2)}) collective-permute-start(bf16[128,2048]{1,0:T(8,128)(2,1)S(1)} %collective-permute-done.3.r0x), channel_id=1, source_target_pairs={{4,5},{5,6},{6,7},{7,4},{12,13},{13,14},{14,15},{15,12},{20,21},{2... | collective-permute-start | bytes 1572872 | tf_op jit(solution)/shard_map/ppermute | solution.py:146
  44.4 0.0 copy-start
  44.4 0.8 copy-done
  45.2 4.8 %collective-permute-start.2 = (bf16[128,2048]{1,0:T(8,128)(2,1)S(1)}, bf16[128,2048]{1,0:T(8,128)(2,1)S(1)}, u32[]{:S(2)}, u32[]{:S(2)}) collective-permute-start(bf16[128,2048]{1,0:T(8,128)(2,1)S(1)} %collective-permute-done.1.r0m), channel_id=1, source_target_pairs={{1,0},{2,1},{3,2},{0,3},{7,6},{4,7},{9,8},{10,9},{11,10},{8,11},{1... | collective-permute-start | bytes 1572872 | tf_op jit(solution)/shard_map/ppermute | solution.py:146
  50.0 7.7 %collective-permute-done.20.rest_3_ = bf16[1024,256]{1,0:T(8,128)(2,1)} collective-permute-done((bf16[1024,256]{1,0:T(8,128)(2,1)S(1)}, bf16[1024,256]{1,0:T(8,128)(2,1)}, u32[]{:S(2)}, u32[]{:S(2)}) %collective-permute-start.20) | collective-permute-done | bytes 524320 | tf_op jit(solution)/shard_map/ppermute | solution.py:149
  57.7 1.3 %collective-permute-start.4 = (bf16[128,2048]{1,0:T(8,128)(2,1)S(1)}, bf16[128,2048]{1,0:T(8,128)(2,1)S(1)}, u32[]{:S(2)}, u32[]{:S(2)}) collective-permute-start(bf16[128,2048]{1,0:T(8,128)(2,1)S(1)} %collective-permute-done.1.r0m), channel_id=1, source_target_pairs={{0,4},{1,5},{2,6},{3,7},{8,12},{9,13},{10,14},{11,15},{16,20},{17,... | collective-permute-start | bytes 1572872 | tf_op jit(solution)/shard_map/ppermute | solution.py:146
  59.0 0.6 collective-permute-start.24
  59.6 0.1 collective-permute-start.23
  59.7 0.4 collective-permute-start.22
  60.1 0.7 slice.37
  60.8 0.7 slice.36
  61.6 2.2 %collective-permute-start.7 = (bf16[128,1024]{1,0:T(8,128)(2,1)}, bf16[128,1024]{1,0:T(8,128)(2,1)S(1)}, u32[]{:S(2)}, u32[]{:S(2)}) collective-permute-start(bf16[128,1024]{1,0:T(8,128)(2,1)} %slice.37), channel_id=1, source_target_pairs={{4,5},{5,6},{6,7},{7,4},{12,13},{13,14},{14,15},{15,12},{20,21},{2... | collective-permute-start | bytes 786440 | tf_op jit(solution)/shard_map/ppermute | solution.py:146
  63.7 11.7 %collective-permute-done.4.r1x = bf16[128,2048]{1,0:T(8,128)(2,1)S(1)} collective-permute-done((bf16[128,2048]{1,0:T(8,128)(2,1)S(1)}, bf16[128,2048]{1,0:T(8,128)(2,1)S(1)}, u32[]{:S(2)}, u32[]{:S(2)}) %collective-permute-start.4) | collective-permute-done | bytes 524320 | tf_op jit(solution)/shard_map/ppermute | solution.py:146
  75.4 0.8 copy-done.2
  76.2 1.3 %collective-permute-start.6 = (bf16[128,1024]{1,0:T(8,128)(2,1)}, bf16[128,1024]{1,0:T(8,128)(2,1)}, u32[]{:S(2)}, u32[]{:S(2)}) collective-permute-start(bf16[128,1024]{1,0:T(8,128)(2,1)} %slice.36), channel_id=1, source_target_pairs={{0,4},{1,5},{2,6},{3,7},{8,12},{9,13},{10,14},{11,15},{16,20},{17,... | collective-permute-start | bytes 786440 | tf_op jit(solution)/shard_map/ppermute | solution.py:146
  77.6 0.6 fusion.5
  79.4 0.1 stack.96.info
  79.5 8.3 %collective-permute-done.6.r2a = bf16[128,1024]{1,0:T(8,128)(2,1)} collective-permute-done((bf16[128,1024]{1,0:T(8,128)(2,1)}, bf16[128,1024]{1,0:T(8,128)(2,1)}, u32[]{:S(2)}, u32[]{:S(2)}) %collective-permute-start.6) | collective-permute-done | bytes 262176 | tf_op jit(solution)/shard_map/ppermute | solution.py:146
  87.9 0.0 copy-start.1
  87.9 1.0 copy-done.1
  88.9 1.0 copy-done.3
  90.0 30.6 %shard_map.46 = bf16[128,8192]{1,0:T(8,128)(2,1)} custom-call(s32[12]{0:T(128)S(1)} %stack.96.info, bf16[128,8192]{1,0:T(8,128)(2,1)} %bitcast.45, bf16[128,2048]{1,0:T(8,128)(2,1)S(1)} %bitcast.39, bf16[128,2048]{1,0:T(8,128)(2,1)S(1)} %copy-done.1, bf16[128,2048]{1,0:T(8,128)(2,1)S(1)} %collective-permute-done.1.r0m, ...), custom_call_target="tpu_custom_call" | custom-call | tf_op jit(solution)/shard_map/pallas_call | solution.py:118
  (31 shorter events, 0.2 us)
Async XLA Ops:
  2.2 0.7 collective-permute-start.8
  3.0 2.7 %collective-permute-start.11 = (bf16[128,256]{1,0:T(8,128)(2,1)S(1)}, bf16[128,256]{1,0:T(8,128)(2,1)S(1)}, u32[]{:S(2)}, u32[]{:S(2)}) collective-permute-start(bf16[128,256]{1,0:T(8,128)(2,1)S(1)} %get-tuple-element.7), channel_id=1, source_target_pairs={{0,16},{8,24},{1,17},{9,25},{2,18},{10,26},{3,19},{11,27},{4,20},{... | collective-permute-start | bytes 196616 | tf_op jit(solution)/shard_map/ppermute | solution.py:149
  3.7 2.0 %collective-permute-start.10 = (bf16[128,256]{1,0:T(8,128)(2,1)S(1)}, bf16[128,256]{1,0:T(8,128)(2,1)S(1)}, u32[]{:S(2)}, u32[]{:S(2)}) collective-permute-start(bf16[128,256]{1,0:T(8,128)(2,1)S(1)} %get-tuple-element.8), channel_id=1, source_target_pairs={{0,32},{8,40},{1,33},{9,41},{2,34},{10,42},{3,35},{11,43},{4,36},{... | collective-permute-start | bytes 196616 | tf_op jit(solution)/shard_map/ppermute | solution.py:149
  4.3 8.2 %collective-permute-start.9 = (bf16[128,256]{1,0:T(8,128)(2,1)S(1)}, bf16[128,256]{1,0:T(8,128)(2,1)S(1)}, u32[]{:S(2)}, u32[]{:S(2)}) collective-permute-start(bf16[128,256]{1,0:T(8,128)(2,1)S(1)} %get-tuple-element.9), channel_id=1, source_target_pairs={{0,48},{8,56},{1,49},{9,57},{2,50},{10,58},{3,51},{11,59},{4,52},{... | collective-permute-start | bytes 196616 | tf_op jit(solution)/shard_map/ppermute | solution.py:149
  12.5 65.1 %copy-start.5 = (s32[16]{0:T(128)S(1)}, s32[16]{0:T(128)}, u32[]{:S(2)}) copy-start(s32[16]{0:T(128)} %param.7) | copy-start | bytes 196
  12.5 5.1 %collective-permute-start.14 = (bf16[128,256]{1,0:T(8,128)(2,1)S(1)}, bf16[128,256]{1,0:T(8,128)(2,1)S(1)}, u32[]{:S(2)}, u32[]{:S(2)}) collective-permute-start(bf16[128,256]{1,0:T(8,128)(2,1)S(1)} %fusion.2), channel_id=1, source_target_pairs={{0,68},{1,69},{2,70},{3,71},{4,64},{5,65},{6,66},{7,67},{8,76},{9,... | collective-permute-start | bytes 196616 | tf_op jit(solution)/shard_map/ppermute | solution.py:163
  13.8 7.7 %collective-permute-start.13 = (bf16[128,256]{1,0:T(8,128)(2,1)S(1)}, bf16[128,256]{1,0:T(8,128)(2,1)S(1)}, u32[]{:S(2)}, u32[]{:S(2)}) collective-permute-start(bf16[128,256]{1,0:T(8,128)(2,1)S(1)} %fusion.2), channel_id=1, source_target_pairs={{0,4},{1,5},{2,6},{3,7},{4,0},{5,1},{6,2},{7,3},{8,12},{9,13},{10,... | collective-permute-start | bytes 196616 | tf_op jit(solution)/shard_map/ppermute | solution.py:163
  16.3 5.2 %collective-permute-start.12 = (bf16[128,256]{1,0:T(8,128)(2,1)S(1)}, bf16[128,256]{1,0:T(8,128)(2,1)S(1)}, u32[]{:S(2)}, u32[]{:S(2)}) collective-permute-start(bf16[128,256]{1,0:T(8,128)(2,1)S(1)} %fusion.2), channel_id=1, source_target_pairs={{0,64},{1,65},{2,66},{3,67},{4,68},{5,69},{6,70},{7,71},{8,72},{9,... | collective-permute-start | bytes 196616 | tf_op jit(solution)/shard_map/ppermute | solution.py:163
  21.6 11.1 %collective-permute-start.16 = (bf16[2,128,256]{2,1,0:T(8,128)(2,1)S(1)}, bf16[2,128,256]{2,1,0:T(8,128)(2,1)S(1)}, u32[]{:S(2)}, u32[]{:S(2)}) collective-permute-start(bf16[2,128,256]{2,1,0:T(8,128)(2,1)S(1)} %get-tuple-element.11), channel_id=1, source_target_pairs={{0,2},{1,3},{2,0},{3,1},{4,6},{5,7},{6,4},{7,5},{8,10},{9,11},{10,... | collective-permute-start | bytes 393224 | tf_op jit(solution)/shard_map/ppermute | solution.py:146
  25.5 9.3 %collective-permute-start.15 = (bf16[2,128,256]{2,1,0:T(8,128)(2,1)S(1)}, bf16[2,128,256]{2,1,0:T(8,128)(2,1)S(1)}, u32[]{:S(2)}, u32[]{:S(2)}) collective-permute-start(bf16[2,128,256]{2,1,0:T(8,128)(2,1)S(1)} %get-tuple-element.11), channel_id=1, source_target_pairs={{0,3},{1,0},{2,1},{3,2},{4,7},{5,4},{6,5},{7,6},{8,11},{9,8},{10,9... | collective-permute-start | bytes 393224 | tf_op jit(solution)/shard_map/ppermute | solution.py:146
  26.2 8.6 %collective-permute-start.17 = (bf16[2,128,256]{2,1,0:T(8,128)(2,1)S(1)}, bf16[2,128,256]{2,1,0:T(8,128)(2,1)S(1)}, u32[]{:S(2)}, u32[]{:S(2)}) collective-permute-start(bf16[2,128,256]{2,1,0:T(8,128)(2,1)S(1)} %get-tuple-element.11), channel_id=1, source_target_pairs={{0,1},{1,2},{2,3},{3,0},{4,5},{5,6},{6,7},{7,4},{8,9},{9,10},{10,1... | collective-permute-start | bytes 393224 | tf_op jit(solution)/shard_map/ppermute | solution.py:146
  27.5 13.9 %collective-permute-start.3 = (bf16[128,2048]{1,0:T(8,128)(2,1)S(1)}, bf16[128,2048]{1,0:T(8,128)(2,1)S(1)}, u32[]{:S(2)}, u32[]{:S(2)}) collective-permute-start(bf16[128,2048]{1,0:T(8,128)(2,1)S(1)} %bitcast.36), channel_id=1, source_target_pairs={{0,4},{1,5},{2,6},{3,7},{8,12},{9,13},{10,14},{11,15},{16,20},{17,... | collective-permute-start | bytes 1572872 | tf_op jit(solution)/shard_map/ppermute | solution.py:146
  28.8 13.3 %collective-permute-start.1 = (bf16[128,2048]{1,0:T(8,128)(2,1)S(1)}, bf16[128,2048]{1,0:T(8,128)(2,1)S(1)}, u32[]{:S(2)}, u32[]{:S(2)}) collective-permute-start(bf16[128,2048]{1,0:T(8,128)(2,1)S(1)} %bitcast.37), channel_id=1, source_target_pairs={{1,0},{2,1},{3,2},{0,3},{4,7},{5,4},{9,8},{10,9},{11,10},{8,11},{1... | collective-permute-start | bytes 1572872 | tf_op jit(solution)/shard_map/ppermute | solution.py:146
  32.7 11.7 %collective-permute-start = (bf16[128,2048]{1,0:T(8,128)(2,1)S(1)}, bf16[128,2048]{1,0:T(8,128)(2,1)S(1)}, u32[]{:S(2)}, u32[]{:S(2)}) collective-permute-start(bf16[128,2048]{1,0:T(8,128)(2,1)S(1)} %bitcast.38), channel_id=1, source_target_pairs={{0,1},{1,2},{2,3},{4,5},{5,6},{6,7},{8,9},{9,10},{10,11},{12,13},{... | collective-permute-start | bytes 1572872 | tf_op jit(solution)/shard_map/ppermute | solution.py:146
  35.1 22.6 %collective-permute-start.20 = (bf16[1024,256]{1,0:T(8,128)(2,1)S(1)}, bf16[1024,256]{1,0:T(8,128)(2,1)}, u32[]{:S(2)}, u32[]{:S(2)}) collective-permute-start(bf16[1024,256]{1,0:T(8,128)(2,1)S(1)} %bitcast.40), channel_id=1, source_target_pairs={{0,48},{8,56},{16,0},{24,8},{32,16},{40,24},{48,32},{56,40},{64,11... | collective-permute-start | bytes 1572872 | tf_op jit(solution)/shard_map/ppermute | solution.py:149
  35.2 22.5 %collective-permute-start.19 = (bf16[1024,256]{1,0:T(8,128)(2,1)S(1)}, bf16[1024,256]{1,0:T(8,128)(2,1)}, u32[]{:S(2)}, u32[]{:S(2)}) collective-permute-start(bf16[1024,256]{1,0:T(8,128)(2,1)S(1)} %bitcast.41), channel_id=1, source_target_pairs={{0,32},{8,40},{16,48},{24,56},{32,0},{40,8},{48,16},{56,24},{64,96... | collective-permute-start | bytes 1572872 | tf_op jit(solution)/shard_map/ppermute | solution.py:149
  41.5 17.5 %collective-permute-start.18 = (bf16[1024,256]{1,0:T(8,128)(2,1)S(1)}, bf16[1024,256]{1,0:T(8,128)(2,1)}, u32[]{:S(2)}, u32[]{:S(2)}) collective-permute-start(bf16[1024,256]{1,0:T(8,128)(2,1)S(1)} %bitcast.42), channel_id=1, source_target_pairs={{0,16},{8,24},{16,32},{24,40},{32,48},{40,56},{48,0},{56,8},{64,80... | collective-permute-start | bytes 1572872 | tf_op jit(solution)/shard_map/ppermute | solution.py:149
  42.1 17.5 %collective-permute-start.5 = (bf16[128,2048]{1,0:T(8,128)(2,1)S(1)}, bf16[128,2048]{1,0:T(8,128)(2,1)S(1)}, u32[]{:S(2)}, u32[]{:S(2)}) collective-permute-start(bf16[128,2048]{1,0:T(8,128)(2,1)S(1)} %collective-permute-done.3.r0x), channel_id=1, source_target_pairs={{4,5},{5,6},{6,7},{7,4},{12,13},{13,14},{14,15},{15,12},{20,21},{2... | collective-permute-start | bytes 1572872 | tf_op jit(solution)/shard_map/ppermute | solution.py:146
  44.4 0.8 copy-start
  45.2 14.5 %collective-permute-start.2 = (bf16[128,2048]{1,0:T(8,128)(2,1)S(1)}, bf16[128,2048]{1,0:T(8,128)(2,1)S(1)}, u32[]{:S(2)}, u32[]{:S(2)}) collective-permute-start(bf16[128,2048]{1,0:T(8,128)(2,1)S(1)} %collective-permute-done.1.r0m), channel_id=1, source_target_pairs={{1,0},{2,1},{3,2},{0,3},{7,6},{4,7},{9,8},{10,9},{11,10},{8,11},{1... | collective-permute-start | bytes 1572872 | tf_op jit(solution)/shard_map/ppermute | solution.py:146
  57.7 3.9 %collective-permute-start.21 = (bf16[1024,256]{1,0:T(8,128)(2,1)S(1)}, bf16[1024,256]{1,0:T(8,128)(2,1)S(1)}, u32[]{:S(2)}, u32[]{:S(2)}) collective-permute-start(bf16[1024,256]{1,0:T(8,128)(2,1)S(1)} %bitcast.43), channel_id=1, source_target_pairs={{0,8},{8,0},{16,24},{24,16},{32,40},{40,32},{48,56},{56,48},{64,72... | collective-permute-start | bytes 1572872 | tf_op jit(solution)/shard_map/ppermute | solution.py:149
  57.7 17.7 %collective-permute-start.4 = (bf16[128,2048]{1,0:T(8,128)(2,1)S(1)}, bf16[128,2048]{1,0:T(8,128)(2,1)S(1)}, u32[]{:S(2)}, u32[]{:S(2)}) collective-permute-start(bf16[128,2048]{1,0:T(8,128)(2,1)S(1)} %collective-permute-done.1.r0m), channel_id=1, source_target_pairs={{0,4},{1,5},{2,6},{3,7},{8,12},{9,13},{10,14},{11,15},{16,20},{17,... | collective-permute-start | bytes 1572872 | tf_op jit(solution)/shard_map/ppermute | solution.py:146
  59.0 28.9 %collective-permute-start.24 = (bf16[1024,256]{1,0:T(8,128)(2,1)}, bf16[1024,256]{1,0:T(8,128)(2,1)}, u32[]{:S(2)}, u32[]{:S(2)}) collective-permute-start(bf16[1024,256]{1,0:T(8,128)(2,1)} %collective-permute-done.20.rest_3_), channel_id=1, source_target_pairs={{0,8},{8,0},{16,24},{24,16},{32,40},{40,32},{48,56},{56,48},{64,72... | collective-permute-start | bytes 1572872 | tf_op jit(solution)/shard_map/ppermute | solution.py:149
  59.6 28.3 %collective-permute-start.23 = (bf16[1024,256]{1,0:T(8,128)(2,1)}, bf16[1024,256]{1,0:T(8,128)(2,1)}, u32[]{:S(2)}, u32[]{:S(2)}) collective-permute-start(bf16[1024,256]{1,0:T(8,128)(2,1)} %collective-permute-done.19.rest_2_), channel_id=1, source_target_pairs={{0,8},{8,0},{16,24},{24,16},{32,40},{40,32},{48,56},{56,48},{64,72... | collective-permute-start | bytes 1572872 | tf_op jit(solution)/shard_map/ppermute | solution.py:149
  59.7 28.2 %collective-permute-start.22 = (bf16[1024,256]{1,0:T(8,128)(2,1)}, bf16[1024,256]{1,0:T(8,128)(2,1)}, u32[]{:S(2)}, u32[]{:S(2)}) collective-permute-start(bf16[1024,256]{1,0:T(8,128)(2,1)} %collective-permute-done.18.rest_1_), channel_id=1, source_target_pairs={{0,8},{8,0},{16,24},{24,16},{32,40},{40,32},{48,56},{56,48},{64,72... | collective-permute-start | bytes 1572872 | tf_op jit(solution)/shard_map/ppermute | solution.py:149
  61.6 13.9 %copy-start.4 = (bf16[1024,256]{1,0:T(8,128)(2,1)}, bf16[1024,256]{1,0:T(8,128)(2,1)S(1)}, u32[]{:S(2)}) copy-start(bf16[1024,256]{1,0:T(8,128)(2,1)S(1)} %collective-permute-done.21.rest_4_) | copy-start | bytes 1572868
  61.6 18.0 %collective-permute-start.7 = (bf16[128,1024]{1,0:T(8,128)(2,1)}, bf16[128,1024]{1,0:T(8,128)(2,1)S(1)}, u32[]{:S(2)}, u32[]{:S(2)}) collective-permute-start(bf16[128,1024]{1,0:T(8,128)(2,1)} %slice.37), channel_id=1, source_target_pairs={{4,5},{5,6},{6,7},{7,4},{12,13},{13,14},{14,15},{15,12},{20,21},{2... | collective-permute-start | bytes 786440 | tf_op jit(solution)/shard_map/ppermute | solution.py:146
  75.4 0.8 copy-start.2
  76.2 11.6 %collective-permute-start.6 = (bf16[128,1024]{1,0:T(8,128)(2,1)}, bf16[128,1024]{1,0:T(8,128)(2,1)}, u32[]{:S(2)}, u32[]{:S(2)}) collective-permute-start(bf16[128,1024]{1,0:T(8,128)(2,1)} %slice.36), channel_id=1, source_target_pairs={{0,4},{1,5},{2,6},{3,7},{8,12},{9,13},{10,14},{11,15},{16,20},{17,... | collective-permute-start | bytes 786440 | tf_op jit(solution)/shard_map/ppermute | solution.py:146
  87.9 1.0 copy-start.1
  88.9 1.0 copy-start.3

commit v2 on v0

v2 whole, which is shorter than its diff:
```python
import math

import jax
import jax.numpy as jnp
from jax import lax
from jax.experimental import pallas as pl
from jax.experimental.pallas import tpu as pltpu
from jax.sharding import PartitionSpec as P

DH = 128
ROWS = 128
KVH = 8
GROUP = 8
PAIR = 2 * DH
SCALE_LOG2 = math.log2(math.e) / math.sqrt(DH)
NEG = -1e30
LEAST, MOST = 2.0**-80, 2.0**100
NT = (((1,), (1,)), ((), ()))
TILE = 256
IN_TILE = TILE // ROWS
PARAMS = pltpu.CompilerParams(vmem_limit_bytes=24 << 20)


def cost(heads, keys):
    pairs = GROUP * heads * ROWS * keys
    return pl.CostEstimate(flops=8 * pairs * DH, bytes_accessed=1 << 22, transcendentals=pairs)


def tiles(q_ref, head):
    for t in range(GROUP // IN_TILE):
        lanes = [lane_of(head, h) for h in range(t * IN_TILE, (t + 1) * IN_TILE)]
        yield t, jnp.concatenate([q_ref[:, lane] for lane in lanes], 0)


def lane_of(head, h):
    return pl.ds(pl.multiple_of((head * GROUP + h) * DH, DH), DH)


def causal_mask():
    row = lax.broadcasted_iota(jnp.int32, (TILE, ROWS), 0) % ROWS
    return row >= lax.broadcasted_iota(jnp.int32, (TILE, ROWS), 1)


def sweep(q_ref, head, k_scr, v_scr, n_keys, causal, put):
    for t, q in tiles(q_ref, head):
        s = lax.dot_general(q, k_scr[:n_keys, :], NT, preferred_element_type=jnp.float32)
        s = s * SCALE_LOG2
        if causal:
            s = jnp.concatenate([jnp.where(causal_mask(), s[:, :ROWS], NEG), s[:, ROWS:]], 1)
        p = jnp.exp2(s).astype(jnp.bfloat16)
        sums = jnp.dot(p, v_scr[:n_keys, :], preferred_element_type=jnp.float32)
        for j in range(IN_TILE):
            put(t * IN_TILE + j, sums[j * ROWS : (j + 1) * ROWS])


def place(k_scr, v_scr, slot, ref, ok):
    rows = slice(slot * ROWS, (slot + 1) * ROWS)
    k_scr[rows, :] = ref[:, :DH]
    v_scr[rows, :DH] = jnp.where(ok, ref[:, DH:], jnp.zeros_like(ref[:, DH:]))
    v_scr[rows, DH:] = jnp.where(ok, jnp.ones((ROWS, DH), jnp.float32), 0.0).astype(jnp.bfloat16)


def own_blocks(info):
    z, right = info[9], info[8] == 1
    return (True, z >= 1, z == 3, z >= 2, right, right, right, right)


def own_kernel(info, q_ref, *rest):
    blocks, (tot_ref, acc_ref, k_own, v_own) = rest[:9], rest[9:]
    head = pl.program_id(0)
    allowed = own_blocks(info)
    columns = pl.ds(pl.multiple_of(head * PAIR, PAIR), PAIR)
    half = pl.ds(pl.multiple_of(lax.rem(head, 4) * PAIR, PAIR), PAIR)

    @pl.when(info[11] > 0)
    def _():
        for slot in range(4):
            place(k_own, v_own, slot, blocks[slot][:, columns], allowed[slot])

        for slot in range(4, 7):
            place(k_own, v_own, slot, blocks[slot][:, columns], allowed[slot])

        @pl.when(head < 4)
        def _():
            place(k_own, v_own, 7, blocks[7][:, half], allowed[7])

        @pl.when(head >= 4)
        def _():
            place(k_own, v_own, 7, blocks[8][:, half], allowed[7])

        lane = lax.broadcasted_iota(jnp.int32, (ROWS, DH), 1)
        totals = []

        def put(h, sums):
            acc_ref[:, lane_of(head, h)] = sums[:, :DH]
            totals.append(jnp.where(lane == h, sums[:, DH:], totals[-1] if totals else 0.0))

        sweep(q_ref, head, k_own, v_own, 8 * ROWS, True, put)
        tot_ref[:, pl.ds(pl.multiple_of(head * DH, DH), DH)] = totals[-1]


def prompt_kernel(info, q_ref, tot_in, acc_in, *rest):
    prompt, stored, rest = rest[:KVH], rest[KVH : KVH + 9], rest[KVH + 9 :]
    o_ref, k_pre, v_pre, flag = rest[:4]
    step = pl.program_id(0)
    head = info[step]
    pre_len, n_live = info[10], info[11]
    chunks = (pre_len + 255) // 256
    row = lax.broadcasted_iota(jnp.int32, (ROWS, DH), 0)

    @pl.when(step == 0)
    def _():
        live = lax.broadcasted_iota(jnp.int32, (8 * ROWS, DH), 0) < pre_len
        v_pre[:, DH:] = jnp.where(live, 1.0, 0.0).astype(jnp.bfloat16)

    @pl.when(n_live > 0)
    def _():
        for n, buffer in enumerate(prompt):

            @pl.when(step == n)
            def _(buffer=buffer):
                k_pre[...] = buffer[:, :DH]
                v_pre[:, :DH] = buffer[:, DH:]

        flag[...] = jnp.zeros_like(flag)

        def finish(h, sums):
            totals = tot_in[:, pl.ds(pl.multiple_of(head * DH, DH), DH)]
            total = totals[:, h : h + 1]
            out = acc_in[:, lane_of(head, h)]
            if sums is None:
                total = jnp.broadcast_to(total, (ROWS, DH))
            else:
                total = total + sums[:, DH:]
                out = out + sums[:, :DH]
            wrong = jnp.where((total >= LEAST) & (total <= MOST), 0.0, 1.0)
            flag[...] = jnp.maximum(flag[...], jnp.where(row < n_live, wrong, 0.0))
            out = jnp.where(row < n_live, out / total, 0.0)
            o_ref[:, h * DH : (h + 1) * DH] = out.astype(jnp.bfloat16)

        @pl.when(chunks == 0)
        def _():
            for h in range(GROUP):
                finish(h, None)

        for n in range(1, 5):

            @pl.when(chunks == n)
            def _(n=n):
                sweep(q_ref, head, k_pre, v_pre, 256 * n, False, finish)

        @pl.when(jnp.max(flag[...]) > 0.5)
        def _():
            with_largest(info, head, q_ref, k_pre, v_pre, stored, o_ref, *rest[4:])

    @pl.when(n_live <= 0)
    def _():
        o_ref[...] = jnp.zeros_like(o_ref)


def with_largest(info, head, q_ref, k_pre, v_pre, stored, o_ref, k_aug, v_aug, land, sem):
    pre_len, n_live = info[10], info[11]
    allowed = own_blocks(info)

    def put(rows, count, key, value, ok):
        first = lax.broadcasted_iota(jnp.int32, (count, DH), 1) == 0
        k_aug[rows, :DH] = key
        k_aug[rows, DH:] = jnp.where(first & jnp.logical_not(ok), NEG, 0.0).astype(jnp.bfloat16)
        v_aug[rows, :DH] = value
        v_aug[rows, DH:] = jnp.ones((count, DH), jnp.bfloat16)

    def fetch(source, columns):
        copy = pltpu.make_async_copy(source.at[:, columns], land, sem)
        copy.start()
        copy.wait()

    columns = pl.ds(pl.multiple_of(head * PAIR, PAIR), PAIR)
    half = pl.ds(pl.multiple_of(lax.rem(head, 4) * PAIR, PAIR), PAIR)
    for slot in range(8):
        if slot < 7:
            fetch(stored[slot], columns)
        else:
            for low, source in ((True, stored[7]), (False, stored[8])):

                @pl.when((head < 4) == low)
                def _(source=source):
                    fetch(source, half)

        rows = slice(slot * ROWS, (slot + 1) * ROWS)
        put(rows, ROWS, land[:, :DH], land[:, DH:], allowed[slot])
    position = lax.broadcasted_iota(jnp.int32, (8 * ROWS, DH), 0)
    rows = slice(8 * ROWS, 16 * ROWS)
    put(rows, 8 * ROWS, k_pre[...], v_pre[:, :DH], position < pre_len)

    row = lax.broadcasted_iota(jnp.int32, (ROWS, PAIR), 0)
    col = lax.broadcasted_iota(jnp.int32, (ROWS, PAIR), 1)
    one = jnp.where(col[:, :DH] == 0, 1.0, 0.0).astype(jnp.bfloat16)

    @pl.loop(0, GROUP)
    def _(h):
        lane = pl.ds(pl.multiple_of(h * DH, DH), DH)
        q = jnp.concatenate([q_ref[:, lane_of(head, h)], one], 1)

        def scores(c):
            keys = pl.ds(pl.multiple_of(c * PAIR, PAIR), PAIR)
            s = lax.dot_general(q, k_aug[keys, :], NT, preferred_element_type=jnp.float32)
            return jnp.where((row >= col) | (col >= ROWS) | (c > 0), s, NEG), keys

        def largest(c, top):
            return jnp.maximum(top, jnp.max(scores(c)[0], axis=1, keepdims=True))

        top = lax.fori_loop(0, 8, largest, jnp.full((ROWS, 1), NEG, jnp.float32))

        def weigh(c, acc):
            s, keys = scores(c)
            p = jnp.exp2((s - top) * SCALE_LOG2).astype(jnp.bfloat16)
            return acc + jnp.dot(p, v_aug[keys, :], preferred_element_type=jnp.float32)

        acc = lax.fori_loop(0, 8, weigh, jnp.zeros((ROWS, PAIR), jnp.float32))
        out = jnp.where(row[:, :DH] < n_live, acc[:, :DH] / acc[:, DH:], 0.0)
        o_ref[:, lane] = out.astype(jnp.bfloat16)


VMEM = pl.BlockSpec(memory_space=pltpu.VMEM)
ANY = pl.BlockSpec(memory_space=pl.ANY)


def scratch():
    return [
        pltpu.VMEM((8 * ROWS, DH), jnp.bfloat16),
        pltpu.VMEM((8 * ROWS, PAIR), jnp.bfloat16),
    ]


def attend_own(info, query, own):
    return pl.pallas_call(
        own_kernel,
        grid_spec=pltpu.PrefetchScalarGridSpec(
            num_scalar_prefetch=1,
            grid=(KVH,),
            in_specs=[VMEM] * (1 + len(own)),
            out_specs=(VMEM, VMEM),
            scratch_shapes=scratch(),
        ),
        out_shape=(
            jax.ShapeDtypeStruct((ROWS, KVH * DH), jnp.float32),
            jax.ShapeDtypeStruct((ROWS, KVH * GROUP * DH), jnp.float32),
        ),
        compiler_params=PARAMS,
        cost_estimate=cost(KVH, 8 * ROWS),
        name="own",
    )(info, query, *own)


def attend_prompt(info, query, state, prompt, own):
    return pl.pallas_call(
        prompt_kernel,
        grid_spec=pltpu.PrefetchScalarGridSpec(
            num_scalar_prefetch=1,
            grid=(KVH,),
            in_specs=[VMEM] * (3 + len(prompt)) + [ANY] * len(own),
            out_specs=pl.BlockSpec((ROWS, GROUP * DH), lambda i, info: (0, info[i])),
            scratch_shapes=scratch()
            + [
                pltpu.VMEM((ROWS, DH), jnp.float32),
                pltpu.VMEM((16 * ROWS, PAIR), jnp.bfloat16),
                pltpu.VMEM((16 * ROWS, PAIR), jnp.bfloat16),
                pltpu.VMEM((ROWS, PAIR), jnp.bfloat16),
                pltpu.SemaphoreType.DMA(()),
            ],
        ),
        out_shape=jax.ShapeDtypeStruct(query.shape, jnp.bfloat16),
        compiler_params=PARAMS,
        cost_estimate=cost(KVH, 8 * ROWS),
        name="prompt",
    )(info, query, *state, *prompt, *own)


def pair_kernel(k_ref, v_ref, o_ref, top_ref):
    for h in range(KVH):
        o_ref[:, h * PAIR : h * PAIR + DH] = k_ref[:, h * DH : (h + 1) * DH]
        o_ref[:, h * PAIR + DH : (h + 1) * PAIR] = v_ref[:, h * DH : (h + 1) * DH]
    top_ref[...] = o_ref[:, 4 * PAIR :]


def pair_up(keys, values):
    return pl.pallas_call(
        pair_kernel,
        out_shape=(
            jax.ShapeDtypeStruct((ROWS, KVH * PAIR), jnp.bfloat16),
            jax.ShapeDtypeStruct((ROWS, 4 * PAIR), jnp.bfloat16),
        ),
    )(keys, values)


def on_device(query_rows, key_rows, value_rows, lengths):
    grp = lax.axis_index("grp")
    hd = lax.axis_index("hd")
    core, y, x_lo = grp % 2, (grp // 2) % 4, grp // 8
    z, x_hi = hd % 4, hd // 4
    query = query_rows[0]
    kv, top = pair_up(key_rows[0], value_rows[0])

    def on_hd(value, pairs):
        return lax.ppermute(value, "hd", pairs)

    def on_grp(value, pairs):
        return lax.ppermute(value, "grp", pairs)

    def along_y(value, d):
        return on_grp(value, [(g, (g & 9) | ((g + 2 * d) & 6)) for g in range(16)])

    def along_z(value, d):
        return on_hd(value, [(4 * x + i, 4 * x + (i + d) % 4) for x in range(2) for i in range(4)])

    def swap(value):
        return on_grp(value, [(g, g ^ 1) for g in range(16)])

    def along_x_hi(value):
        return on_hd(value, [(i, i ^ 4) for i in range(8)])

    tie = lax.optimization_barrier

    steps = (0, 1, 3, 2)
    heads = [4 * c + (y - d) % 4 for d in steps for c in (core, 1 - core)]
    pre_len = jnp.where(grp == 0, 0, lengths[0])
    n_live = lengths[grp] - hd * ROWS
    info = jnp.stack([jnp.int32(v) for v in heads + [x_hi, z, pre_len, n_live]])

    r0x, r0p, r0m = along_x_hi(kv), along_z(kv, 1), along_z(kv, 3)
    four = jnp.where(core == 0, kv[:, : 4 * PAIR], swap(top))
    two = jnp.where(y == 2, along_y(four[:, 2 * PAIR :], 2), four[:, : 2 * PAIR])
    r0x, r0p, r0m, two = tie((r0x, r0p, r0m, two))

    r1x, r1p, r1m = along_x_hi(r0m), along_z(r0x, 1), along_z(r0m, 3)
    one = jnp.where(y % 2 == 1, along_y(two[:, PAIR:], 1), two[:, :PAIR])
    r1x, r1p, r1m, one = tie((r1x, r1p, r1m, one))

    r2a, r2b = along_x_hi(r1m[:, : 4 * PAIR]), along_z(r1p[:, 4 * PAIR :], 1)
    piece = jnp.where(x_lo == 0, one, on_grp(one, [(g, g ^ 8) for g in range(16)]))
    other = along_x_hi(piece)
    both = jnp.stack(
        [jnp.where(x_hi == 0, piece, other), jnp.where(x_hi == 0, other, piece)]
    )
    behind = [both] + [along_z(both, d) for d in range(1, 4)]
    orders = [
        jnp.stack([behind[(at - i) % 4] for i in range(4)], 1).reshape(8 * ROWS, PAIR)
        for at in range(4)
    ]
    mine = lax.select_n(z, *orders)
    position = lax.broadcasted_iota(jnp.int32, mine.shape, 0)
    lane = lax.broadcasted_iota(jnp.int32, mine.shape, 1)
    mine = jnp.where((lane < DH) | (position < lengths[0]), mine, 0)

    parts = [mine] + [along_y(mine, d) for d in steps[1:]]
    own = (kv, r0p, r0m, r1m, r0x, r1x, r1p, r2a, r2b)
    state = attend_own(info, query, own)
    parts, state = tie((parts, state))
    prompt = [part for value in parts for part in (value, swap(value))]
    return attend_prompt(info, query, state, prompt, own)[None]


def solution(mesh):
    placed = (P("grp", "hd", None), P("grp", "hd", None), P("grp", "hd", None), P())
    return jax.shard_map(
        on_device, mesh=mesh, in_specs=placed, out_specs=P("grp", "hd", None), check_vma=False
    )
```

time: 318 us -> 425 us (1.34)
  Pallas kernels: 0 us -> 350 us
  waiting for transfers between devices: 130 us -> 30.9 us
  matrix products: 57.2 us -> 0 us
  other arithmetic: 39.9 us -> 3.54 us
  blocking collectives: 32.8 us -> 0 us
  local copies, waits for them, and re-layouts: 25.9 us -> 0.75 us
  starting transfers between devices: 16.3 us -> 36.1 us
  between operations: 13.5 us -> 1.41 us
    pallas_call x0 -> x3, Pallas kernels: none -> 350 us  [the longest x1 335 us: attend_prompt(): pl.pallas_call(prompt_kernel, grid_spec=pltpu.PrefetchScalarGridSpec(num_...]
    psum x1 -> x0, waiting for transfers between devices: 122 us -> none  [spread(): return lax.psum(jnp.where(mine, value, jnp.zeros_like(value)), axis)]
    dot_general x4 -> x0, matrix products: 57.2 us -> none  [the longest x2 29.4 us: per_block(): jnp.einsum('gqk,kd->gqd', weights, v_head, preferred_element_type=jnp.flo...]
    ppermute x0 -> x23, starting transfers between devices: none -> 36.1 us  [the longest x12 20.3 us: on_hd(): return lax.ppermute(value, 'hd', pairs)]
    all_to_all x1 -> x0, blocking collectives: 32.8 us -> none  [on_device(): lax.all_to_all(head_out, 'hd', split_axis=0, concat_axis=1, tiled=True)]
    ppermute x0 -> x23, waiting for transfers between devices: none -> 30.9 us  [the longest x11 18.4 us: on_grp(): return lax.ppermute(value, 'grp', pairs)]
    reduce_sum x2 -> x0, other arithmetic: 30.2 us -> none  [per_block(): total = jnp.sum(probs, -1)]
    all_to_all x3 -> x0, starting transfers between devices: 16.1 us -> none  [the longest x1 8.32 us: on_device(): lax.all_to_all(own_v, 'hd', split_axis=1, concat_axis=0, tiled=True)]
  transfers between devices with their start and end apart: 4 -> 23, of which waited for: 3 -> 14; matrix products, arithmetic and copies ran while one was open for 4% -> 1% of each run, Pallas kernels for 0% -> 3%
where the time goes in v2:
time: 425 us; the launch traced here: 422 us
  Pallas kernels  350 us (82%)
  starting transfers between devices  36.1 us (8%)
  waiting for transfers between devices  30.9 us (7%)
    pallas_call x1, Pallas kernels, attend_prompt(): pl.pallas_call(prompt_kernel, grid_spec=pltpu.PrefetchScalarGridSpec(num_...  335 us
    ppermute x12, starting transfers between devices, on_hd(): return lax.ppermute(value, 'hd', pairs)  20.3 us
    ppermute x11, waiting for transfers between devices, on_grp(): return lax.ppermute(value, 'grp', pairs)  18.4 us
    ppermute x11, starting transfers between devices, on_grp(): return lax.ppermute(value, 'grp', pairs)  15.8 us
    pallas_call x1, Pallas kernels, attend_own(): pl.pallas_call(own_kernel, grid_spec=pltpu.PrefetchScalarGridSpec(num_sca...  12.5 us
    ppermute x12, waiting for transfers between devices, on_hd(): return lax.ppermute(value, 'hd', pairs)  12.5 us
  transfers between devices with their start and end apart: 23, of which 14 were waited for; matrix products, arithmetic and copies ran while one was open for 1% of the time, Pallas kernels for 3%

profile of v2, /device:TPU:1, one launch (start us, length us, event | category | flops | bytes accessed | tf_op | source)
XLA Modules:
  0.0 422.5 jit_solution(17773267563125078260)
XLA Ops:
  0.0 2.0 shard_map.46
  2.0 1.4 collective-permute-start.3
  3.4 3.8 collective-permute-start.2
  7.3 0.0 collective-permute-start.1
  7.3 2.7 collective-permute-start
  10.0 1.0 slice_select_fusion
  11.1 3.0 collective-permute-start.4
  14.1 3.1 collective-permute-done.4
  17.2 1.8 collective-permute-done.2.rest_2_.rest_10_
  19.0 3.0 collective-permute-done.1.rest_1_.rest_9_
  21.9 0.3 collective-permute-done.rest_4_.rest_12_
  22.2 0.0 collective-permute-start.6
  22.2 2.7 collective-permute-start.7
  24.9 2.7 collective-permute-start.5
  27.7 1.3 collective-permute-start.8
  29.0 3.4 collective-permute-done.8
  32.4 3.4 collective-permute-done.6.rest_6_.rest_14_
  35.8 2.4 collective-permute-done.5.rest_5_.rest_13_
  38.2 1.2 collective-permute-start.9
  39.4 1.9 collective-permute-done.9
  41.3 2.8 collective-permute-start.10
  44.1 0.6 fusion.2
  44.7 1.6 collective-permute-done.10
  46.3 0.9 collective-permute-start.12
  47.2 0.9 collective-permute-start.11
  48.1 0.6 collective-permute-start.13
  49.7 0.1 stack.96.info
  49.8 0.6 iota_compare_fusion
  50.4 0.0 copy-start
  50.4 0.0 copy-start.1
  50.5 0.5 collective-permute-start.18
  50.9 2.7 collective-permute-start.17
  53.7 1.6 fusion
  55.4 0.3 or_select_fusion.rest_0_
  55.6 3.0 collective-permute-start.16
  58.6 0.8 collective-permute-start.15
  59.4 0.7 collective-permute-start.14
  60.1 12.5 %own.1 = (f32[128,1024]{1,0:T(8,128)S(1)}, f32[128,8192]{1,0:T(8,128)S(1)}) custom-call(s32[12]{0:T(128)S(1)} %stack.96.info, bf16[128,8192]{1,0:T(8,128)(2,1)S(1)} %bitcast.29, bf16[128,2048]{1,0:T(8,128)(2,1)S(1)} %copy-done, bf16[128,2048]{1,0:T(8,128)(2,1)S(1)} %collective-permute-done.1.rest_1_.rest_9_, ...), custom_call_target="tpu_custom_call" | custom-call | flops 8589934592 | bytes 4194304 | tf_op jit(solution)/shard_map/own/pallas_call | solution.py:236
  72.6 6.7 %collective-permute-done.15.rest_4_ = bf16[1024,256]{1,0:T(8,128)(2,1)S(1)} collective-permute-done((bf16[1024,256]{1,0:T(8,128)(2,1)S(1)}, bf16[1024,256]{1,0:T(8,128)(2,1)S(1)}, u32[]{:S(2)}, u32[]{:S(2)}) %collective-permute-start.15) | collective-permute-done | bytes 524320 | tf_op jit(solution)/shard_map/ppermute | solution.py:308
  79.3 3.9 collective-permute-start.19
  83.2 0.0 collective-permute-start.20
  83.2 0.5 collective-permute-start.21
  83.7 0.0 collective-permute-start.22
  83.7 1.0 collective-permute-done.19.rest_1_
  84.7 0.7 collective-permute-done.20.rest_3_
  85.5 0.7 collective-permute-done.21.rest_5_
  86.2 0.7 collective-permute-done.22.rest_7_
  87.0 335.3 %prompt.1 = bf16[128,8192]{1,0:T(8,128)(2,1)} custom-call(s32[12]{0:T(128)S(1)} %stack.96.info, bf16[128,8192]{1,0:T(8,128)(2,1)S(1)} %bitcast.30, f32[128,1024]{1,0:T(8,128)S(1)} %get-tuple-element.35.tot_in, f32[128,8192]{1,0:T(8,128)S(1)} %get-tuple-element.36.acc_in, bf16[1024,256]{1,0:T(8,128)(2,1)S(1)} %or_select_fusion.rest_0_, ...), custom_call_target="tpu_custom_call" | custom-call | flops 8589934592 | bytes 4194304 | tf_op jit(solution)/shard_map/prompt/pallas_call | solution.py:256
  (24 shorter events, 0.2 us)
Async XLA Ops:
  0.0 44.1 %copy-start.2 = (s32[16]{0:T(128)S(1)}, s32[16]{0:T(128)}, u32[]{:S(2)}) copy-start(s32[16]{0:T(128)} %param.7) | copy-start | bytes 196
  2.0 8.0 %collective-permute-start.3 = (bf16[128,1024]{1,0:T(8,128)(2,1)}, bf16[128,1024]{1,0:T(8,128)(2,1)S(1)}, u32[]{:S(2)}, u32[]{:S(2)}) collective-permute-start(bf16[128,1024]{1,0:T(8,128)(2,1)} %get-tuple-element.24), channel_id=1, source_target_pairs={{0,8},{8,0},{16,24},{24,16},{32,40},{40,32},{48,56},{56,48},{64,72... | collective-permute-start | bytes 786440 | tf_op jit(solution)/shard_map/ppermute | solution.py:308
  3.4 15.5 %collective-permute-start.2 = (bf16[128,2048]{1,0:T(8,128)(2,1)}, bf16[128,2048]{1,0:T(8,128)(2,1)S(1)}, u32[]{:S(2)}, u32[]{:S(2)}) collective-permute-start(bf16[128,2048]{1,0:T(8,128)(2,1)} %get-tuple-element.23.rest_0_.rest_8_), channel_id=1, source_target_pairs={{0,3},{1,0},{2,1},{3,2},{4,7},{5,4},{6,5},{7,6},{8,11},{9,8},{10,9... | collective-permute-start | bytes 1572872 | tf_op jit(solution)/shard_map/ppermute | solution.py:305
  7.3 14.7 %collective-permute-start.1 = (bf16[128,2048]{1,0:T(8,128)(2,1)}, bf16[128,2048]{1,0:T(8,128)(2,1)S(1)}, u32[]{:S(2)}, u32[]{:S(2)}) collective-permute-start(bf16[128,2048]{1,0:T(8,128)(2,1)} %get-tuple-element.23.rest_0_.rest_8_), channel_id=1, source_target_pairs={{0,1},{1,2},{2,3},{3,0},{4,5},{5,6},{6,7},{7,4},{8,9},{9,10},{10,1... | collective-permute-start | bytes 1572872 | tf_op jit(solution)/shard_map/ppermute | solution.py:305
  7.3 15.0 %collective-permute-start = (bf16[128,2048]{1,0:T(8,128)(2,1)}, bf16[128,2048]{1,0:T(8,128)(2,1)S(1)}, u32[]{:S(2)}, u32[]{:S(2)}) collective-permute-start(bf16[128,2048]{1,0:T(8,128)(2,1)} %get-tuple-element.23.rest_0_.rest_8_), channel_id=1, source_target_pairs={{0,4},{1,5},{2,6},{3,7},{4,0},{5,1},{6,2},{7,3},{8,12},{9,13},{10,... | collective-permute-start | bytes 1572872 | tf_op jit(solution)/shard_map/ppermute | solution.py:305
  11.1 6.1 %collective-permute-start.4 = (bf16[128,512]{1,0:T(8,128)(2,1)S(1)}, bf16[128,512]{1,0:T(8,128)(2,1)S(1)}, u32[]{:S(2)}, u32[]{:S(2)}) collective-permute-start(bf16[128,512]{1,0:T(8,128)(2,1)S(1)} %slice.33), channel_id=1, source_target_pairs={{0,32},{8,40},{16,48},{24,56},{32,0},{40,8},{48,16},{56,24},{64,96... | collective-permute-start | bytes 393224 | tf_op jit(solution)/shard_map/ppermute | solution.py:308
  22.2 13.5 %collective-permute-start.6 = (bf16[128,2048]{1,0:T(8,128)(2,1)S(1)}, bf16[128,2048]{1,0:T(8,128)(2,1)S(1)}, u32[]{:S(2)}, u32[]{:S(2)}) collective-permute-start(bf16[128,2048]{1,0:T(8,128)(2,1)S(1)} %collective-permute-done.rest_4_.rest_12_), channel_id=1, source_target_pairs={{0,1},{1,2},{2,3},{3,0},{4,5},{5,6},{6,7},{7,4},{8,9},{9,10},{10,1... | collective-permute-start | bytes 1572872 | tf_op jit(solution)/shard_map/ppermute | solution.py:305
  22.2 13.5 %collective-permute-start.7 = (bf16[128,2048]{1,0:T(8,128)(2,1)S(1)}, bf16[128,2048]{1,0:T(8,128)(2,1)S(1)}, u32[]{:S(2)}, u32[]{:S(2)}) collective-permute-start(bf16[128,2048]{1,0:T(8,128)(2,1)S(1)} %collective-permute-done.2.rest_2_.rest_10_), channel_id=1, source_target_pairs={{0,3},{1,0},{2,1},{3,2},{4,7},{5,4},{6,5},{7,6},{8,11},{9,8},{10,9... | collective-permute-start | bytes 1572872 | tf_op jit(solution)/shard_map/ppermute | solution.py:305
  24.9 13.3 %collective-permute-start.5 = (bf16[128,2048]{1,0:T(8,128)(2,1)S(1)}, bf16[128,2048]{1,0:T(8,128)(2,1)S(1)}, u32[]{:S(2)}, u32[]{:S(2)}) collective-permute-start(bf16[128,2048]{1,0:T(8,128)(2,1)S(1)} %collective-permute-done.2.rest_2_.rest_10_), channel_id=1, source_target_pairs={{0,4},{1,5},{2,6},{3,7},{4,0},{5,1},{6,2},{7,3},{8,12},{9,13},{10,... | collective-permute-start | bytes 1572872 | tf_op jit(solution)/shard_map/ppermute | solution.py:305
  27.7 4.7 %collective-permute-start.8 = (bf16[128,256]{1,0:T(8,128)(2,1)S(1)}, bf16[128,256]{1,0:T(8,128)(2,1)S(1)}, u32[]{:S(2)}, u32[]{:S(2)}) collective-permute-start(bf16[128,256]{1,0:T(8,128)(2,1)S(1)} %slice.29), channel_id=1, source_target_pairs={{0,16},{8,24},{16,32},{24,40},{32,48},{40,56},{48,0},{56,8},{64,80... | collective-permute-start | bytes 196616 | tf_op jit(solution)/shard_map/ppermute | solution.py:308
  38.2 3.1 collective-permute-start.9
  41.3 4.9 %collective-permute-start.10 = (bf16[128,256]{1,0:T(8,128)(2,1)S(1)}, bf16[128,256]{1,0:T(8,128)(2,1)S(1)}, u32[]{:S(2)}, u32[]{:S(2)}) collective-permute-start(bf16[128,256]{1,0:T(8,128)(2,1)S(1)} %broadcast_select_fusion), channel_id=1, source_target_pairs={{0,4},{1,5},{2,6},{3,7},{4,0},{5,1},{6,2},{7,3},{8,12},{9,13},{10,... | collective-permute-start | bytes 196616 | tf_op jit(solution)/shard_map/ppermute | solution.py:305
  46.3 7.4 %collective-permute-start.12 = (bf16[2,128,256]{2,1,0:T(8,128)(2,1)S(1)}, bf16[2,128,256]{2,1,0:T(8,128)(2,1)S(1)}, u32[]{:S(2)}, u32[]{:S(2)}) collective-permute-start(bf16[2,128,256]{2,1,0:T(8,128)(2,1)S(1)} %get-tuple-element.42), channel_id=1, source_target_pairs={{0,2},{1,3},{2,0},{3,1},{4,6},{5,7},{6,4},{7,5},{8,10},{9,11},{10,... | collective-permute-start | bytes 393224 | tf_op jit(solution)/shard_map/ppermute | solution.py:305
  47.2 6.5 %collective-permute-start.11 = (bf16[2,128,256]{2,1,0:T(8,128)(2,1)S(1)}, bf16[2,128,256]{2,1,0:T(8,128)(2,1)}, u32[]{:S(2)}, u32[]{:S(2)}) collective-permute-start(bf16[2,128,256]{2,1,0:T(8,128)(2,1)S(1)} %get-tuple-element.42), channel_id=1, source_target_pairs={{0,3},{1,0},{2,1},{3,2},{4,7},{5,4},{6,5},{7,6},{8,11},{9,8},{10,9... | collective-permute-start | bytes 393224 | tf_op jit(solution)/shard_map/ppermute | solution.py:305
  48.1 5.6 %collective-permute-start.13 = (bf16[2,128,256]{2,1,0:T(8,128)(2,1)S(1)}, bf16[2,128,256]{2,1,0:T(8,128)(2,1)}, u32[]{:S(2)}, u32[]{:S(2)}) collective-permute-start(bf16[2,128,256]{2,1,0:T(8,128)(2,1)S(1)} %get-tuple-element.42), channel_id=1, source_target_pairs={{0,1},{1,2},{2,3},{3,0},{4,5},{5,6},{6,7},{7,4},{8,9},{9,10},{10,1... | collective-permute-start | bytes 393224 | tf_op jit(solution)/shard_map/ppermute | solution.py:305
  50.4 9.7 %copy-start = (bf16[128,2048]{1,0:T(8,128)(2,1)S(1)}, bf16[128,2048]{1,0:T(8,128)(2,1)}, u32[]{:S(2)}) copy-start(bf16[128,2048]{1,0:T(8,128)(2,1)} %get-tuple-element.23.rest_0_.rest_8_) | copy-start | bytes 1572868
  50.4 9.7 %copy-start.1 = (bf16[1,128,8192]{2,1,0:T(8,128)(2,1)S(1)}, bf16[1,128,8192]{2,1,0:T(8,128)(2,1)}, u32[]{:S(2)}) copy-start(bf16[1,128,8192]{2,1,0:T(8,128)(2,1)} %param.4) | copy-start | bytes 6291460
  50.5 9.6 %collective-permute-start.18 = (bf16[128,1024]{1,0:T(8,128)(2,1)S(1)}, bf16[128,1024]{1,0:T(8,128)(2,1)S(1)}, u32[]{:S(2)}, u32[]{:S(2)}) collective-permute-start(bf16[128,1024]{1,0:T(8,128)(2,1)S(1)} %slice.32), channel_id=1, source_target_pairs={{0,1},{1,2},{2,3},{3,0},{4,5},{5,6},{6,7},{7,4},{8,9},{9,10},{10,1... | collective-permute-start | bytes 786440 | tf_op jit(solution)/shard_map/ppermute | solution.py:305
  50.9 9.1 %collective-permute-start.17 = (bf16[128,1024]{1,0:T(8,128)(2,1)S(1)}, bf16[128,1024]{1,0:T(8,128)(2,1)S(1)}, u32[]{:S(2)}, u32[]{:S(2)}) collective-permute-start(bf16[128,1024]{1,0:T(8,128)(2,1)S(1)} %slice.31), channel_id=1, source_target_pairs={{0,4},{1,5},{2,6},{3,7},{4,0},{5,1},{6,2},{7,3},{8,12},{9,13},{10,... | collective-permute-start | bytes 786440 | tf_op jit(solution)/shard_map/ppermute | solution.py:305
  55.6 17.0 %collective-permute-start.16 = (bf16[1024,256]{1,0:T(8,128)(2,1)S(1)}, bf16[1024,256]{1,0:T(8,128)(2,1)S(1)}, u32[]{:S(2)}, u32[]{:S(2)}) collective-permute-start(bf16[1024,256]{1,0:T(8,128)(2,1)S(1)} %or_select_fusion.rest_0_), channel_id=1, source_target_pairs={{0,32},{8,40},{16,48},{24,56},{32,0},{40,8},{48,16},{56,24},{64,96... | collective-permute-start | bytes 1572872 | tf_op jit(solution)/shard_map/ppermute | solution.py:308
  58.6 20.7 %collective-permute-start.15 = (bf16[1024,256]{1,0:T(8,128)(2,1)S(1)}, bf16[1024,256]{1,0:T(8,128)(2,1)S(1)}, u32[]{:S(2)}, u32[]{:S(2)}) collective-permute-start(bf16[1024,256]{1,0:T(8,128)(2,1)S(1)} %or_select_fusion.rest_0_), channel_id=1, source_target_pairs={{0,48},{8,56},{16,0},{24,8},{32,16},{40,24},{48,32},{56,40},{64,11... | collective-permute-start | bytes 1572872 | tf_op jit(solution)/shard_map/ppermute | solution.py:308
  59.4 20.0 %collective-permute-start.14 = (bf16[1024,256]{1,0:T(8,128)(2,1)S(1)}, bf16[1024,256]{1,0:T(8,128)(2,1)S(1)}, u32[]{:S(2)}, u32[]{:S(2)}) collective-permute-start(bf16[1024,256]{1,0:T(8,128)(2,1)S(1)} %or_select_fusion.rest_0_), channel_id=1, source_target_pairs={{0,16},{8,24},{16,32},{24,40},{32,48},{40,56},{48,0},{56,8},{64,80... | collective-permute-start | bytes 1572872 | tf_op jit(solution)/shard_map/ppermute | solution.py:308
  79.3 5.4 %collective-permute-start.19 = (bf16[1024,256]{1,0:T(8,128)(2,1)S(1)}, bf16[1024,256]{1,0:T(8,128)(2,1)S(1)}, u32[]{:S(2)}, u32[]{:S(2)}) collective-permute-start(bf16[1024,256]{1,0:T(8,128)(2,1)S(1)} %or_select_fusion.rest_0_), channel_id=1, source_target_pairs={{0,8},{8,0},{16,24},{24,16},{32,40},{40,32},{48,56},{56,48},{64,72... | collective-permute-start | bytes 1572872 | tf_op jit(solution)/shard_map/ppermute | solution.py:308
  83.2 2.3 collective-permute-start.20
  83.2 3.0 collective-permute-start.21
  83.7 3.3 collective-permute-start.22

commit v3 on v2

--- a/solution.py
+++ b/solution.py
@@ -329,19 +329,19 @@
 
     r0x, r0p, r0m = along_x_hi(kv), along_z(kv, 1), along_z(kv, 3)
     four = jnp.where(core == 0, kv[:, : 4 * PAIR], swap(top))
-    two = jnp.where(y == 2, along_y(four[:, 2 * PAIR :], 2), four[:, : 2 * PAIR])
-    r0x, r0p, r0m, two = tie((r0x, r0p, r0m, two))
-
-    r1x, r1p, r1m = along_x_hi(r0m), along_z(r0x, 1), along_z(r0m, 3)
-    one = jnp.where(y % 2 == 1, along_y(two[:, PAIR:], 1), two[:, :PAIR])
-    r1x, r1p, r1m, one = tie((r1x, r1p, r1m, one))
-
-    r2a, r2b = along_x_hi(r1m[:, : 4 * PAIR]), along_z(r1p[:, 4 * PAIR :], 1)
+    one = four[:, :PAIR]
+    for d in range(1, 4):
+        one = jnp.where(y == d, along_y(four[:, d * PAIR : (d + 1) * PAIR], d), one)
+    r0x, r0p, r0m, one = tie((r0x, r0p, r0m, one))
+
     piece = jnp.where(x_lo == 0, one, on_grp(one, [(g, g ^ 8) for g in range(16)]))
-    other = along_x_hi(piece)
+    other, r0x_t, r0m_t = tie((along_x_hi(piece), r0x, r0m))
     both = jnp.stack(
         [jnp.where(x_hi == 0, piece, other), jnp.where(x_hi == 0, other, piece)]
     )
+
+    r1x, r1p, r1m = along_x_hi(r0m_t), along_z(r0x_t, 1), along_z(r0m_t, 3)
+    r2a, r2b = along_x_hi(r1m[:, : 4 * PAIR]), along_z(r1p[:, 4 * PAIR :], 1)
     behind = [both] + [along_z(both, d) for d in range(1, 4)]
     orders = [
         jnp.stack([behind[(at - i) % 4] for i in range(4)], 1).reshape(8 * ROWS, PAIR)
@@ -352,11 +352,11 @@
     lane = lax.broadcasted_iota(jnp.int32, mine.shape, 1)
     mine = jnp.where((lane < DH) | (position < lengths[0]), mine, 0)
 
-    parts = [mine] + [along_y(mine, d) for d in steps[1:]]
+    m, e1, e3, e2 = [mine] + [along_y(mine, d) for d in steps[1:]]
     own = (kv, r0p, r0m, r1m, r0x, r1x, r1p, r2a, r2b)
     state = attend_own(info, query, own)
-    parts, state = tie((parts, state))
-    prompt = [part for value in parts for part in (value, swap(value))]
+    (m, e1, e3, e2), state = tie(((m, e1, e3, e2), state))
+    prompt = [part for value in (m, e1, e3, e2) for part in (value, swap(value))]
     return attend_prompt(info, query, state, prompt, own)[None]
 
 

time: 425 us -> 416 us (0.979)
  waiting for transfers between devices: 30.9 us -> 22.2 us
    ppermute x11 -> x12, waiting for transfers between devices: 18.4 us -> 11.9 us  [on_grp(): return lax.ppermute(value, 'grp', pairs)]
    ppermute x11 -> x12, starting transfers between devices: 15.8 us -> 19 us  [on_grp(): return lax.ppermute(value, 'grp', pairs)]
  transfers between devices with their start and end apart: 23 -> 24, of which waited for: 14 -> 14; matrix products, arithmetic and copies ran while one was open for 1% -> 1% of each run, Pallas kernels for 3% -> 3%
where the time goes in v3:
time: 416 us
  Pallas kernels  350 us (84%)
  starting transfers between devices  37.9 us (9%)
  waiting for transfers between devices  22.2 us (5%)
    pallas_call x1, Pallas kernels, attend_prompt(): pl.pallas_call(prompt_kernel, grid_spec=pltpu.PrefetchScalarGridSpec(num_...  335 us
    ppermute x12, starting transfers between devices, on_grp(): return lax.ppermute(value, 'grp', pairs)  19 us
    ppermute x12, starting transfers between devices, on_hd(): return lax.ppermute(value, 'hd', pairs)  18.8 us
    pallas_call x1, Pallas kernels, attend_own(): pl.pallas_call(own_kernel, grid_spec=pltpu.PrefetchScalarGridSpec(num_sca...  12.5 us
    ppermute x12, waiting for transfers between devices, on_grp(): return lax.ppermute(value, 'grp', pairs)  11.9 us
    ppermute x12, waiting for transfers between devices, on_hd(): return lax.ppermute(value, 'hd', pairs)  10.3 us
  transfers between devices with their start and end apart: 24, of which 14 were waited for; matrix products, arithmetic and copies ran while one was open for 1% of the time, Pallas kernels for 3%

profile of v3, /device:TPU:1, one launch (start us, length us, event | category | flops | bytes accessed | tf_op | source)
XLA Modules:
  0.0 415.9 jit_solution(244082155265468782)
XLA Ops:
  0.0 2.0 shard_map.46
  2.0 1.4 collective-permute-start.3
  3.4 3.8 collective-permute-start.2
  7.3 0.0 collective-permute-start.1
  7.3 2.7 collective-permute-start
  10.0 1.0 slice_select_fusion
  11.1 1.4 collective-permute-start.6
  12.4 2.6 collective-permute-start.5
  15.0 0.8 collective-permute-done.6
  15.8 1.5 collective-permute-start.4
  17.3 0.8 collective-permute-done.5
  18.1 1.2 collective-permute-done.4
  19.3 2.7 collective-permute-done.1.rest_1_.rest_9_
  21.9 0.3 collective-permute-done.rest_4_.rest_12_
  22.2 1.2 collective-permute-start.7
  23.4 1.9 collective-permute-done.7
  25.4 2.8 collective-permute-start.8
  28.2 1.9 collective-permute-done.8
  30.1 0.6 fusion.5
  30.7 2.7 collective-permute-start.15
  33.4 1.0 collective-permute-start.10
  34.4 0.4 collective-permute-start.9
  34.8 1.1 collective-permute-start.11
  35.9 0.7 iota_compare_fusion
  36.6 4.7 %collective-permute-done.17.rest_6_.rest_14_ = bf16[128,2048]{1,0:T(8,128)(2,1)S(1)} collective-permute-done((bf16[128,2048]{1,0:T(8,128)(2,1)S(1)}, bf16[128,2048]{1,0:T(8,128)(2,1)S(1)}, u32[]{:S(2)}, u32[]{:S(2)}) %collective-permute-start.17) | collective-permute-done | bytes 524320 | tf_op jit(solution)/shard_map/ppermute | solution.py:305
  41.3 2.7 collective-permute-start.16
  45.4 0.1 stack.96.info
  45.4 0.0 copy-start
  45.5 0.0 copy-start.1
  45.5 0.1 collective-permute-start.19
  45.6 1.5 collective-permute-start.18
  47.1 1.6 fusion
  48.8 0.3 or_select_fusion.rest_0_
  49.0 3.0 collective-permute-start.14
  52.0 0.8 collective-permute-start.13
  52.8 0.7 collective-permute-start.12
  53.5 0.7 collective-permute-done.18.rest_7_.rest_15_
  54.2 12.5 %own.1 = (f32[128,1024]{1,0:T(8,128)S(1)}, f32[128,8192]{1,0:T(8,128)S(1)}) custom-call(s32[12]{0:T(128)S(1)} %stack.96.info, bf16[128,8192]{1,0:T(8,128)(2,1)S(1)} %bitcast.29, bf16[128,2048]{1,0:T(8,128)(2,1)S(1)} %copy-done, bf16[128,2048]{1,0:T(8,128)(2,1)S(1)} %collective-permute-done.1.rest_1_.rest_9_, ...), custom_call_target="tpu_custom_call" | custom-call | flops 8589934592 | bytes 4194304 | tf_op jit(solution)/shard_map/own/pallas_call | solution.py:236
  66.7 4.0 collective-permute-done.13.rest_4_
  70.7 6.0 %collective-permute-start.20 = (bf16[1024,256]{1,0:T(8,128)(2,1)S(1)}, bf16[1024,256]{1,0:T(8,128)(2,1)S(1)}, u32[]{:S(2)}, u32[]{:S(2)}) collective-permute-start(bf16[1024,256]{1,0:T(8,128)(2,1)S(1)} %or_select_fusion.rest_0_), channel_id=1, source_target_pairs={{0,8},{8,0},{16,24},{24,16},{32,40},{40,32},{48,56},{56,48},{64,72... | collective-permute-start | bytes 1572872 | tf_op jit(solution)/shard_map/ppermute | solution.py:308
  76.6 0.0 collective-permute-start.21
  76.6 0.5 collective-permute-start.22
  77.2 0.0 collective-permute-start.23
  77.2 1.0 collective-permute-done.20.rest_1_
  78.2 0.7 collective-permute-done.21.rest_3_
  78.9 0.7 collective-permute-done.22.rest_5_
  79.7 0.7 collective-permute-done.23.rest_7_
  80.4 335.3 %prompt.1 = bf16[128,8192]{1,0:T(8,128)(2,1)} custom-call(s32[12]{0:T(128)S(1)} %stack.96.info, bf16[128,8192]{1,0:T(8,128)(2,1)S(1)} %bitcast.30, f32[128,1024]{1,0:T(8,128)S(1)} %get-tuple-element.33.tot_in, f32[128,8192]{1,0:T(8,128)S(1)} %get-tuple-element.34.acc_in, bf16[1024,256]{1,0:T(8,128)(2,1)S(1)} %or_select_fusion.rest_0_, ...), custom_call_target="tpu_custom_call" | custom-call | flops 8589934592 | bytes 4194304 | tf_op jit(solution)/shard_map/prompt/pallas_call | solution.py:256
  (24 shorter events, 0.2 us)
Async XLA Ops:
  0.0 30.1 %copy-start.2 = (s32[16]{0:T(128)S(1)}, s32[16]{0:T(128)}, u32[]{:S(2)}) copy-start(s32[16]{0:T(128)} %param.7) | copy-start | bytes 196
  2.0 8.0 %collective-permute-start.3 = (bf16[128,1024]{1,0:T(8,128)(2,1)}, bf16[128,1024]{1,0:T(8,128)(2,1)S(1)}, u32[]{:S(2)}, u32[]{:S(2)}) collective-permute-start(bf16[128,1024]{1,0:T(8,128)(2,1)} %get-tuple-element.23), channel_id=1, source_target_pairs={{0,8},{8,0},{16,24},{24,16},{32,40},{40,32},{48,56},{56,48},{64,72... | collective-permute-start | bytes 786440 | tf_op jit(solution)/shard_map/ppermute | solution.py:308
  3.4 15.8 %collective-permute-start.2 = (bf16[128,2048]{1,0:T(8,128)(2,1)}, bf16[128,2048]{1,0:T(8,128)(2,1)S(1)}, u32[]{:S(2)}, u32[]{:S(2)}) collective-permute-start(bf16[128,2048]{1,0:T(8,128)(2,1)} %get-tuple-element.22.rest_0_.rest_8_), channel_id=1, source_target_pairs={{0,3},{1,0},{2,1},{3,2},{4,7},{5,4},{6,5},{7,6},{8,11},{9,8},{10,9... | collective-permute-start | bytes 1572872 | tf_op jit(solution)/shard_map/ppermute | solution.py:305
  7.3 14.7 %collective-permute-start.1 = (bf16[128,2048]{1,0:T(8,128)(2,1)}, bf16[128,2048]{1,0:T(8,128)(2,1)S(1)}, u32[]{:S(2)}, u32[]{:S(2)}) collective-permute-start(bf16[128,2048]{1,0:T(8,128)(2,1)} %get-tuple-element.22.rest_0_.rest_8_), channel_id=1, source_target_pairs={{0,1},{1,2},{2,3},{3,0},{4,5},{5,6},{6,7},{7,4},{8,9},{9,10},{10,1... | collective-permute-start | bytes 1572872 | tf_op jit(solution)/shard_map/ppermute | solution.py:305
  7.3 15.0 %collective-permute-start = (bf16[128,2048]{1,0:T(8,128)(2,1)}, bf16[128,2048]{1,0:T(8,128)(2,1)S(1)}, u32[]{:S(2)}, u32[]{:S(2)}) collective-permute-start(bf16[128,2048]{1,0:T(8,128)(2,1)} %get-tuple-element.22.rest_0_.rest_8_), channel_id=1, source_target_pairs={{0,4},{1,5},{2,6},{3,7},{4,0},{5,1},{6,2},{7,3},{8,12},{9,13},{10,... | collective-permute-start | bytes 1572872 | tf_op jit(solution)/shard_map/ppermute | solution.py:305
  11.1 4.8 %collective-permute-start.6 = (bf16[128,256]{1,0:T(8,128)(2,1)S(1)}, bf16[128,256]{1,0:T(8,128)(2,1)S(1)}, u32[]{:S(2)}, u32[]{:S(2)}) collective-permute-start(bf16[128,256]{1,0:T(8,128)(2,1)S(1)} %get-tuple-element.39), channel_id=1, source_target_pairs={{0,16},{8,24},{16,32},{24,40},{32,48},{40,56},{48,0},{56,8},{64,80... | collective-permute-start | bytes 196616 | tf_op jit(solution)/shard_map/ppermute | solution.py:308
  12.4 5.6 %collective-permute-start.5 = (bf16[128,256]{1,0:T(8,128)(2,1)S(1)}, bf16[128,256]{1,0:T(8,128)(2,1)S(1)}, u32[]{:S(2)}, u32[]{:S(2)}) collective-permute-start(bf16[128,256]{1,0:T(8,128)(2,1)S(1)} %get-tuple-element.40), channel_id=1, source_target_pairs={{0,32},{8,40},{16,48},{24,56},{32,0},{40,8},{48,16},{56,24},{64,96... | collective-permute-start | bytes 196616 | tf_op jit(solution)/shard_map/ppermute | solution.py:308
  15.8 3.4 collective-permute-start.4
  22.2 3.1 collective-permute-start.7
  25.4 4.7 %collective-permute-start.8 = (bf16[128,256]{1,0:T(8,128)(2,1)S(1)}, bf16[128,256]{1,0:T(8,128)(2,1)S(1)}, u32[]{:S(2)}, u32[]{:S(2)}) collective-permute-start(bf16[128,256]{1,0:T(8,128)(2,1)S(1)} %broadcast_select_fusion), channel_id=1, source_target_pairs={{0,4},{1,5},{2,6},{3,7},{4,0},{5,1},{6,2},{7,3},{8,12},{9,13},{10,... | collective-permute-start | bytes 196616 | tf_op jit(solution)/shard_map/ppermute | solution.py:305
  30.1 11.2 %collective-permute-start.17 = (bf16[128,2048]{1,0:T(8,128)(2,1)S(1)}, bf16[128,2048]{1,0:T(8,128)(2,1)S(1)}, u32[]{:S(2)}, u32[]{:S(2)}) collective-permute-start(bf16[128,2048]{1,0:T(8,128)(2,1)S(1)} %collective-permute-done.rest_4_.rest_12_), channel_id=1, source_target_pairs={{0,1},{1,2},{2,3},{3,0},{4,5},{5,6},{6,7},{7,4},{8,9},{9,10},{10,1... | collective-permute-start | bytes 1572872 | tf_op jit(solution)/shard_map/ppermute | solution.py:305
  30.7 14.8 %collective-permute-start.15 = (bf16[128,2048]{1,0:T(8,128)(2,1)S(1)}, bf16[128,2048]{1,0:T(8,128)(2,1)S(1)}, u32[]{:S(2)}, u32[]{:S(2)}) collective-permute-start(bf16[128,2048]{1,0:T(8,128)(2,1)S(1)} %collective-permute-done.2.rest_2_.rest_10_), channel_id=1, source_target_pairs={{0,3},{1,0},{2,1},{3,2},{4,7},{5,4},{6,5},{7,6},{8,11},{9,8},{10,9... | collective-permute-start | bytes 1572872 | tf_op jit(solution)/shard_map/ppermute | solution.py:305
  33.4 12.2 %collective-permute-start.10 = (bf16[2,128,256]{2,1,0:T(8,128)(2,1)S(1)}, bf16[2,128,256]{2,1,0:T(8,128)(2,1)S(1)}, u32[]{:S(2)}, u32[]{:S(2)}) collective-permute-start(bf16[2,128,256]{2,1,0:T(8,128)(2,1)S(1)} %get-tuple-element.43), channel_id=1, source_target_pairs={{0,2},{1,3},{2,0},{3,1},{4,6},{5,7},{6,4},{7,5},{8,10},{9,11},{10,... | collective-permute-start | bytes 393224 | tf_op jit(solution)/shard_map/ppermute | solution.py:305
  34.4 12.7 %collective-permute-start.9 = (bf16[2,128,256]{2,1,0:T(8,128)(2,1)S(1)}, bf16[2,128,256]{2,1,0:T(8,128)(2,1)}, u32[]{:S(2)}, u32[]{:S(2)}) collective-permute-start(bf16[2,128,256]{2,1,0:T(8,128)(2,1)S(1)} %get-tuple-element.43), channel_id=1, source_target_pairs={{0,3},{1,0},{2,1},{3,2},{4,7},{5,4},{6,5},{7,6},{8,11},{9,8},{10,9... | collective-permute-start | bytes 393224 | tf_op jit(solution)/shard_map/ppermute | solution.py:305
  34.8 12.3 %collective-permute-start.11 = (bf16[2,128,256]{2,1,0:T(8,128)(2,1)S(1)}, bf16[2,128,256]{2,1,0:T(8,128)(2,1)}, u32[]{:S(2)}, u32[]{:S(2)}) collective-permute-start(bf16[2,128,256]{2,1,0:T(8,128)(2,1)S(1)} %get-tuple-element.43), channel_id=1, source_target_pairs={{0,1},{1,2},{2,3},{3,0},{4,5},{5,6},{6,7},{7,4},{8,9},{9,10},{10,1... | collective-permute-start | bytes 393224 | tf_op jit(solution)/shard_map/ppermute | solution.py:305
  41.3 11.5 %collective-permute-start.16 = (bf16[128,2048]{1,0:T(8,128)(2,1)S(1)}, bf16[128,2048]{1,0:T(8,128)(2,1)S(1)}, u32[]{:S(2)}, u32[]{:S(2)}) collective-permute-start(bf16[128,2048]{1,0:T(8,128)(2,1)S(1)} %collective-permute-done.2.rest_2_.rest_10_), channel_id=1, source_target_pairs={{0,4},{1,5},{2,6},{3,7},{4,0},{5,1},{6,2},{7,3},{8,12},{9,13},{10,... | collective-permute-start | bytes 1572872 | tf_op jit(solution)/shard_map/ppermute | solution.py:305
  45.4 8.8 %copy-start = (bf16[128,2048]{1,0:T(8,128)(2,1)S(1)}, bf16[128,2048]{1,0:T(8,128)(2,1)}, u32[]{:S(2)}) copy-start(bf16[128,2048]{1,0:T(8,128)(2,1)} %get-tuple-element.22.rest_0_.rest_8_) | copy-start | bytes 1572868
  45.5 8.8 %copy-start.1 = (bf16[1,128,8192]{2,1,0:T(8,128)(2,1)S(1)}, bf16[1,128,8192]{2,1,0:T(8,128)(2,1)}, u32[]{:S(2)}) copy-start(bf16[1,128,8192]{2,1,0:T(8,128)(2,1)} %param.4) | copy-start | bytes 6291460
  45.5 8.0 %collective-permute-start.19 = (bf16[128,1024]{1,0:T(8,128)(2,1)S(1)}, bf16[128,1024]{1,0:T(8,128)(2,1)S(1)}, u32[]{:S(2)}, u32[]{:S(2)}) collective-permute-start(bf16[128,1024]{1,0:T(8,128)(2,1)S(1)} %slice.38), channel_id=1, source_target_pairs={{0,1},{1,2},{2,3},{3,0},{4,5},{5,6},{6,7},{7,4},{8,9},{9,10},{10,1... | collective-permute-start | bytes 786440 | tf_op jit(solution)/shard_map/ppermute | solution.py:305
  45.6 8.6 %collective-permute-start.18 = (bf16[128,1024]{1,0:T(8,128)(2,1)S(1)}, bf16[128,1024]{1,0:T(8,128)(2,1)S(1)}, u32[]{:S(2)}, u32[]{:S(2)}) collective-permute-start(bf16[128,1024]{1,0:T(8,128)(2,1)S(1)} %slice.37), channel_id=1, source_target_pairs={{0,4},{1,5},{2,6},{3,7},{4,0},{5,1},{6,2},{7,3},{8,12},{9,13},{10,... | collective-permute-start | bytes 786440 | tf_op jit(solution)/shard_map/ppermute | solution.py:305
  49.0 17.6 %collective-permute-start.14 = (bf16[1024,256]{1,0:T(8,128)(2,1)S(1)}, bf16[1024,256]{1,0:T(8,128)(2,1)S(1)}, u32[]{:S(2)}, u32[]{:S(2)}) collective-permute-start(bf16[1024,256]{1,0:T(8,128)(2,1)S(1)} %or_select_fusion.rest_0_), channel_id=1, source_target_pairs={{0,32},{8,40},{16,48},{24,56},{32,0},{40,8},{48,16},{56,24},{64,96... | collective-permute-start | bytes 1572872 | tf_op jit(solution)/shard_map/ppermute | solution.py:308
  52.0 18.6 %collective-permute-start.13 = (bf16[1024,256]{1,0:T(8,128)(2,1)S(1)}, bf16[1024,256]{1,0:T(8,128)(2,1)S(1)}, u32[]{:S(2)}, u32[]{:S(2)}) collective-permute-start(bf16[1024,256]{1,0:T(8,128)(2,1)S(1)} %or_select_fusion.rest_0_), channel_id=1, source_target_pairs={{0,48},{8,56},{16,0},{24,8},{32,16},{40,24},{48,32},{56,40},{64,11... | collective-permute-start | bytes 1572872 | tf_op jit(solution)/shard_map/ppermute | solution.py:308
  52.8 17.8 %collective-permute-start.12 = (bf16[1024,256]{1,0:T(8,128)(2,1)S(1)}, bf16[1024,256]{1,0:T(8,128)(2,1)S(1)}, u32[]{:S(2)}, u32[]{:S(2)}) collective-permute-start(bf16[1024,256]{1,0:T(8,128)(2,1)S(1)} %or_select_fusion.rest_0_), channel_id=1, source_target_pairs={{0,16},{8,24},{16,32},{24,40},{32,48},{40,56},{48,0},{56,8},{64,80... | collective-permute-start | bytes 1572872 | tf_op jit(solution)/shard_map/ppermute | solution.py:308
  70.7 7.5 %collective-permute-start.20 = (bf16[1024,256]{1,0:T(8,128)(2,1)S(1)}, bf16[1024,256]{1,0:T(8,128)(2,1)S(1)}, u32[]{:S(2)}, u32[]{:S(2)}) collective-permute-start(bf16[1024,256]{1,0:T(8,128)(2,1)S(1)} %or_select_fusion.rest_0_), channel_id=1, source_target_pairs={{0,8},{8,0},{16,24},{24,16},{32,40},{40,32},{48,56},{56,48},{64,72... | collective-permute-start | bytes 1572872 | tf_op jit(solution)/shard_map/ppermute | solution.py:308
  76.6 2.3 collective-permute-start.21
  76.6 3.0 collective-permute-start.22
  77.2 3.3 collective-permute-start.23

commit v4 on v3

--- a/solution.py
+++ b/solution.py
@@ -1,3 +1,4 @@
+import functools
 import math
 
 import jax
@@ -89,73 +90,106 @@
             place(k_own, v_own, 7, blocks[8][:, half], allowed[7])
 
         lane = lax.broadcasted_iota(jnp.int32, (ROWS, DH), 1)
-        totals = []
-
-        def put(h, sums):
-            acc_ref[:, lane_of(head, h)] = sums[:, :DH]
-            totals.append(jnp.where(lane == h, sums[:, DH:], totals[-1] if totals else 0.0))
-
-        sweep(q_ref, head, k_own, v_own, 8 * ROWS, True, put)
-        tot_ref[:, pl.ds(pl.multiple_of(head * DH, DH), DH)] = totals[-1]
-
-
-def prompt_kernel(info, q_ref, tot_in, acc_in, *rest):
-    prompt, stored, rest = rest[:KVH], rest[KVH : KVH + 9], rest[KVH + 9 :]
-    o_ref, k_pre, v_pre, flag = rest[:4]
-    step = pl.program_id(0)
-    head = info[step]
+
+        def run(n_keys):
+            totals = []
+
+            def put(h, sums):
+                acc_ref[:, lane_of(head, h)] = sums[:, :DH]
+                totals.append(jnp.where(lane == h, sums[:, DH:], totals[-1] if totals else 0.0))
+
+            sweep(q_ref, head, k_own, v_own, n_keys, True, put)
+            tot_ref[:, pl.ds(pl.multiple_of(head * DH, DH), DH)] = totals[-1]
+
+        @pl.when(info[8] == 1)
+        def _():
+            run(8 * ROWS)
+
+        @pl.when(info[8] == 0)
+        def _():
+            run(4 * ROWS)
+
+
+def prompt_kernel(first, count, aliased, info, q_ref, tot_in, acc_in, *rest):
+    prompt, stored, rest = rest[:count], rest[count : count + 9], rest[count + 9 + aliased :]
+    o_hbm, k_pre, v_pre, out, flags, sems = rest[:6]
     pre_len, n_live = info[10], info[11]
     chunks = (pre_len + 255) // 256
     row = lax.broadcasted_iota(jnp.int32, (ROWS, DH), 0)
 
-    @pl.when(step == 0)
+    def store(i):
+        columns = pl.ds(pl.multiple_of(info[first + i] * GROUP * DH, GROUP * DH), GROUP * DH)
+        return pltpu.make_async_copy(out.at[i], o_hbm.at[:, columns], sems.at[i])
+
+    def take(i):
+        for n, buffer in enumerate(prompt):
+
+            @pl.when(i == n)
+            def _(buffer=buffer):
+                k_pre[...] = buffer[:, :DH]
+                v_pre[:, :DH] = buffer[:, DH:]
+
+    def attend(n_keys):
+        @pl.loop(0, count)
+        def _(i):
+            head = info[first + i]
+            take(i)
+            flags[i] = jnp.zeros((ROWS, DH), jnp.float32)
+
+            def finish(h, sums):
+                totals = tot_in[:, pl.ds(pl.multiple_of(head * DH, DH), DH)]
+                total = totals[:, h : h + 1]
+                value = acc_in[:, lane_of(head, h)]
+                if sums is None:
+                    total = jnp.broadcast_to(total, (ROWS, DH))
+                else:
+                    total = total + sums[:, DH:]
+                    value = value + sums[:, :DH]
+                wrong = jnp.where((total >= LEAST) & (total <= MOST), 0.0, 1.0)
+                flags[i] = jnp.maximum(flags[i], jnp.where(row < n_live, wrong, 0.0))
+                value = jnp.where(row < n_live, value / total, 0.0)
+                out[i, :, h * DH : (h + 1) * DH] = value.astype(jnp.bfloat16)
+
+            if n_keys == 0:
+                for h in range(GROUP):
+                    finish(h, None)
+            else:
+                sweep(q_ref, head, k_pre, v_pre, n_keys, False, finish)
+            store(i).start()
+
+    @pl.when(n_live > 0)
     def _():
         live = lax.broadcasted_iota(jnp.int32, (8 * ROWS, DH), 0) < pre_len
         v_pre[:, DH:] = jnp.where(live, 1.0, 0.0).astype(jnp.bfloat16)
+        for n in (0, 2, 3, 4):
+
+            @pl.when((chunks == n) | ((n == 2) & (chunks == 1)))
+            def _(n=n):
+                attend(256 * n)
+
+    @pl.when(n_live <= 0)
+    def _():
+        out[...] = jnp.zeros_like(out)
+        for i in range(count):
+            store(i).start()
+
+    for i in range(count):
+        store(i).wait()
 
     @pl.when(n_live > 0)
     def _():
-        for n, buffer in enumerate(prompt):
-
-            @pl.when(step == n)
-            def _(buffer=buffer):
-                k_pre[...] = buffer[:, :DH]
-                v_pre[:, :DH] = buffer[:, DH:]
-
-        flag[...] = jnp.zeros_like(flag)
-
-        def finish(h, sums):
-            totals = tot_in[:, pl.ds(pl.multiple_of(head * DH, DH), DH)]
-            total = totals[:, h : h + 1]
-            out = acc_in[:, lane_of(head, h)]
-            if sums is None:
-                total = jnp.broadcast_to(total, (ROWS, DH))
-            else:
-                total = total + sums[:, DH:]
-                out = out + sums[:, :DH]
-            wrong = jnp.where((total >= LEAST) & (total <= MOST), 0.0, 1.0)
-            flag[...] = jnp.maximum(flag[...], jnp.where(row < n_live, wrong, 0.0))
-            out = jnp.where(row < n_live, out / total, 0.0)
-            o_ref[:, h * DH : (h + 1) * DH] = out.astype(jnp.bfloat16)
-
-        @pl.when(chunks == 0)
+        @pl.when(jnp.max(flags[...]) > 0.5)
         def _():
-            for h in range(GROUP):
-                finish(h, None)
-
-        for n in range(1, 5):
-
-            @pl.when(chunks == n)
-            def _(n=n):
-                sweep(q_ref, head, k_pre, v_pre, 256 * n, False, finish)
-
-        @pl.when(jnp.max(flag[...]) > 0.5)
-        def _():
-            with_largest(info, head, q_ref, k_pre, v_pre, stored, o_ref, *rest[4:])
-
-    @pl.when(n_live <= 0)
-    def _():
-        o_ref[...] = jnp.zeros_like(o_ref)
+            @pl.loop(0, count)
+            def _(i):
+                @pl.when(jnp.max(flags[i]) > 0.5)
+                def _():
+                    take(i)
+                    with_largest(
+                        info, info[first + i], q_ref, k_pre, v_pre, stored, out.at[i], *rest[6:]
+                    )
+                    store(i).start()
+                    store(i).wait()
 
 
 def with_largest(info, head, q_ref, k_pre, v_pre, stored, o_ref, k_aug, v_aug, land, sem):
@@ -252,17 +286,22 @@
     )(info, query, *own)
 
 
-def attend_prompt(info, query, state, prompt, own):
+def attend_prompt(info, query, state, prompt, own, first, before):
+    last = () if before is None else (before,)
+    operands = (info, query, *state, *prompt, *own, *last)
+    count = len(prompt)
     return pl.pallas_call(
-        prompt_kernel,
+        functools.partial(prompt_kernel, first, count, len(last)),
         grid_spec=pltpu.PrefetchScalarGridSpec(
             num_scalar_prefetch=1,
-            grid=(KVH,),
-            in_specs=[VMEM] * (3 + len(prompt)) + [ANY] * len(own),
-            out_specs=pl.BlockSpec((ROWS, GROUP * DH), lambda i, info: (0, info[i])),
+            grid=(1,),
+            in_specs=[VMEM] * (3 + count) + [ANY] * (len(own) + len(last)),
+            out_specs=ANY,
             scratch_shapes=scratch()
             + [
-                pltpu.VMEM((ROWS, DH), jnp.float32),
+                pltpu.VMEM((count, ROWS, GROUP * DH), jnp.bfloat16),
+                pltpu.VMEM((count, ROWS, DH), jnp.float32),
+                pltpu.SemaphoreType.DMA((count,)),
                 pltpu.VMEM((16 * ROWS, PAIR), jnp.bfloat16),
                 pltpu.VMEM((16 * ROWS, PAIR), jnp.bfloat16),
                 pltpu.VMEM((ROWS, PAIR), jnp.bfloat16),
@@ -270,10 +309,11 @@
             ],
         ),
         out_shape=jax.ShapeDtypeStruct(query.shape, jnp.bfloat16),
+        input_output_aliases={} if before is None else {len(operands) - 1: 0},
         compiler_params=PARAMS,
-        cost_estimate=cost(KVH, 8 * ROWS),
-        name="prompt",
-    )(info, query, *state, *prompt, *own)
+        cost_estimate=cost(count, 8 * ROWS),
+        name=f"prompt{first}",
+    )(*operands)
 
 
 def pair_kernel(k_ref, v_ref, o_ref, top_ref):
@@ -322,7 +362,7 @@
     tie = lax.optimization_barrier
 
     steps = (0, 1, 3, 2)
-    heads = [4 * c + (y - d) % 4 for d in steps for c in (core, 1 - core)]
+    heads = [4 * c + (y - d) % 4 for c in (core, 1 - core) for d in steps]
     pre_len = jnp.where(grp == 0, 0, lengths[0])
     n_live = lengths[grp] - hd * ROWS
     info = jnp.stack([jnp.int32(v) for v in heads + [x_hi, z, pre_len, n_live]])
@@ -352,12 +392,13 @@
     lane = lax.broadcasted_iota(jnp.int32, mine.shape, 1)
     mine = jnp.where((lane < DH) | (position < lengths[0]), mine, 0)
 
-    m, e1, e3, e2 = [mine] + [along_y(mine, d) for d in steps[1:]]
+    parts = [mine] + [along_y(mine, d) for d in steps[1:]]
     own = (kv, r0p, r0m, r1m, r0x, r1x, r1p, r2a, r2b)
     state = attend_own(info, query, own)
-    (m, e1, e3, e2), state = tie(((m, e1, e3, e2), state))
-    prompt = [part for value in (m, e1, e3, e2) for part in (value, swap(value))]
-    return attend_prompt(info, query, state, prompt, own)[None]
+    parts, state = tie((parts, state))
+    swapped = [swap(value) for value in parts]
+    out = attend_prompt(info, query, state, parts, own, 0, None)
+    return attend_prompt(info, query, state, swapped, own, 4, out)[None]
 
 
 def solution(mesh):

time: 416 us -> 423 us (1.017)
  Pallas kernels: 350 us -> 355 us
    pallas_call x1 -> x2, Pallas kernels: 335 us -> 345 us  [attend_prompt(): pl.pallas_call(functools.partial(prompt_kernel, first, count, len(last)),...]
    pallas_call x1, Pallas kernels: 12.5 us -> 8.21 us  [attend_own(): pl.pallas_call(own_kernel, grid_spec=pltpu.PrefetchScalarGridSpec(num_sca...]
  transfers between devices with their start and end apart: 24 -> 24, of which waited for: 14 -> 10; matrix products, arithmetic and copies ran while one was open for 1% -> 1% of each run, Pallas kernels for 3% -> 43%
where the time goes in v4:
time: 423 us
  Pallas kernels  355 us (84%)
  starting transfers between devices  37.9 us (9%)
  waiting for transfers between devices  23.2 us (5%)
    pallas_call x2, Pallas kernels, attend_prompt(): pl.pallas_call(functools.partial(prompt_kernel, first, count, len(last)),...  345 us
    ppermute x12, starting transfers between devices, on_grp(): return lax.ppermute(value, 'grp', pairs)  19 us
    ppermute x12, starting transfers between devices, on_hd(): return lax.ppermute(value, 'hd', pairs)  18.8 us
    ppermute x12, waiting for transfers between devices, on_grp(): return lax.ppermute(value, 'grp', pairs)  12.9 us
    ppermute x12, waiting for transfers between devices, on_hd(): return lax.ppermute(value, 'hd', pairs)  10.3 us
  transfers between devices with their start and end apart: 24, of which 10 were waited for; matrix products, arithmetic and copies ran while one was open for 1% of the time, Pallas kernels for 43%

profile of v4, /device:TPU:1, one launch (start us, length us, event | category | flops | bytes accessed | tf_op | source)
XLA Modules:
  0.0 422.7 jit_solution(11605963882333214106)
XLA Ops:
  0.0 2.0 shard_map.46
  2.0 1.4 collective-permute-start.3
  3.4 3.8 collective-permute-start.2
  7.3 2.7 collective-permute-start
  10.0 0.0 collective-permute-done.3
  10.0 1.0 slice_select_fusion
  11.1 1.4 collective-permute-start.6
  12.4 2.6 collective-permute-start.5
  15.0 0.8 collective-permute-done.6
  15.8 1.5 collective-permute-start.4
  17.3 0.8 collective-permute-done.5
  18.1 1.2 collective-permute-done.4
  19.2 0.0 collective-permute-done.2.rest_2_.rest_6_
  19.3 2.7 collective-permute-done.1.rest_1_.rest_5_
  21.9 0.3 collective-permute-done.rest_4_.rest_8_
  22.2 1.2 collective-permute-start.7
  23.4 1.9 collective-permute-done.7
  25.4 2.8 collective-permute-start.8
  28.2 1.9 collective-permute-done.8
  30.1 0.0 collective-permute-start.17
  30.1 0.6 fusion.5
  30.7 2.7 collective-permute-start.15
  33.4 1.0 collective-permute-start.10
  34.4 0.4 collective-permute-start.9
  34.8 1.1 collective-permute-start.11
  35.9 0.7 iota_compare_fusion
  36.6 4.7 %collective-permute-done.17.rest_6_.rest_10_ = bf16[128,2048]{1,0:T(8,128)(2,1)S(1)} collective-permute-done((bf16[128,2048]{1,0:T(8,128)(2,1)S(1)}, bf16[128,2048]{1,0:T(8,128)(2,1)S(1)}, u32[]{:S(2)}, u32[]{:S(2)}) %collective-permute-start.17) | collective-permute-done | bytes 524320 | tf_op jit(solution)/shard_map/ppermute | solution.py:345
  41.3 2.7 collective-permute-start.16
  45.4 0.1 stack.96.info
  45.4 0.0 copy-start
  45.5 0.0 copy-start.1
  45.5 0.0 collective-permute-done.15.rest_3_.rest_7_
  45.5 0.1 collective-permute-start.19
  45.6 1.5 collective-permute-start.18
  47.1 1.6 fusion
  48.8 0.3 or_select_fusion.rest_0_
  49.0 3.0 collective-permute-start.14
  52.0 0.8 collective-permute-start.13
  52.8 0.7 collective-permute-start.12
  53.5 0.7 collective-permute-done.18.rest_7_.rest_11_
  54.2 8.2 %own.1 = (f32[128,1024]{1,0:T(8,128)S(1)}, f32[128,8192]{1,0:T(8,128)S(1)}) custom-call(s32[12]{0:T(128)S(1)} %stack.96.info, bf16[128,8192]{1,0:T(8,128)(2,1)S(1)} %bitcast.29, bf16[128,2048]{1,0:T(8,128)(2,1)S(1)} %copy-done.1, bf16[128,2048]{1,0:T(8,128)(2,1)S(1)} %collective-permute-done.1.rest_1_.rest_5_, ...), custom_call_target="tpu_custom_call" | custom-call | flops 8589934592 | bytes 4194304 | tf_op jit(solution)/shard_map/own/pallas_call | solution.py:270
  62.4 8.2 %collective-permute-done.13.rest_2_ = bf16[1024,256]{1,0:T(8,128)(2,1)S(1)} collective-permute-done((bf16[1024,256]{1,0:T(8,128)(2,1)S(1)}, bf16[1024,256]{1,0:T(8,128)(2,1)S(1)}, u32[]{:S(2)}, u32[]{:S(2)}) %collective-permute-start.13) | collective-permute-done | bytes 524320 | tf_op jit(solution)/shard_map/ppermute | solution.py:348
  70.7 6.0 %collective-permute-start.20 = (bf16[1024,256]{1,0:T(8,128)(2,1)S(1)}, bf16[1024,256]{1,0:T(8,128)(2,1)S(1)}, u32[]{:S(2)}, u32[]{:S(2)}) collective-permute-start(bf16[1024,256]{1,0:T(8,128)(2,1)S(1)} %or_select_fusion.rest_0_), channel_id=1, source_target_pairs={{0,8},{8,0},{16,24},{24,16},{32,40},{40,32},{48,56},{56,48},{64,72... | collective-permute-start | bytes 1572872 | tf_op jit(solution)/shard_map/ppermute | solution.py:348
  76.6 0.0 collective-permute-start.21
  76.6 0.5 collective-permute-start.22
  77.2 0.0 collective-permute-start.23
  77.2 172.7 %prompt0.1.rest_13_ = bf16[128,8192]{1,0:T(8,128)(2,1)} custom-call(s32[12]{0:T(128)S(1)} %stack.96.info, bf16[128,8192]{1,0:T(8,128)(2,1)S(1)} %bitcast.30, f32[128,1024]{1,0:T(8,128)S(1)} %get-tuple-element.33.tot_in, f32[128,8192]{1,0:T(8,128)S(1)} %get-tuple-element.34.acc_in, bf16[1024,256]{1,0:T(8,128)(2,1)S(1)} %or_select_fusion.rest_0_, ...), custom_call_target="tpu_custom_call" | custom-call | flops 4294967296 | bytes 4194304 | tf_op jit(solution)/shard_map/prompt0/pallas_call | solution.py:293
  249.9 172.5 %prompt4.1 = bf16[128,8192]{1,0:T(8,128)(2,1)} custom-call(s32[12]{0:T(128)S(1)} %stack.96.info, bf16[128,8192]{1,0:T(8,128)(2,1)S(1)} %bitcast.31, f32[128,1024]{1,0:T(8,128)S(1)} %get-tuple-element.33.tot_in, f32[128,8192]{1,0:T(8,128)S(1)} %get-tuple-element.34.acc_in, ...), custom_call_target="tpu_custom_call", output_to_operand_aliasing={{}: (17, {})} | custom-call | flops 4294967296 | bytes 4194304 | tf_op jit(solution)/shard_map/prompt4/pallas_call | solution.py:293
  (25 shorter events, 0.2 us)
Async XLA Ops:
  0.0 30.1 %copy-start.2 = (s32[16]{0:T(128)S(1)}, s32[16]{0:T(128)}, u32[]{:S(2)}) copy-start(s32[16]{0:T(128)} %param.7) | copy-start | bytes 196
  2.0 8.0 %collective-permute-start.3 = (bf16[128,1024]{1,0:T(8,128)(2,1)}, bf16[128,1024]{1,0:T(8,128)(2,1)S(1)}, u32[]{:S(2)}, u32[]{:S(2)}) collective-permute-start(bf16[128,1024]{1,0:T(8,128)(2,1)} %get-tuple-element.23), channel_id=1, source_target_pairs={{0,8},{8,0},{16,24},{24,16},{32,40},{40,32},{48,56},{56,48},{64,72... | collective-permute-start | bytes 786440 | tf_op jit(solution)/shard_map/ppermute | solution.py:348
  3.4 15.8 %collective-permute-start.2 = (bf16[128,2048]{1,0:T(8,128)(2,1)}, bf16[128,2048]{1,0:T(8,128)(2,1)S(1)}, u32[]{:S(2)}, u32[]{:S(2)}) collective-permute-start(bf16[128,2048]{1,0:T(8,128)(2,1)} %get-tuple-element.22.rest_0_.rest_4_), channel_id=1, source_target_pairs={{0,3},{1,0},{2,1},{3,2},{4,7},{5,4},{6,5},{7,6},{8,11},{9,8},{10,9... | collective-permute-start | bytes 1572872 | tf_op jit(solution)/shard_map/ppermute | solution.py:345
  7.3 14.7 %collective-permute-start.1 = (bf16[128,2048]{1,0:T(8,128)(2,1)}, bf16[128,2048]{1,0:T(8,128)(2,1)S(1)}, u32[]{:S(2)}, u32[]{:S(2)}) collective-permute-start(bf16[128,2048]{1,0:T(8,128)(2,1)} %get-tuple-element.22.rest_0_.rest_4_), channel_id=1, source_target_pairs={{0,1},{1,2},{2,3},{3,0},{4,5},{5,6},{6,7},{7,4},{8,9},{9,10},{10,1... | collective-permute-start | bytes 1572872 | tf_op jit(solution)/shard_map/ppermute | solution.py:345
  7.3 15.0 %collective-permute-start = (bf16[128,2048]{1,0:T(8,128)(2,1)}, bf16[128,2048]{1,0:T(8,128)(2,1)S(1)}, u32[]{:S(2)}, u32[]{:S(2)}) collective-permute-start(bf16[128,2048]{1,0:T(8,128)(2,1)} %get-tuple-element.22.rest_0_.rest_4_), channel_id=1, source_target_pairs={{0,4},{1,5},{2,6},{3,7},{4,0},{5,1},{6,2},{7,3},{8,12},{9,13},{10,... | collective-permute-start | bytes 1572872 | tf_op jit(solution)/shard_map/ppermute | solution.py:345
  11.1 4.8 %collective-permute-start.6 = (bf16[128,256]{1,0:T(8,128)(2,1)S(1)}, bf16[128,256]{1,0:T(8,128)(2,1)S(1)}, u32[]{:S(2)}, u32[]{:S(2)}) collective-permute-start(bf16[128,256]{1,0:T(8,128)(2,1)S(1)} %get-tuple-element.39), channel_id=1, source_target_pairs={{0,16},{8,24},{16,32},{24,40},{32,48},{40,56},{48,0},{56,8},{64,80... | collective-permute-start | bytes 196616 | tf_op jit(solution)/shard_map/ppermute | solution.py:348
  12.4 5.6 %collective-permute-start.5 = (bf16[128,256]{1,0:T(8,128)(2,1)S(1)}, bf16[128,256]{1,0:T(8,128)(2,1)S(1)}, u32[]{:S(2)}, u32[]{:S(2)}) collective-permute-start(bf16[128,256]{1,0:T(8,128)(2,1)S(1)} %get-tuple-element.40), channel_id=1, source_target_pairs={{0,32},{8,40},{16,48},{24,56},{32,0},{40,8},{48,16},{56,24},{64,96... | collective-permute-start | bytes 196616 | tf_op jit(solution)/shard_map/ppermute | solution.py:348
  15.8 3.4 collective-permute-start.4
  22.2 3.1 collective-permute-start.7
  25.4 4.7 %collective-permute-start.8 = (bf16[128,256]{1,0:T(8,128)(2,1)S(1)}, bf16[128,256]{1,0:T(8,128)(2,1)S(1)}, u32[]{:S(2)}, u32[]{:S(2)}) collective-permute-start(bf16[128,256]{1,0:T(8,128)(2,1)S(1)} %broadcast_select_fusion), channel_id=1, source_target_pairs={{0,4},{1,5},{2,6},{3,7},{4,0},{5,1},{6,2},{7,3},{8,12},{9,13},{10,... | collective-permute-start | bytes 196616 | tf_op jit(solution)/shard_map/ppermute | solution.py:345
  30.1 11.2 %collective-permute-start.17 = (bf16[128,2048]{1,0:T(8,128)(2,1)S(1)}, bf16[128,2048]{1,0:T(8,128)(2,1)S(1)}, u32[]{:S(2)}, u32[]{:S(2)}) collective-permute-start(bf16[128,2048]{1,0:T(8,128)(2,1)S(1)} %collective-permute-done.rest_4_.rest_8_), channel_id=1, source_target_pairs={{0,1},{1,2},{2,3},{3,0},{4,5},{5,6},{6,7},{7,4},{8,9},{9,10},{10,1... | collective-permute-start | bytes 1572872 | tf_op jit(solution)/shard_map/ppermute | solution.py:345
  30.7 14.8 %collective-permute-start.15 = (bf16[128,2048]{1,0:T(8,128)(2,1)S(1)}, bf16[128,2048]{1,0:T(8,128)(2,1)S(1)}, u32[]{:S(2)}, u32[]{:S(2)}) collective-permute-start(bf16[128,2048]{1,0:T(8,128)(2,1)S(1)} %collective-permute-done.2.rest_2_.rest_6_), channel_id=1, source_target_pairs={{0,3},{1,0},{2,1},{3,2},{4,7},{5,4},{6,5},{7,6},{8,11},{9,8},{10,9... | collective-permute-start | bytes 1572872 | tf_op jit(solution)/shard_map/ppermute | solution.py:345
  33.4 12.2 %collective-permute-start.10 = (bf16[2,128,256]{2,1,0:T(8,128)(2,1)S(1)}, bf16[2,128,256]{2,1,0:T(8,128)(2,1)S(1)}, u32[]{:S(2)}, u32[]{:S(2)}) collective-permute-start(bf16[2,128,256]{2,1,0:T(8,128)(2,1)S(1)} %get-tuple-element.43), channel_id=1, source_target_pairs={{0,2},{1,3},{2,0},{3,1},{4,6},{5,7},{6,4},{7,5},{8,10},{9,11},{10,... | collective-permute-start | bytes 393224 | tf_op jit(solution)/shard_map/ppermute | solution.py:345
  34.4 12.7 %collective-permute-start.9 = (bf16[2,128,256]{2,1,0:T(8,128)(2,1)S(1)}, bf16[2,128,256]{2,1,0:T(8,128)(2,1)}, u32[]{:S(2)}, u32[]{:S(2)}) collective-permute-start(bf16[2,128,256]{2,1,0:T(8,128)(2,1)S(1)} %get-tuple-element.43), channel_id=1, source_target_pairs={{0,3},{1,0},{2,1},{3,2},{4,7},{5,4},{6,5},{7,6},{8,11},{9,8},{10,9... | collective-permute-start | bytes 393224 | tf_op jit(solution)/shard_map/ppermute | solution.py:345
  34.8 12.3 %collective-permute-start.11 = (bf16[2,128,256]{2,1,0:T(8,128)(2,1)S(1)}, bf16[2,128,256]{2,1,0:T(8,128)(2,1)}, u32[]{:S(2)}, u32[]{:S(2)}) collective-permute-start(bf16[2,128,256]{2,1,0:T(8,128)(2,1)S(1)} %get-tuple-element.43), channel_id=1, source_target_pairs={{0,1},{1,2},{2,3},{3,0},{4,5},{5,6},{6,7},{7,4},{8,9},{9,10},{10,1... | collective-permute-start | bytes 393224 | tf_op jit(solution)/shard_map/ppermute | solution.py:345
  41.3 11.5 %collective-permute-start.16 = (bf16[128,2048]{1,0:T(8,128)(2,1)S(1)}, bf16[128,2048]{1,0:T(8,128)(2,1)S(1)}, u32[]{:S(2)}, u32[]{:S(2)}) collective-permute-start(bf16[128,2048]{1,0:T(8,128)(2,1)S(1)} %collective-permute-done.2.rest_2_.rest_6_), channel_id=1, source_target_pairs={{0,4},{1,5},{2,6},{3,7},{4,0},{5,1},{6,2},{7,3},{8,12},{9,13},{10,... | collective-permute-start | bytes 1572872 | tf_op jit(solution)/shard_map/ppermute | solution.py:345
  45.4 8.8 %copy-start = (bf16[1,128,8192]{2,1,0:T(8,128)(2,1)S(1)}, bf16[1,128,8192]{2,1,0:T(8,128)(2,1)}, u32[]{:S(2)}) copy-start(bf16[1,128,8192]{2,1,0:T(8,128)(2,1)} %param.4) | copy-start | bytes 6291460
  45.5 8.8 %copy-start.1 = (bf16[128,2048]{1,0:T(8,128)(2,1)S(1)}, bf16[128,2048]{1,0:T(8,128)(2,1)}, u32[]{:S(2)}) copy-start(bf16[128,2048]{1,0:T(8,128)(2,1)} %get-tuple-element.22.rest_0_.rest_4_) | copy-start | bytes 1572868
  45.5 8.0 %collective-permute-start.19 = (bf16[128,1024]{1,0:T(8,128)(2,1)S(1)}, bf16[128,1024]{1,0:T(8,128)(2,1)S(1)}, u32[]{:S(2)}, u32[]{:S(2)}) collective-permute-start(bf16[128,1024]{1,0:T(8,128)(2,1)S(1)} %slice.38), channel_id=1, source_target_pairs={{0,1},{1,2},{2,3},{3,0},{4,5},{5,6},{6,7},{7,4},{8,9},{9,10},{10,1... | collective-permute-start | bytes 786440 | tf_op jit(solution)/shard_map/ppermute | solution.py:345
  45.6 8.6 %collective-permute-start.18 = (bf16[128,1024]{1,0:T(8,128)(2,1)S(1)}, bf16[128,1024]{1,0:T(8,128)(2,1)S(1)}, u32[]{:S(2)}, u32[]{:S(2)}) collective-permute-start(bf16[128,1024]{1,0:T(8,128)(2,1)S(1)} %slice.37), channel_id=1, source_target_pairs={{0,4},{1,5},{2,6},{3,7},{4,0},{5,1},{6,2},{7,3},{8,12},{9,13},{10,... | collective-permute-start | bytes 786440 | tf_op jit(solution)/shard_map/ppermute | solution.py:345
  49.0 13.4 %collective-permute-start.14 = (bf16[1024,256]{1,0:T(8,128)(2,1)S(1)}, bf16[1024,256]{1,0:T(8,128)(2,1)S(1)}, u32[]{:S(2)}, u32[]{:S(2)}) collective-permute-start(bf16[1024,256]{1,0:T(8,128)(2,1)S(1)} %or_select_fusion.rest_0_), channel_id=1, source_target_pairs={{0,32},{8,40},{16,48},{24,56},{32,0},{40,8},{48,16},{56,24},{64,96... | collective-permute-start | bytes 1572872 | tf_op jit(solution)/shard_map/ppermute | solution.py:348
  52.0 18.6 %collective-permute-start.13 = (bf16[1024,256]{1,0:T(8,128)(2,1)S(1)}, bf16[1024,256]{1,0:T(8,128)(2,1)S(1)}, u32[]{:S(2)}, u32[]{:S(2)}) collective-permute-start(bf16[1024,256]{1,0:T(8,128)(2,1)S(1)} %or_select_fusion.rest_0_), channel_id=1, source_target_pairs={{0,48},{8,56},{16,0},{24,8},{32,16},{40,24},{48,32},{56,40},{64,11... | collective-permute-start | bytes 1572872 | tf_op jit(solution)/shard_map/ppermute | solution.py:348
  52.8 17.8 %collective-permute-start.12 = (bf16[1024,256]{1,0:T(8,128)(2,1)S(1)}, bf16[1024,256]{1,0:T(8,128)(2,1)S(1)}, u32[]{:S(2)}, u32[]{:S(2)}) collective-permute-start(bf16[1024,256]{1,0:T(8,128)(2,1)S(1)} %or_select_fusion.rest_0_), channel_id=1, source_target_pairs={{0,16},{8,24},{16,32},{24,40},{32,48},{40,56},{48,0},{56,8},{64,80... | collective-permute-start | bytes 1572872 | tf_op jit(solution)/shard_map/ppermute | solution.py:348
  70.7 179.2 %collective-permute-start.20 = (bf16[1024,256]{1,0:T(8,128)(2,1)S(1)}, bf16[1024,256]{1,0:T(8,128)(2,1)S(1)}, u32[]{:S(2)}, u32[]{:S(2)}) collective-permute-start(bf16[1024,256]{1,0:T(8,128)(2,1)S(1)} %or_select_fusion.rest_0_), channel_id=1, source_target_pairs={{0,8},{8,0},{16,24},{24,16},{32,40},{40,32},{48,56},{56,48},{64,72... | collective-permute-start | bytes 1572872 | tf_op jit(solution)/shard_map/ppermute | solution.py:348
  76.6 173.3 %collective-permute-start.21 = (bf16[1024,256]{1,0:T(8,128)(2,1)S(1)}, bf16[1024,256]{1,0:T(8,128)(2,1)S(1)}, u32[]{:S(2)}, u32[]{:S(2)}) collective-permute-start(bf16[1024,256]{1,0:T(8,128)(2,1)S(1)} %collective-permute-done.12.rest_1_), channel_id=1, source_target_pairs={{0,8},{8,0},{16,24},{24,16},{32,40},{40,32},{48,56},{56,48},{64,72... | collective-permute-start | bytes 1572872 | tf_op jit(solution)/shard_map/ppermute | solution.py:348
  76.6 173.3 %collective-permute-start.22 = (bf16[1024,256]{1,0:T(8,128)(2,1)S(1)}, bf16[1024,256]{1,0:T(8,128)(2,1)S(1)}, u32[]{:S(2)}, u32[]{:S(2)}) collective-permute-start(bf16[1024,256]{1,0:T(8,128)(2,1)S(1)} %collective-permute-done.13.rest_2_), channel_id=1, source_target_pairs={{0,8},{8,0},{16,24},{24,16},{32,40},{40,32},{48,56},{56,48},{64,72... | collective-permute-start | bytes 1572872 | tf_op jit(solution)/shard_map/ppermute | solution.py:348
  77.2 172.8 %collective-permute-start.23 = (bf16[1024,256]{1,0:T(8,128)(2,1)S(1)}, bf16[1024,256]{1,0:T(8,128)(2,1)S(1)}, u32[]{:S(2)}, u32[]{:S(2)}) collective-permute-start(bf16[1024,256]{1,0:T(8,128)(2,1)S(1)} %collective-permute-done.14.rest_3_), channel_id=1, source_target_pairs={{0,8},{8,0},{16,24},{24,16},{32,40},{40,32},{48,56},{56,48},{64,72... | collective-permute-start | bytes 1572872 | tf_op jit(solution)/shard_map/ppermute | solution.py:348

commit v5 on v4

--- a/solution.py
+++ b/solution.py
@@ -71,24 +71,13 @@
     head = pl.program_id(0)
     allowed = own_blocks(info)
     columns = pl.ds(pl.multiple_of(head * PAIR, PAIR), PAIR)
-    half = pl.ds(pl.multiple_of(lax.rem(head, 4) * PAIR, PAIR), PAIR)
 
     @pl.when(info[11] > 0)
     def _():
-        for slot in range(4):
+        for slot in range(7):
             place(k_own, v_own, slot, blocks[slot][:, columns], allowed[slot])
-
-        for slot in range(4, 7):
-            place(k_own, v_own, slot, blocks[slot][:, columns], allowed[slot])
-
-        @pl.when(head < 4)
-        def _():
-            place(k_own, v_own, 7, blocks[7][:, half], allowed[7])
-
-        @pl.when(head >= 4)
-        def _():
-            place(k_own, v_own, 7, blocks[8][:, half], allowed[7])
-
+        last = jnp.concatenate([blocks[7][:, columns], blocks[8][:, columns]], 0)
+        place(k_own, v_own, 7, last, allowed[7])
         lane = lax.broadcasted_iota(jnp.int32, (ROWS, DH), 1)
 
         def run(n_keys):
@@ -134,20 +123,22 @@
         def _(i):
             head = info[first + i]
             take(i)
-            flags[i] = jnp.zeros((ROWS, DH), jnp.float32)
+            lane = lax.broadcasted_iota(jnp.int32, (ROWS, DH), 1)
+            own_totals = tot_in[:, pl.ds(pl.multiple_of(head * DH, DH), DH)]
+            totals = [jnp.ones((ROWS, DH), jnp.float32)]
 
             def finish(h, sums):
-                totals = tot_in[:, pl.ds(pl.multiple_of(head * DH, DH), DH)]
-                total = totals[:, h : h + 1]
+                total = own_totals[:, h : h + 1]
                 value = acc_in[:, lane_of(head, h)]
                 if sums is None:
                     total = jnp.broadcast_to(total, (ROWS, DH))
                 else:
                     total = total + sums[:, DH:]
                     value = value + sums[:, :DH]
-                wrong = jnp.where((total >= LEAST) & (total <= MOST), 0.0, 1.0)
-                flags[i] = jnp.maximum(flags[i], jnp.where(row < n_live, wrong, 0.0))
-                value = jnp.where(row < n_live, value / total, 0.0)
+                totals.append(jnp.where(lane == h, total, totals[-1]))
+                scale = pl.reciprocal(total, approx=True)
+                scale = scale * (2.0 - total * scale)
+                value = jnp.where(row < n_live, value * scale, 0.0)
                 out[i, :, h * DH : (h + 1) * DH] = value.astype(jnp.bfloat16)
 
             if n_keys == 0:
@@ -156,6 +147,8 @@
             else:
                 sweep(q_ref, head, k_pre, v_pre, n_keys, False, finish)
             store(i).start()
+            fine = (totals[-1] >= LEAST) & (totals[-1] <= MOST)
+            flags[i] = jnp.where(fine | (row >= n_live), 0.0, 1.0)
 
     @pl.when(n_live > 0)
     def _():
@@ -203,23 +196,18 @@
         v_aug[rows, :DH] = value
         v_aug[rows, DH:] = jnp.ones((count, DH), jnp.bfloat16)
 
-    def fetch(source, columns):
-        copy = pltpu.make_async_copy(source.at[:, columns], land, sem)
+    def fetch(source, target):
+        columns = pl.ds(pl.multiple_of(head * PAIR, PAIR), PAIR)
+        copy = pltpu.make_async_copy(source.at[:, columns], target, sem)
         copy.start()
         copy.wait()
 
-    columns = pl.ds(pl.multiple_of(head * PAIR, PAIR), PAIR)
-    half = pl.ds(pl.multiple_of(lax.rem(head, 4) * PAIR, PAIR), PAIR)
     for slot in range(8):
         if slot < 7:
-            fetch(stored[slot], columns)
+            fetch(stored[slot], land)
         else:
-            for low, source in ((True, stored[7]), (False, stored[8])):
-
-                @pl.when((head < 4) == low)
-                def _(source=source):
-                    fetch(source, half)
-
+            fetch(stored[7], land.at[: ROWS // 2, :])
+            fetch(stored[8], land.at[ROWS // 2 :, :])
         rows = slice(slot * ROWS, (slot + 1) * ROWS)
         put(rows, ROWS, land[:, :DH], land[:, DH:], allowed[slot])
     position = lax.broadcasted_iota(jnp.int32, (8 * ROWS, DH), 0)
@@ -381,7 +369,7 @@
     )
 
     r1x, r1p, r1m = along_x_hi(r0m_t), along_z(r0x_t, 1), along_z(r0m_t, 3)
-    r2a, r2b = along_x_hi(r1m[:, : 4 * PAIR]), along_z(r1p[:, 4 * PAIR :], 1)
+    r2a, r2b = along_x_hi(r1m[: ROWS // 2]), along_z(r1p[ROWS // 2 :], 1)
     behind = [both] + [along_z(both, d) for d in range(1, 4)]
     orders = [
         jnp.stack([behind[(at - i) % 4] for i in range(4)], 1).reshape(8 * ROWS, PAIR)

time: 423 us -> 424 us (level)
  no operation moved by 1% of the time
where the time goes in v5:
time: 424 us; the launch traced here: 423 us
  Pallas kernels  355 us (84%)
  starting transfers between devices  37.9 us (9%)
  waiting for transfers between devices  23.3 us (5%)
    pallas_call x2, Pallas kernels, attend_prompt(): pl.pallas_call(functools.partial(prompt_kernel, first, count, len(last)),...  345 us
    ppermute x12, starting transfers between devices, on_grp(): return lax.ppermute(value, 'grp', pairs)  19 us
    ppermute x12, starting transfers between devices, on_hd(): return lax.ppermute(value, 'hd', pairs)  18.8 us
    ppermute x12, waiting for transfers between devices, on_grp(): return lax.ppermute(value, 'grp', pairs)  13 us
    ppermute x12, waiting for transfers between devices, on_hd(): return lax.ppermute(value, 'hd', pairs)  10.3 us
  transfers between devices with their start and end apart: 24, of which 10 were waited for; matrix products, arithmetic and copies ran while one was open for 1% of the time, Pallas kernels for 43%

profile of v5, /device:TPU:1, one launch (start us, length us, event | category | flops | bytes accessed | tf_op | source)
XLA Modules:
  0.0 422.5 jit_solution(18127479751218703819)
XLA Ops:
  0.0 2.0 shard_map.46
  2.0 1.4 collective-permute-start.3
  3.4 3.8 collective-permute-start.2
  7.3 2.7 collective-permute-start
  10.0 0.0 collective-permute-done.3
  10.0 1.0 slice_select_fusion
  11.1 1.4 collective-permute-start.6
  12.4 2.6 collective-permute-start.5
  15.0 0.8 collective-permute-done.6
  15.8 1.5 collective-permute-start.4
  17.3 0.8 collective-permute-done.5
  18.1 1.2 collective-permute-done.4
  19.2 0.0 collective-permute-done.2.rest_2_.rest_6_
  19.3 2.7 collective-permute-done.1.rest_1_.rest_5_
  21.9 0.3 collective-permute-done.rest_4_.rest_8_
  22.2 1.2 collective-permute-start.7
  23.4 1.9 collective-permute-done.7
  25.4 2.8 collective-permute-start.8
  28.2 1.9 collective-permute-done.8
  30.1 0.0 collective-permute-start.17
  30.1 0.6 fusion.5
  30.7 2.7 collective-permute-start.15
  33.4 1.0 collective-permute-start.10
  34.4 0.4 collective-permute-start.9
  34.8 1.1 collective-permute-start.11
  35.9 0.7 iota_compare_fusion
  36.6 4.7 %collective-permute-done.17.rest_6_.rest_10_ = bf16[128,2048]{1,0:T(8,128)(2,1)S(1)} collective-permute-done((bf16[128,2048]{1,0:T(8,128)(2,1)S(1)}, bf16[128,2048]{1,0:T(8,128)(2,1)S(1)}, u32[]{:S(2)}, u32[]{:S(2)}) %collective-permute-start.17) | collective-permute-done | bytes 524320 | tf_op jit(solution)/shard_map/ppermute | solution.py:333
  41.3 2.7 collective-permute-start.16
  45.4 0.1 stack.96.info
  45.4 0.0 copy-start
  45.5 0.0 copy-start.1
  45.5 0.0 collective-permute-done.15.rest_3_.rest_7_
  45.5 0.1 collective-permute-start.19
  45.6 1.5 collective-permute-start.18
  47.1 1.6 fusion
  48.8 0.3 or_select_fusion.rest_0_
  49.0 3.0 collective-permute-start.14
  52.0 0.8 collective-permute-start.13
  52.8 0.7 collective-permute-start.12
  53.5 0.7 collective-permute-done.18.rest_7_.rest_11_
  54.2 8.1 %own.1 = (f32[128,1024]{1,0:T(8,128)S(1)}, f32[128,8192]{1,0:T(8,128)S(1)}) custom-call(s32[12]{0:T(128)S(1)} %stack.96.info, bf16[128,8192]{1,0:T(8,128)(2,1)S(1)} %bitcast.29, bf16[128,2048]{1,0:T(8,128)(2,1)S(1)} %copy-done.1, bf16[128,2048]{1,0:T(8,128)(2,1)S(1)} %collective-permute-done.1.rest_1_.rest_5_, ...), custom_call_target="tpu_custom_call" | custom-call | flops 8589934592 | bytes 4194304 | tf_op jit(solution)/shard_map/own/pallas_call | solution.py:258
  62.3 8.3 %collective-permute-done.13.rest_2_ = bf16[1024,256]{1,0:T(8,128)(2,1)S(1)} collective-permute-done((bf16[1024,256]{1,0:T(8,128)(2,1)S(1)}, bf16[1024,256]{1,0:T(8,128)(2,1)S(1)}, u32[]{:S(2)}, u32[]{:S(2)}) %collective-permute-start.13) | collective-permute-done | bytes 524320 | tf_op jit(solution)/shard_map/ppermute | solution.py:336
  70.7 6.0 %collective-permute-start.20 = (bf16[1024,256]{1,0:T(8,128)(2,1)S(1)}, bf16[1024,256]{1,0:T(8,128)(2,1)S(1)}, u32[]{:S(2)}, u32[]{:S(2)}) collective-permute-start(bf16[1024,256]{1,0:T(8,128)(2,1)S(1)} %or_select_fusion.rest_0_), channel_id=1, source_target_pairs={{0,8},{8,0},{16,24},{24,16},{32,40},{40,32},{48,56},{56,48},{64,72... | collective-permute-start | bytes 1572872 | tf_op jit(solution)/shard_map/ppermute | solution.py:336
  76.6 0.0 collective-permute-start.21
  76.6 0.5 collective-permute-start.22
  77.2 0.0 collective-permute-start.23
  77.2 172.7 %prompt0.1.rest_13_ = bf16[128,8192]{1,0:T(8,128)(2,1)} custom-call(s32[12]{0:T(128)S(1)} %stack.96.info, bf16[128,8192]{1,0:T(8,128)(2,1)S(1)} %bitcast.30, f32[128,1024]{1,0:T(8,128)S(1)} %get-tuple-element.33.tot_in, f32[128,8192]{1,0:T(8,128)S(1)} %get-tuple-element.34.acc_in, bf16[1024,256]{1,0:T(8,128)(2,1)S(1)} %or_select_fusion.rest_0_, ...), custom_call_target="tpu_custom_call" | custom-call | flops 4294967296 | bytes 4194304 | tf_op jit(solution)/shard_map/prompt0/pallas_call | solution.py:281
  249.9 172.5 %prompt4.1 = bf16[128,8192]{1,0:T(8,128)(2,1)} custom-call(s32[12]{0:T(128)S(1)} %stack.96.info, bf16[128,8192]{1,0:T(8,128)(2,1)S(1)} %bitcast.31, f32[128,1024]{1,0:T(8,128)S(1)} %get-tuple-element.33.tot_in, f32[128,8192]{1,0:T(8,128)S(1)} %get-tuple-element.34.acc_in, ...), custom_call_target="tpu_custom_call", output_to_operand_aliasing={{}: (17, {})} | custom-call | flops 4294967296 | bytes 4194304 | tf_op jit(solution)/shard_map/prompt4/pallas_call | solution.py:281
  (25 shorter events, 0.2 us)
Async XLA Ops:
  0.0 30.1 %copy-start.2 = (s32[16]{0:T(128)S(1)}, s32[16]{0:T(128)}, u32[]{:S(2)}) copy-start(s32[16]{0:T(128)} %param.7) | copy-start | bytes 196
  2.0 8.0 %collective-permute-start.3 = (bf16[128,1024]{1,0:T(8,128)(2,1)}, bf16[128,1024]{1,0:T(8,128)(2,1)S(1)}, u32[]{:S(2)}, u32[]{:S(2)}) collective-permute-start(bf16[128,1024]{1,0:T(8,128)(2,1)} %get-tuple-element.23), channel_id=1, source_target_pairs={{0,8},{8,0},{16,24},{24,16},{32,40},{40,32},{48,56},{56,48},{64,72... | collective-permute-start | bytes 786440 | tf_op jit(solution)/shard_map/ppermute | solution.py:336
  3.4 15.8 %collective-permute-start.2 = (bf16[128,2048]{1,0:T(8,128)(2,1)}, bf16[128,2048]{1,0:T(8,128)(2,1)S(1)}, u32[]{:S(2)}, u32[]{:S(2)}) collective-permute-start(bf16[128,2048]{1,0:T(8,128)(2,1)} %get-tuple-element.22.rest_0_.rest_4_), channel_id=1, source_target_pairs={{0,3},{1,0},{2,1},{3,2},{4,7},{5,4},{6,5},{7,6},{8,11},{9,8},{10,9... | collective-permute-start | bytes 1572872 | tf_op jit(solution)/shard_map/ppermute | solution.py:333
  7.3 14.7 %collective-permute-start.1 = (bf16[128,2048]{1,0:T(8,128)(2,1)}, bf16[128,2048]{1,0:T(8,128)(2,1)S(1)}, u32[]{:S(2)}, u32[]{:S(2)}) collective-permute-start(bf16[128,2048]{1,0:T(8,128)(2,1)} %get-tuple-element.22.rest_0_.rest_4_), channel_id=1, source_target_pairs={{0,1},{1,2},{2,3},{3,0},{4,5},{5,6},{6,7},{7,4},{8,9},{9,10},{10,1... | collective-permute-start | bytes 1572872 | tf_op jit(solution)/shard_map/ppermute | solution.py:333
  7.3 15.0 %collective-permute-start = (bf16[128,2048]{1,0:T(8,128)(2,1)}, bf16[128,2048]{1,0:T(8,128)(2,1)S(1)}, u32[]{:S(2)}, u32[]{:S(2)}) collective-permute-start(bf16[128,2048]{1,0:T(8,128)(2,1)} %get-tuple-element.22.rest_0_.rest_4_), channel_id=1, source_target_pairs={{0,4},{1,5},{2,6},{3,7},{4,0},{5,1},{6,2},{7,3},{8,12},{9,13},{10,... | collective-permute-start | bytes 1572872 | tf_op jit(solution)/shard_map/ppermute | solution.py:333
  11.1 4.8 %collective-permute-start.6 = (bf16[128,256]{1,0:T(8,128)(2,1)S(1)}, bf16[128,256]{1,0:T(8,128)(2,1)S(1)}, u32[]{:S(2)}, u32[]{:S(2)}) collective-permute-start(bf16[128,256]{1,0:T(8,128)(2,1)S(1)} %get-tuple-element.39), channel_id=1, source_target_pairs={{0,16},{8,24},{16,32},{24,40},{32,48},{40,56},{48,0},{56,8},{64,80... | collective-permute-start | bytes 196616 | tf_op jit(solution)/shard_map/ppermute | solution.py:336
  12.4 5.6 %collective-permute-start.5 = (bf16[128,256]{1,0:T(8,128)(2,1)S(1)}, bf16[128,256]{1,0:T(8,128)(2,1)S(1)}, u32[]{:S(2)}, u32[]{:S(2)}) collective-permute-start(bf16[128,256]{1,0:T(8,128)(2,1)S(1)} %get-tuple-element.40), channel_id=1, source_target_pairs={{0,32},{8,40},{16,48},{24,56},{32,0},{40,8},{48,16},{56,24},{64,96... | collective-permute-start | bytes 196616 | tf_op jit(solution)/shard_map/ppermute | solution.py:336
  15.8 3.4 collective-permute-start.4
  22.2 3.1 collective-permute-start.7
  25.4 4.7 %collective-permute-start.8 = (bf16[128,256]{1,0:T(8,128)(2,1)S(1)}, bf16[128,256]{1,0:T(8,128)(2,1)S(1)}, u32[]{:S(2)}, u32[]{:S(2)}) collective-permute-start(bf16[128,256]{1,0:T(8,128)(2,1)S(1)} %broadcast_select_fusion), channel_id=1, source_target_pairs={{0,4},{1,5},{2,6},{3,7},{4,0},{5,1},{6,2},{7,3},{8,12},{9,13},{10,... | collective-permute-start | bytes 196616 | tf_op jit(solution)/shard_map/ppermute | solution.py:333
  30.1 11.2 %collective-permute-start.17 = (bf16[128,2048]{1,0:T(8,128)(2,1)S(1)}, bf16[128,2048]{1,0:T(8,128)(2,1)S(1)}, u32[]{:S(2)}, u32[]{:S(2)}) collective-permute-start(bf16[128,2048]{1,0:T(8,128)(2,1)S(1)} %collective-permute-done.rest_4_.rest_8_), channel_id=1, source_target_pairs={{0,1},{1,2},{2,3},{3,0},{4,5},{5,6},{6,7},{7,4},{8,9},{9,10},{10,1... | collective-permute-start | bytes 1572872 | tf_op jit(solution)/shard_map/ppermute | solution.py:333
  30.7 14.8 %collective-permute-start.15 = (bf16[128,2048]{1,0:T(8,128)(2,1)S(1)}, bf16[128,2048]{1,0:T(8,128)(2,1)S(1)}, u32[]{:S(2)}, u32[]{:S(2)}) collective-permute-start(bf16[128,2048]{1,0:T(8,128)(2,1)S(1)} %collective-permute-done.2.rest_2_.rest_6_), channel_id=1, source_target_pairs={{0,3},{1,0},{2,1},{3,2},{4,7},{5,4},{6,5},{7,6},{8,11},{9,8},{10,9... | collective-permute-start | bytes 1572872 | tf_op jit(solution)/shard_map/ppermute | solution.py:333
  33.4 12.2 %collective-permute-start.10 = (bf16[2,128,256]{2,1,0:T(8,128)(2,1)S(1)}, bf16[2,128,256]{2,1,0:T(8,128)(2,1)S(1)}, u32[]{:S(2)}, u32[]{:S(2)}) collective-permute-start(bf16[2,128,256]{2,1,0:T(8,128)(2,1)S(1)} %get-tuple-element.43), channel_id=1, source_target_pairs={{0,2},{1,3},{2,0},{3,1},{4,6},{5,7},{6,4},{7,5},{8,10},{9,11},{10,... | collective-permute-start | bytes 393224 | tf_op jit(solution)/shard_map/ppermute | solution.py:333
  34.4 12.7 %collective-permute-start.9 = (bf16[2,128,256]{2,1,0:T(8,128)(2,1)S(1)}, bf16[2,128,256]{2,1,0:T(8,128)(2,1)}, u32[]{:S(2)}, u32[]{:S(2)}) collective-permute-start(bf16[2,128,256]{2,1,0:T(8,128)(2,1)S(1)} %get-tuple-element.43), channel_id=1, source_target_pairs={{0,3},{1,0},{2,1},{3,2},{4,7},{5,4},{6,5},{7,6},{8,11},{9,8},{10,9... | collective-permute-start | bytes 393224 | tf_op jit(solution)/shard_map/ppermute | solution.py:333
  34.8 12.3 %collective-permute-start.11 = (bf16[2,128,256]{2,1,0:T(8,128)(2,1)S(1)}, bf16[2,128,256]{2,1,0:T(8,128)(2,1)}, u32[]{:S(2)}, u32[]{:S(2)}) collective-permute-start(bf16[2,128,256]{2,1,0:T(8,128)(2,1)S(1)} %get-tuple-element.43), channel_id=1, source_target_pairs={{0,1},{1,2},{2,3},{3,0},{4,5},{5,6},{6,7},{7,4},{8,9},{9,10},{10,1... | collective-permute-start | bytes 393224 | tf_op jit(solution)/shard_map/ppermute | solution.py:333
  41.3 11.5 %collective-permute-start.16 = (bf16[128,2048]{1,0:T(8,128)(2,1)S(1)}, bf16[128,2048]{1,0:T(8,128)(2,1)S(1)}, u32[]{:S(2)}, u32[]{:S(2)}) collective-permute-start(bf16[128,2048]{1,0:T(8,128)(2,1)S(1)} %collective-permute-done.2.rest_2_.rest_6_), channel_id=1, source_target_pairs={{0,4},{1,5},{2,6},{3,7},{4,0},{5,1},{6,2},{7,3},{8,12},{9,13},{10,... | collective-permute-start | bytes 1572872 | tf_op jit(solution)/shard_map/ppermute | solution.py:333
  45.4 8.8 %copy-start = (bf16[1,128,8192]{2,1,0:T(8,128)(2,1)S(1)}, bf16[1,128,8192]{2,1,0:T(8,128)(2,1)}, u32[]{:S(2)}) copy-start(bf16[1,128,8192]{2,1,0:T(8,128)(2,1)} %param.4) | copy-start | bytes 6291460
  45.5 8.8 %copy-start.1 = (bf16[128,2048]{1,0:T(8,128)(2,1)S(1)}, bf16[128,2048]{1,0:T(8,128)(2,1)}, u32[]{:S(2)}) copy-start(bf16[128,2048]{1,0:T(8,128)(2,1)} %get-tuple-element.22.rest_0_.rest_4_) | copy-start | bytes 1572868
  45.5 8.0 %collective-permute-start.19 = (bf16[64,2048]{1,0:T(8,128)(2,1)S(1)}, bf16[64,2048]{1,0:T(8,128)(2,1)S(1)}, u32[]{:S(2)}, u32[]{:S(2)}) collective-permute-start(bf16[64,2048]{1,0:T(8,128)(2,1)S(1)} %slice.38), channel_id=1, source_target_pairs={{0,1},{1,2},{2,3},{3,0},{4,5},{5,6},{6,7},{7,4},{8,9},{9,10},{10,1... | collective-permute-start | bytes 786440 | tf_op jit(solution)/shard_map/ppermute | solution.py:333
  45.6 8.6 %collective-permute-start.18 = (bf16[64,2048]{1,0:T(8,128)(2,1)S(1)}, bf16[64,2048]{1,0:T(8,128)(2,1)S(1)}, u32[]{:S(2)}, u32[]{:S(2)}) collective-permute-start(bf16[64,2048]{1,0:T(8,128)(2,1)S(1)} %slice.37), channel_id=1, source_target_pairs={{0,4},{1,5},{2,6},{3,7},{4,0},{5,1},{6,2},{7,3},{8,12},{9,13},{10,... | collective-permute-start | bytes 786440 | tf_op jit(solution)/shard_map/ppermute | solution.py:333
  49.0 13.3 %collective-permute-start.14 = (bf16[1024,256]{1,0:T(8,128)(2,1)S(1)}, bf16[1024,256]{1,0:T(8,128)(2,1)S(1)}, u32[]{:S(2)}, u32[]{:S(2)}) collective-permute-start(bf16[1024,256]{1,0:T(8,128)(2,1)S(1)} %or_select_fusion.rest_0_), channel_id=1, source_target_pairs={{0,32},{8,40},{16,48},{24,56},{32,0},{40,8},{48,16},{56,24},{64,96... | collective-permute-start | bytes 1572872 | tf_op jit(solution)/shard_map/ppermute | solution.py:336
  52.0 18.6 %collective-permute-start.13 = (bf16[1024,256]{1,0:T(8,128)(2,1)S(1)}, bf16[1024,256]{1,0:T(8,128)(2,1)S(1)}, u32[]{:S(2)}, u32[]{:S(2)}) collective-permute-start(bf16[1024,256]{1,0:T(8,128)(2,1)S(1)} %or_select_fusion.rest_0_), channel_id=1, source_target_pairs={{0,48},{8,56},{16,0},{24,8},{32,16},{40,24},{48,32},{56,40},{64,11... | collective-permute-start | bytes 1572872 | tf_op jit(solution)/shard_map/ppermute | solution.py:336
  52.8 17.8 %collective-permute-start.12 = (bf16[1024,256]{1,0:T(8,128)(2,1)S(1)}, bf16[1024,256]{1,0:T(8,128)(2,1)S(1)}, u32[]{:S(2)}, u32[]{:S(2)}) collective-permute-start(bf16[1024,256]{1,0:T(8,128)(2,1)S(1)} %or_select_fusion.rest_0_), channel_id=1, source_target_pairs={{0,16},{8,24},{16,32},{24,40},{32,48},{40,56},{48,0},{56,8},{64,80... | collective-permute-start | bytes 1572872 | tf_op jit(solution)/shard_map/ppermute | solution.py:336
  70.7 179.2 %collective-permute-start.20 = (bf16[1024,256]{1,0:T(8,128)(2,1)S(1)}, bf16[1024,256]{1,0:T(8,128)(2,1)S(1)}, u32[]{:S(2)}, u32[]{:S(2)}) collective-permute-start(bf16[1024,256]{1,0:T(8,128)(2,1)S(1)} %or_select_fusion.rest_0_), channel_id=1, source_target_pairs={{0,8},{8,0},{16,24},{24,16},{32,40},{40,32},{48,56},{56,48},{64,72... | collective-permute-start | bytes 1572872 | tf_op jit(solution)/shard_map/ppermute | solution.py:336
  76.6 173.2 %collective-permute-start.21 = (bf16[1024,256]{1,0:T(8,128)(2,1)S(1)}, bf16[1024,256]{1,0:T(8,128)(2,1)S(1)}, u32[]{:S(2)}, u32[]{:S(2)}) collective-permute-start(bf16[1024,256]{1,0:T(8,128)(2,1)S(1)} %collective-permute-done.12.rest_1_), channel_id=1, source_target_pairs={{0,8},{8,0},{16,24},{24,16},{32,40},{40,32},{48,56},{56,48},{64,72... | collective-permute-start | bytes 1572872 | tf_op jit(solution)/shard_map/ppermute | solution.py:336
  76.6 173.2 %collective-permute-start.22 = (bf16[1024,256]{1,0:T(8,128)(2,1)S(1)}, bf16[1024,256]{1,0:T(8,128)(2,1)S(1)}, u32[]{:S(2)}, u32[]{:S(2)}) collective-permute-start(bf16[1024,256]{1,0:T(8,128)(2,1)S(1)} %collective-permute-done.13.rest_2_), channel_id=1, source_target_pairs={{0,8},{8,0},{16,24},{24,16},{32,40},{40,32},{48,56},{56,48},{64,72... | collective-permute-start | bytes 1572872 | tf_op jit(solution)/shard_map/ppermute | solution.py:336
  77.2 172.7 %collective-permute-start.23 = (bf16[1024,256]{1,0:T(8,128)(2,1)S(1)}, bf16[1024,256]{1,0:T(8,128)(2,1)S(1)}, u32[]{:S(2)}, u32[]{:S(2)}) collective-permute-start(bf16[1024,256]{1,0:T(8,128)(2,1)S(1)} %collective-permute-done.14.rest_3_), channel_id=1, source_target_pairs={{0,8},{8,0},{16,24},{24,16},{32,40},{40,32},{48,56},{56,48},{64,72... | collective-permute-start | bytes 1572872 | tf_op jit(solution)/shard_map/ppermute | solution.py:336

commit v6 on v4

--- a/solution.py
+++ b/solution.py
@@ -375,12 +375,12 @@
     r0x, r0p, r0m, one = tie((r0x, r0p, r0m, one))
 
     piece = jnp.where(x_lo == 0, one, on_grp(one, [(g, g ^ 8) for g in range(16)]))
-    other, r0x_t, r0m_t = tie((along_x_hi(piece), r0x, r0m))
+    other, r0m_t = tie((along_x_hi(piece), r0m))
     both = jnp.stack(
         [jnp.where(x_hi == 0, piece, other), jnp.where(x_hi == 0, other, piece)]
     )
 
-    r1x, r1p, r1m = along_x_hi(r0m_t), along_z(r0x_t, 1), along_z(r0m_t, 3)
+    r1x, r1p, r1m = along_x_hi(r0m_t), along_z(r0x, 1), along_z(r0m, 3)
     r2a, r2b = along_x_hi(r1m[:, : 4 * PAIR]), along_z(r1p[:, 4 * PAIR :], 1)
     behind = [both] + [along_z(both, d) for d in range(1, 4)]
     orders = [

time: 423 us -> 422 us (level)
  starting transfers between devices: 37.9 us -> 32.3 us
    ppermute x12, waiting for transfers between devices: 12.9 us -> 17.7 us  [on_grp(): return lax.ppermute(value, 'grp', pairs)]
    ppermute x12, starting transfers between devices: 19 us -> 14.5 us  [on_grp(): return lax.ppermute(value, 'grp', pairs)]
  transfers between devices with their start and end apart: 24 -> 24, of which waited for: 10 -> 11; matrix products, arithmetic and copies ran while one was open for 1% -> 1% of each run, Pallas kernels for 43% -> 43%
where the time goes in v6:
time: 422 us; the launch traced here: 423 us
  Pallas kernels  358 us (85%)
  starting transfers between devices  32.3 us (8%)
  waiting for transfers between devices  26.9 us (6%)
    pallas_call x2, Pallas kernels, attend_prompt(): pl.pallas_call(functools.partial(prompt_kernel, first, count, len(last)),...  347 us
    ppermute x12, starting transfers between devices, on_hd(): return lax.ppermute(value, 'hd', pairs)  17.9 us
    ppermute x12, waiting for transfers between devices, on_grp(): return lax.ppermute(value, 'grp', pairs)  17.7 us
    ppermute x12, starting transfers between devices, on_grp(): return lax.ppermute(value, 'grp', pairs)  14.5 us
    ppermute x12, waiting for transfers between devices, on_hd(): return lax.ppermute(value, 'hd', pairs)  9.19 us
  transfers between devices with their start and end apart: 24, of which 11 were waited for; matrix products, arithmetic and copies ran while one was open for 1% of the time, Pallas kernels for 43%

profile of v6, /device:TPU:1, one launch (start us, length us, event | category | flops | bytes accessed | tf_op | source)
XLA Modules:
  0.0 423.0 jit_solution(18109047099807607680)
XLA Ops:
  0.0 2.0 shard_map.46
  2.0 1.4 collective-permute-start.3
  3.4 3.8 collective-permute-start.2
  7.3 0.0 collective-permute-start.1
  7.3 2.7 collective-permute-start
  10.0 1.0 slice_select_fusion
  11.1 1.4 collective-permute-start.6
  12.4 2.6 collective-permute-start.5
  15.0 0.8 collective-permute-done.6
  15.8 1.5 collective-permute-start.4
  17.3 0.8 collective-permute-done.5
  18.1 1.2 collective-permute-done.4
  19.3 2.7 collective-permute-done.1.rest_1_.rest_5_
  21.9 0.3 collective-permute-done.rest_4_.rest_8_
  22.2 1.2 collective-permute-start.7
  23.4 0.0 collective-permute-start.17
  23.4 1.9 collective-permute-done.7
  25.4 2.8 collective-permute-start.8
  28.2 0.6 fusion.5
  28.8 2.4 collective-permute-start.15
  31.2 0.0 collective-permute-done.8
  31.2 0.6 collective-permute-start.10
  31.8 1.0 collective-permute-start.9
  32.8 0.5 collective-permute-start.11
  33.3 0.7 iota_compare_fusion
  34.0 2.7 collective-permute-done.17.rest_6_.rest_10_
  36.7 2.5 collective-permute-start.16
  40.5 0.1 stack.96.info
  40.5 0.0 copy-start
  40.6 0.0 copy-start.1
  40.6 0.1 collective-permute-start.19
  40.7 1.5 collective-permute-start.18
  42.2 3.1 collective-permute-done.9
  45.3 1.6 fusion
  47.0 0.3 or_select_fusion.rest_0_
  47.2 3.0 collective-permute-start.14
  50.2 0.8 collective-permute-start.13
  51.0 0.7 collective-permute-start.12
  51.7 0.4 collective-permute-done.18.rest_7_.rest_11_
  52.1 8.2 %own.1 = (f32[128,1024]{1,0:T(8,128)S(1)}, f32[128,8192]{1,0:T(8,128)S(1)}) custom-call(s32[12]{0:T(128)S(1)} %stack.96.info, bf16[128,8192]{1,0:T(8,128)(2,1)S(1)} %bitcast.29, bf16[128,2048]{1,0:T(8,128)(2,1)S(1)} %copy-done.1, bf16[128,2048]{1,0:T(8,128)(2,1)S(1)} %collective-permute-done.1.rest_1_.rest_5_, ...), custom_call_target="tpu_custom_call" | custom-call | flops 8589934592 | bytes 4194304 | tf_op jit(solution)/shard_map/own/pallas_call | solution.py:270
  60.3 12.9 %collective-permute-done.13.rest_2_ = bf16[1024,256]{1,0:T(8,128)(2,1)S(1)} collective-permute-done((bf16[1024,256]{1,0:T(8,128)(2,1)S(1)}, bf16[1024,256]{1,0:T(8,128)(2,1)S(1)}, u32[]{:S(2)}, u32[]{:S(2)}) %collective-permute-start.13) | collective-permute-done | bytes 524320 | tf_op jit(solution)/shard_map/ppermute | solution.py:348
  73.2 0.1 collective-permute-done.12.rest_1_
  73.4 1.4 collective-permute-start.20
  74.8 0.0 collective-permute-start.21
  74.8 0.5 collective-permute-start.22
  75.3 0.0 collective-permute-start.23
  75.3 173.8 %prompt0.1.rest_13_ = bf16[128,8192]{1,0:T(8,128)(2,1)} custom-call(s32[12]{0:T(128)S(1)} %stack.96.info, bf16[128,8192]{1,0:T(8,128)(2,1)S(1)} %bitcast.30, f32[128,1024]{1,0:T(8,128)S(1)} %get-tuple-element.31.tot_in, f32[128,8192]{1,0:T(8,128)S(1)} %get-tuple-element.32.acc_in, bf16[1024,256]{1,0:T(8,128)(2,1)S(1)} %or_select_fusion.rest_0_, ...), custom_call_target="tpu_custom_call" | custom-call | flops 4294967296 | bytes 4194304 | tf_op jit(solution)/shard_map/prompt0/pallas_call | solution.py:293
  249.2 173.6 %prompt4.1 = bf16[128,8192]{1,0:T(8,128)(2,1)} custom-call(s32[12]{0:T(128)S(1)} %stack.96.info, bf16[128,8192]{1,0:T(8,128)(2,1)S(1)} %bitcast.31, f32[128,1024]{1,0:T(8,128)S(1)} %get-tuple-element.31.tot_in, f32[128,8192]{1,0:T(8,128)S(1)} %get-tuple-element.32.acc_in, ...), custom_call_target="tpu_custom_call", output_to_operand_aliasing={{}: (17, {})} | custom-call | flops 4294967296 | bytes 4194304 | tf_op jit(solution)/shard_map/prompt4/pallas_call | solution.py:293
  (25 shorter events, 0.2 us)
Async XLA Ops:
  0.0 28.2 %copy-start.2 = (s32[16]{0:T(128)S(1)}, s32[16]{0:T(128)}, u32[]{:S(2)}) copy-start(s32[16]{0:T(128)} %param.7) | copy-start | bytes 196
  2.0 8.0 %collective-permute-start.3 = (bf16[128,1024]{1,0:T(8,128)(2,1)}, bf16[128,1024]{1,0:T(8,128)(2,1)S(1)}, u32[]{:S(2)}, u32[]{:S(2)}) collective-permute-start(bf16[128,1024]{1,0:T(8,128)(2,1)} %get-tuple-element.22), channel_id=1, source_target_pairs={{0,8},{8,0},{16,24},{24,16},{32,40},{40,32},{48,56},{56,48},{64,72... | collective-permute-start | bytes 786440 | tf_op jit(solution)/shard_map/ppermute | solution.py:348
  3.4 15.8 %collective-permute-start.2 = (bf16[128,2048]{1,0:T(8,128)(2,1)}, bf16[128,2048]{1,0:T(8,128)(2,1)S(1)}, u32[]{:S(2)}, u32[]{:S(2)}) collective-permute-start(bf16[128,2048]{1,0:T(8,128)(2,1)} %get-tuple-element.21.rest_0_.rest_4_), channel_id=1, source_target_pairs={{0,3},{1,0},{2,1},{3,2},{4,7},{5,4},{6,5},{7,6},{8,11},{9,8},{10,9... | collective-permute-start | bytes 1572872 | tf_op jit(solution)/shard_map/ppermute | solution.py:345
  7.3 14.7 %collective-permute-start.1 = (bf16[128,2048]{1,0:T(8,128)(2,1)}, bf16[128,2048]{1,0:T(8,128)(2,1)S(1)}, u32[]{:S(2)}, u32[]{:S(2)}) collective-permute-start(bf16[128,2048]{1,0:T(8,128)(2,1)} %get-tuple-element.21.rest_0_.rest_4_), channel_id=1, source_target_pairs={{0,1},{1,2},{2,3},{3,0},{4,5},{5,6},{6,7},{7,4},{8,9},{9,10},{10,1... | collective-permute-start | bytes 1572872 | tf_op jit(solution)/shard_map/ppermute | solution.py:345
  7.3 15.0 %collective-permute-start = (bf16[128,2048]{1,0:T(8,128)(2,1)}, bf16[128,2048]{1,0:T(8,128)(2,1)S(1)}, u32[]{:S(2)}, u32[]{:S(2)}) collective-permute-start(bf16[128,2048]{1,0:T(8,128)(2,1)} %get-tuple-element.21.rest_0_.rest_4_), channel_id=1, source_target_pairs={{0,4},{1,5},{2,6},{3,7},{4,0},{5,1},{6,2},{7,3},{8,12},{9,13},{10,... | collective-permute-start | bytes 1572872 | tf_op jit(solution)/shard_map/ppermute | solution.py:345
  11.1 4.8 %collective-permute-start.6 = (bf16[128,256]{1,0:T(8,128)(2,1)S(1)}, bf16[128,256]{1,0:T(8,128)(2,1)S(1)}, u32[]{:S(2)}, u32[]{:S(2)}) collective-permute-start(bf16[128,256]{1,0:T(8,128)(2,1)S(1)} %get-tuple-element.37), channel_id=1, source_target_pairs={{0,16},{8,24},{16,32},{24,40},{32,48},{40,56},{48,0},{56,8},{64,80... | collective-permute-start | bytes 196616 | tf_op jit(solution)/shard_map/ppermute | solution.py:348
  12.4 5.6 %collective-permute-start.5 = (bf16[128,256]{1,0:T(8,128)(2,1)S(1)}, bf16[128,256]{1,0:T(8,128)(2,1)S(1)}, u32[]{:S(2)}, u32[]{:S(2)}) collective-permute-start(bf16[128,256]{1,0:T(8,128)(2,1)S(1)} %get-tuple-element.38), channel_id=1, source_target_pairs={{0,32},{8,40},{16,48},{24,56},{32,0},{40,8},{48,16},{56,24},{64,96... | collective-permute-start | bytes 196616 | tf_op jit(solution)/shard_map/ppermute | solution.py:348
  15.8 3.4 collective-permute-start.4
  22.2 3.1 collective-permute-start.7
  23.4 13.2 %collective-permute-start.17 = (bf16[128,2048]{1,0:T(8,128)(2,1)S(1)}, bf16[128,2048]{1,0:T(8,128)(2,1)S(1)}, u32[]{:S(2)}, u32[]{:S(2)}) collective-permute-start(bf16[128,2048]{1,0:T(8,128)(2,1)S(1)} %collective-permute-done.rest_4_.rest_8_), channel_id=1, source_target_pairs={{0,1},{1,2},{2,3},{3,0},{4,5},{5,6},{6,7},{7,4},{8,9},{9,10},{10,1... | collective-permute-start | bytes 1572872 | tf_op jit(solution)/shard_map/ppermute | solution.py:345
  25.4 5.8 %collective-permute-start.8 = (bf16[128,256]{1,0:T(8,128)(2,1)S(1)}, bf16[128,256]{1,0:T(8,128)(2,1)S(1)}, u32[]{:S(2)}, u32[]{:S(2)}) collective-permute-start(bf16[128,256]{1,0:T(8,128)(2,1)S(1)} %broadcast_select_fusion), channel_id=1, source_target_pairs={{0,4},{1,5},{2,6},{3,7},{4,0},{5,1},{6,2},{7,3},{8,12},{9,13},{10,... | collective-permute-start | bytes 196616 | tf_op jit(solution)/shard_map/ppermute | solution.py:345
  28.8 11.8 %collective-permute-start.15 = (bf16[128,2048]{1,0:T(8,128)(2,1)S(1)}, bf16[128,2048]{1,0:T(8,128)(2,1)S(1)}, u32[]{:S(2)}, u32[]{:S(2)}) collective-permute-start(bf16[128,2048]{1,0:T(8,128)(2,1)S(1)} %collective-permute-done.2.rest_2_.rest_6_), channel_id=1, source_target_pairs={{0,3},{1,0},{2,1},{3,2},{4,7},{5,4},{6,5},{7,6},{8,11},{9,8},{10,9... | collective-permute-start | bytes 1572872 | tf_op jit(solution)/shard_map/ppermute | solution.py:345
  31.2 9.5 %collective-permute-start.10 = (bf16[2,128,256]{2,1,0:T(8,128)(2,1)S(1)}, bf16[2,128,256]{2,1,0:T(8,128)(2,1)S(1)}, u32[]{:S(2)}, u32[]{:S(2)}) collective-permute-start(bf16[2,128,256]{2,1,0:T(8,128)(2,1)S(1)} %get-tuple-element.41), channel_id=1, source_target_pairs={{0,2},{1,3},{2,0},{3,1},{4,6},{5,7},{6,4},{7,5},{8,10},{9,11},{10,... | collective-permute-start | bytes 393224 | tf_op jit(solution)/shard_map/ppermute | solution.py:345
  31.8 13.5 %collective-permute-start.9 = (bf16[2,128,256]{2,1,0:T(8,128)(2,1)S(1)}, bf16[2,128,256]{2,1,0:T(8,128)(2,1)}, u32[]{:S(2)}, u32[]{:S(2)}) collective-permute-start(bf16[2,128,256]{2,1,0:T(8,128)(2,1)S(1)} %get-tuple-element.41), channel_id=1, source_target_pairs={{0,3},{1,0},{2,1},{3,2},{4,7},{5,4},{6,5},{7,6},{8,11},{9,8},{10,9... | collective-permute-start | bytes 393224 | tf_op jit(solution)/shard_map/ppermute | solution.py:345
  32.8 12.5 %collective-permute-start.11 = (bf16[2,128,256]{2,1,0:T(8,128)(2,1)S(1)}, bf16[2,128,256]{2,1,0:T(8,128)(2,1)}, u32[]{:S(2)}, u32[]{:S(2)}) collective-permute-start(bf16[2,128,256]{2,1,0:T(8,128)(2,1)S(1)} %get-tuple-element.41), channel_id=1, source_target_pairs={{0,1},{1,2},{2,3},{3,0},{4,5},{5,6},{6,7},{7,4},{8,9},{9,10},{10,1... | collective-permute-start | bytes 393224 | tf_op jit(solution)/shard_map/ppermute | solution.py:345
  36.7 14.3 %collective-permute-start.16 = (bf16[128,2048]{1,0:T(8,128)(2,1)S(1)}, bf16[128,2048]{1,0:T(8,128)(2,1)S(1)}, u32[]{:S(2)}, u32[]{:S(2)}) collective-permute-start(bf16[128,2048]{1,0:T(8,128)(2,1)S(1)} %collective-permute-done.2.rest_2_.rest_6_), channel_id=1, source_target_pairs={{0,4},{1,5},{2,6},{3,7},{4,0},{5,1},{6,2},{7,3},{8,12},{9,13},{10,... | collective-permute-start | bytes 1572872 | tf_op jit(solution)/shard_map/ppermute | solution.py:345
  40.5 11.6 %copy-start = (bf16[1,128,8192]{2,1,0:T(8,128)(2,1)S(1)}, bf16[1,128,8192]{2,1,0:T(8,128)(2,1)}, u32[]{:S(2)}) copy-start(bf16[1,128,8192]{2,1,0:T(8,128)(2,1)} %param.4) | copy-start | bytes 6291460
  40.6 11.6 %copy-start.1 = (bf16[128,2048]{1,0:T(8,128)(2,1)S(1)}, bf16[128,2048]{1,0:T(8,128)(2,1)}, u32[]{:S(2)}) copy-start(bf16[128,2048]{1,0:T(8,128)(2,1)} %get-tuple-element.21.rest_0_.rest_4_) | copy-start | bytes 1572868
  40.6 11.1 %collective-permute-start.19 = (bf16[128,1024]{1,0:T(8,128)(2,1)S(1)}, bf16[128,1024]{1,0:T(8,128)(2,1)S(1)}, u32[]{:S(2)}, u32[]{:S(2)}) collective-permute-start(bf16[128,1024]{1,0:T(8,128)(2,1)S(1)} %slice.38), channel_id=1, source_target_pairs={{0,1},{1,2},{2,3},{3,0},{4,5},{5,6},{6,7},{7,4},{8,9},{9,10},{10,1... | collective-permute-start | bytes 786440 | tf_op jit(solution)/shard_map/ppermute | solution.py:345
  40.7 11.4 %collective-permute-start.18 = (bf16[128,1024]{1,0:T(8,128)(2,1)S(1)}, bf16[128,1024]{1,0:T(8,128)(2,1)S(1)}, u32[]{:S(2)}, u32[]{:S(2)}) collective-permute-start(bf16[128,1024]{1,0:T(8,128)(2,1)S(1)} %slice.37), channel_id=1, source_target_pairs={{0,4},{1,5},{2,6},{3,7},{4,0},{5,1},{6,2},{7,3},{8,12},{9,13},{10,... | collective-permute-start | bytes 786440 | tf_op jit(solution)/shard_map/ppermute | solution.py:345
  47.2 13.1 %collective-permute-start.14 = (bf16[1024,256]{1,0:T(8,128)(2,1)S(1)}, bf16[1024,256]{1,0:T(8,128)(2,1)S(1)}, u32[]{:S(2)}, u32[]{:S(2)}) collective-permute-start(bf16[1024,256]{1,0:T(8,128)(2,1)S(1)} %or_select_fusion.rest_0_), channel_id=1, source_target_pairs={{0,32},{8,40},{16,48},{24,56},{32,0},{40,8},{48,16},{56,24},{64,96... | collective-permute-start | bytes 1572872 | tf_op jit(solution)/shard_map/ppermute | solution.py:348
  50.2 23.0 %collective-permute-start.13 = (bf16[1024,256]{1,0:T(8,128)(2,1)S(1)}, bf16[1024,256]{1,0:T(8,128)(2,1)S(1)}, u32[]{:S(2)}, u32[]{:S(2)}) collective-permute-start(bf16[1024,256]{1,0:T(8,128)(2,1)S(1)} %or_select_fusion.rest_0_), channel_id=1, source_target_pairs={{0,48},{8,56},{16,0},{24,8},{32,16},{40,24},{48,32},{56,40},{64,11... | collective-permute-start | bytes 1572872 | tf_op jit(solution)/shard_map/ppermute | solution.py:348
  51.0 22.4 %collective-permute-start.12 = (bf16[1024,256]{1,0:T(8,128)(2,1)S(1)}, bf16[1024,256]{1,0:T(8,128)(2,1)S(1)}, u32[]{:S(2)}, u32[]{:S(2)}) collective-permute-start(bf16[1024,256]{1,0:T(8,128)(2,1)S(1)} %or_select_fusion.rest_0_), channel_id=1, source_target_pairs={{0,16},{8,24},{16,32},{24,40},{32,48},{40,56},{48,0},{56,8},{64,80... | collective-permute-start | bytes 1572872 | tf_op jit(solution)/shard_map/ppermute | solution.py:348
  73.4 175.8 %collective-permute-start.20 = (bf16[1024,256]{1,0:T(8,128)(2,1)S(1)}, bf16[1024,256]{1,0:T(8,128)(2,1)S(1)}, u32[]{:S(2)}, u32[]{:S(2)}) collective-permute-start(bf16[1024,256]{1,0:T(8,128)(2,1)S(1)} %or_select_fusion.rest_0_), channel_id=1, source_target_pairs={{0,8},{8,0},{16,24},{24,16},{32,40},{40,32},{48,56},{56,48},{64,72... | collective-permute-start | bytes 1572872 | tf_op jit(solution)/shard_map/ppermute | solution.py:348
  74.8 174.3 %collective-permute-start.21 = (bf16[1024,256]{1,0:T(8,128)(2,1)S(1)}, bf16[1024,256]{1,0:T(8,128)(2,1)S(1)}, u32[]{:S(2)}, u32[]{:S(2)}) collective-permute-start(bf16[1024,256]{1,0:T(8,128)(2,1)S(1)} %collective-permute-done.12.rest_1_), channel_id=1, source_target_pairs={{0,8},{8,0},{16,24},{24,16},{32,40},{40,32},{48,56},{56,48},{64,72... | collective-permute-start | bytes 1572872 | tf_op jit(solution)/shard_map/ppermute | solution.py:348
  74.8 174.4 %collective-permute-start.22 = (bf16[1024,256]{1,0:T(8,128)(2,1)S(1)}, bf16[1024,256]{1,0:T(8,128)(2,1)S(1)}, u32[]{:S(2)}, u32[]{:S(2)}) collective-permute-start(bf16[1024,256]{1,0:T(8,128)(2,1)S(1)} %collective-permute-done.13.rest_2_), channel_id=1, source_target_pairs={{0,8},{8,0},{16,24},{24,16},{32,40},{40,32},{48,56},{56,48},{64,72... | collective-permute-start | bytes 1572872 | tf_op jit(solution)/shard_map/ppermute | solution.py:348
  75.3 173.9 %collective-permute-start.23 = (bf16[1024,256]{1,0:T(8,128)(2,1)S(1)}, bf16[1024,256]{1,0:T(8,128)(2,1)S(1)}, u32[]{:S(2)}, u32[]{:S(2)}) collective-permute-start(bf16[1024,256]{1,0:T(8,128)(2,1)S(1)} %collective-permute-done.14.rest_3_), channel_id=1, source_target_pairs={{0,8},{8,0},{16,24},{24,16},{32,40},{40,32},{48,56},{56,48},{64,72... | collective-permute-start | bytes 1572872 | tf_op jit(solution)/shard_map/ppermute | solution.py:348
